TPU v7x, 32 devices: a whole 2x2x4 slice. The times are simulated.
32 devices in a mesh: fsdp: 16 (over z, y, x), dp: 2 (over core).
Axes of the slice: x: 2, y: 2, z: 4, core: 2. Of those that a mesh axis runs over, the one named last changes fastest.
Arguments:
- tokens: bfloat16 [256, 257, 384], P(('fsdp', 'dp')), may hold values from -6 to 6
- duplicate: int32 [256, 257], P(('fsdp', 'dp')), may hold values 0 or 1
- targets: float32 [256, 384], P(('fsdp', 'dp')), may hold values from -6 to 6
- ln1_gain: bfloat16 [384], P('fsdp'), may hold values from 0.5 to 1.5
- ln1_bias: bfloat16 [384], P('fsdp'), may hold values from -1.796875 to 1.796875
- qkv_weight: bfloat16 [384, 1152], P('fsdp'), may hold values from -0.3125 to 0.3125
- qv_bias: bfloat16 [768], P('fsdp'), may hold values from -1.796875 to 1.796875
- out_weight: bfloat16 [384, 384], P('fsdp'), may hold values from -1.25 to 1.25
- out_bias: bfloat16 [384], P('fsdp'), may hold values from -1.796875 to 1.796875
- ln2_gain: bfloat16 [384], P('fsdp'), may hold values from 0.5 to 1.5
- ln2_bias: bfloat16 [384], P('fsdp'), may hold values from -1.796875 to 1.796875
- fc1_weight: bfloat16 [384, 1536], P('fsdp'), may hold values from -0.3125 to 0.3125
- fc1_bias: bfloat16 [1536], P('fsdp'), may hold values from -1.796875 to 1.796875
- fc2_weight: bfloat16 [1536, 384], P('fsdp'), may hold values from -0.15625 to 0.15625
- fc2_bias: bfloat16 [384], P('fsdp'), may hold values from -1.796875 to 1.796875
Outputs:
- block_output: bfloat16 [256, 257, 384], P(('fsdp', 'dp'))
- input_grad: float32 [256, 257, 384], P(('fsdp', 'dp'))
- ln1_gain_grad: float32 [384], P('fsdp')
- ln1_bias_grad: float32 [384], P('fsdp')
- qkv_weight_grad: float32 [384, 1152], P('fsdp')
- qv_bias_grad: float32 [768], P('fsdp')
- out_weight_grad: float32 [384, 384], P('fsdp')
- out_bias_grad: float32 [384], P('fsdp')
- ln2_gain_grad: float32 [384], P('fsdp')
- ln2_bias_grad: float32 [384], P('fsdp')
- fc1_weight_grad: float32 [384, 1536], P('fsdp')
- fc1_bias_grad: float32 [1536], P('fsdp')
- fc2_weight_grad: float32 [1536, 384], P('fsdp')
- fc2_bias_grad: float32 [384], P('fsdp')
Inputs may be any that keep to these rules, and one draw needn't show every extreme that they name: 1 marks a duplicate patch; the entry at position 0, the class token, is not read.
All inputs are finite; a program needn't handle non-finite values. No bound on the sum of `duplicate` on one device may be relied on, other than what follows from the above.
Results may differ from a plain program's by a relative error of at most 0.009.
Values may be sent and summed in bfloat16 or wider, within the bound.
A program may use at most 128 MiB of HBM per device.

v0:
```python
import jax
import jax.numpy as jnp
from jax import lax
from jax.sharding import PartitionSpec as P

HEADS = 6
HEAD_DIM = 64


EPSILON = 1e-06


def layer_norm(values, gain, shift):
    centre = jnp.mean(values, -1, keepdims=True)
    centred = values - centre
    spread = jnp.mean(centred * centred, -1, keepdims=True)
    return centred * lax.rsqrt(spread + EPSILON) * gain + shift


def gelu_exact(values):
    return jax.nn.gelu(values, approximate=False)


def block_forward(tok_block, weights):
    (
        ln1_gain,
        ln1_bias,
        qkv_weight,
        qv_bias,
        out_weight,
        out_bias,
        ln2_gain,
        ln2_bias,
        fc1_weight,
        fc1_bias,
        fc2_weight,
        fc2_bias,
    ) = weights
    image_count, seq_len, feature_width = tok_block.shape
    tok_rows = tok_block.astype(jnp.float32).reshape(image_count * seq_len, feature_width)
    gain_one = ln1_gain.astype(jnp.float32)
    shift_one = ln1_bias.astype(jnp.float32)
    gain_two = ln2_gain.astype(jnp.float32)
    shift_two = ln2_bias.astype(jnp.float32)
    normed1 = layer_norm(tok_rows, gain_one, shift_one).astype(jnp.bfloat16)
    bias_half = qv_bias.astype(jnp.float32)
    bias_full = jnp.concatenate(
        [
            bias_half[:feature_width],
            jnp.zeros((feature_width,), jnp.float32),
            bias_half[feature_width:],
        ]
    )
    qkv = (jnp.dot(normed1, qkv_weight, preferred_element_type=jnp.float32) + bias_full).astype(
        jnp.bfloat16
    )
    qkv = qkv.reshape(image_count, seq_len, 3, HEADS, HEAD_DIM)
    queries = qkv[:, :, 0]
    key_heads = qkv[:, :, 1]
    value_heads = qkv[:, :, 2]
    score_scale = HEAD_DIM ** (-0.5)
    scores = (
        jnp.einsum("bqhd,bkhd->bhqk", queries, key_heads, preferred_element_type=jnp.float32)
        * score_scale
    )
    shares = jax.nn.softmax(scores, -1)
    shares_low = shares.astype(jnp.bfloat16)
    attended = jnp.einsum(
        "bhqk,bkhd->bqhd", shares_low, value_heads, preferred_element_type=jnp.float32
    )
    attended = attended.reshape(image_count * seq_len, feature_width).astype(jnp.bfloat16)
    middle = (
        tok_rows
        + jnp.dot(attended, out_weight, preferred_element_type=jnp.float32)
        + out_bias.astype(jnp.float32)
    )
    normed2 = layer_norm(middle, gain_two, shift_two).astype(jnp.bfloat16)
    hidden_pre = jnp.dot(normed2, fc1_weight, preferred_element_type=jnp.float32) + fc1_bias.astype(
        jnp.float32
    )
    activated, gelu_pull = jax.vjp(gelu_exact, hidden_pre)
    activated_low = activated.astype(jnp.bfloat16)
    final = (
        middle
        + jnp.dot(activated_low, fc2_weight, preferred_element_type=jnp.float32)
        + fc2_bias.astype(jnp.float32)
    )
    saved = (
        tok_rows,
        normed1,
        queries,
        key_heads,
        value_heads,
        shares,
        shares_low,
        attended,
        middle,
        normed2,
        gelu_pull,
        activated_low,
    )
    return (final, saved)


def block_backward(saved, d_final, weights):
    (
        ln1_gain,
        ln1_bias,
        qkv_weight,
        qv_bias,
        out_weight,
        out_bias,
        ln2_gain,
        ln2_bias,
        fc1_weight,
        fc1_bias,
        fc2_weight,
        fc2_bias,
    ) = weights
    (
        tok_rows,
        normed1,
        queries,
        key_heads,
        value_heads,
        shares,
        shares_low,
        attended,
        middle,
        normed2,
        gelu_pull,
        activated_low,
    ) = saved
    image_count, seq_len = (queries.shape[0], queries.shape[1])
    feature_width = tok_rows.shape[1]
    score_scale = HEAD_DIM ** (-0.5)
    d_branch2 = d_final.astype(jnp.bfloat16)
    fc2_grad = jnp.dot(activated_low.T, d_branch2, preferred_element_type=jnp.float32)
    fc2_bias_sum = jnp.sum(d_branch2.astype(jnp.float32), 0)
    d_activated = jnp.dot(d_branch2, fc2_weight.T, preferred_element_type=jnp.float32)
    (d_hidden,) = gelu_pull(d_activated)
    d_pre = d_hidden.astype(jnp.bfloat16)
    fc1_grad = jnp.dot(normed2.T, d_pre, preferred_element_type=jnp.float32)
    fc1_bias_sum = jnp.sum(d_pre.astype(jnp.float32), 0)
    d_normed2 = jnp.dot(d_pre, fc1_weight.T, preferred_element_type=jnp.float32)
    unused_two, norm_two_pull = jax.vjp(
        layer_norm, middle, ln2_gain.astype(jnp.float32), ln2_bias.astype(jnp.float32)
    )
    d_middle_norm, ln2_gain_sum, ln2_bias_sum = norm_two_pull(d_normed2)
    d_middle = d_final + d_middle_norm
    d_branch1 = d_middle.astype(jnp.bfloat16)
    out_grad = jnp.dot(attended.T, d_branch1, preferred_element_type=jnp.float32)
    out_bias_sum = jnp.sum(d_branch1.astype(jnp.float32), 0)
    d_attended = jnp.dot(d_branch1, out_weight.T, preferred_element_type=jnp.float32).astype(
        jnp.bfloat16
    )
    d_attended = d_attended.reshape(image_count, seq_len, HEADS, HEAD_DIM)
    d_shares = jnp.einsum(
        "bqhd,bkhd->bhqk", d_attended, value_heads, preferred_element_type=jnp.float32
    )
    row_total = jnp.sum(shares * d_shares, -1, keepdims=True)
    d_scores = (shares * (d_shares - row_total)).astype(jnp.bfloat16)
    d_queries = (
        jnp.einsum("bhqk,bkhd->bqhd", d_scores, key_heads, preferred_element_type=jnp.float32)
        * score_scale
    )
    d_keys = (
        jnp.einsum("bhqk,bqhd->bkhd", d_scores, queries, preferred_element_type=jnp.float32)
        * score_scale
    )
    d_values = jnp.einsum(
        "bhqk,bqhd->bkhd", shares_low, d_attended, preferred_element_type=jnp.float32
    )
    d_qkv = (
        jnp.stack([d_queries, d_keys, d_values], 2)
        .reshape(image_count * seq_len, 3 * feature_width)
        .astype(jnp.bfloat16)
    )
    qkv_grad = jnp.dot(normed1.T, d_qkv, preferred_element_type=jnp.float32)
    column_sums = jnp.sum(d_qkv.astype(jnp.float32), 0)
    qv_bias_sum = jnp.concatenate([column_sums[:feature_width], column_sums[2 * feature_width :]])
    d_normed1 = jnp.dot(d_qkv, qkv_weight.T, preferred_element_type=jnp.float32)
    unused_one, norm_one_pull = jax.vjp(
        layer_norm, tok_rows, ln1_gain.astype(jnp.float32), ln1_bias.astype(jnp.float32)
    )
    d_rows_norm, ln1_gain_sum, ln1_bias_sum = norm_one_pull(d_normed1)
    d_rows = d_middle + d_rows_norm
    grads = (
        ln1_gain_sum,
        ln1_bias_sum,
        qkv_grad,
        qv_bias_sum,
        out_grad,
        out_bias_sum,
        ln2_gain_sum,
        ln2_bias_sum,
        fc1_grad,
        fc1_bias_sum,
        fc2_grad,
        fc2_bias_sum,
    )
    return (d_rows.reshape(image_count, seq_len, feature_width), grads)


def final_cotangent(dup_block, target_block):
    seq_len = dup_block.shape[1]
    position = jnp.arange(seq_len)[None, :]
    keep = jnp.where(
        position == 0, jnp.float32(1.0), jnp.float32(1.0) - dup_block.astype(jnp.float32)
    )
    count = jnp.sum(keep, -1)
    cotangent = seq_len * keep[:, :, None] * target_block[:, None, :] / count[:, None, None]
    return cotangent.reshape(dup_block.shape[0] * seq_len, target_block.shape[1])


def per_device(
    tokens,
    duplicate,
    targets,
    ln1_gain,
    ln1_bias,
    qkv_weight,
    qv_bias,
    out_weight,
    out_bias,
    ln2_gain,
    ln2_bias,
    fc1_weight,
    fc1_bias,
    fc2_weight,
    fc2_bias,
):
    gathered = (
        lax.all_gather(ln1_gain, "fsdp", axis=0, tiled=True),
        lax.all_gather(ln1_bias, "fsdp", axis=0, tiled=True),
        lax.all_gather(qkv_weight, "fsdp", axis=0, tiled=True),
        lax.all_gather(qv_bias, "fsdp", axis=0, tiled=True),
        lax.all_gather(out_weight, "fsdp", axis=0, tiled=True),
        lax.all_gather(out_bias, "fsdp", axis=0, tiled=True),
        lax.all_gather(ln2_gain, "fsdp", axis=0, tiled=True),
        lax.all_gather(ln2_bias, "fsdp", axis=0, tiled=True),
        lax.all_gather(fc1_weight, "fsdp", axis=0, tiled=True),
        lax.all_gather(fc1_bias, "fsdp", axis=0, tiled=True),
        lax.all_gather(fc2_weight, "fsdp", axis=0, tiled=True),
        lax.all_gather(fc2_bias, "fsdp", axis=0, tiled=True),
    )
    image_count, seq_len, feature_width = tokens.shape
    block_count = image_count // 2
    tok_blocks = tokens.reshape(block_count, 2, seq_len, feature_width)
    dup_blocks = duplicate.reshape(block_count, 2, seq_len)
    target_blocks = targets.reshape(block_count, 2, feature_width)
    start = tuple((jnp.zeros(weight.shape, jnp.float32) for weight in gathered))

    def make_backward(weights):

        def backward_step(carry, inputs_block):
            tok_block, dup_block, target_block = inputs_block
            final, saved = block_forward(tok_block, weights)
            d_rows, grads = block_backward(saved, final_cotangent(dup_block, target_block), weights)
            updated = tuple((total + grad for total, grad in zip(carry, grads)))
            return (updated, (final.astype(jnp.bfloat16).reshape(tok_block.shape), d_rows))

        return backward_step

    def forward_step(carry, tok_block):
        final, unused_saved = block_forward(tok_block, gathered)
        return (carry, final.astype(jnp.bfloat16).reshape(tok_block.shape))

    unused_carry, out_blocks = lax.scan(forward_step, jnp.float32(0.0), tok_blocks)
    again = (
        lax.all_gather(ln1_gain, "fsdp", axis=0, tiled=True),
        lax.all_gather(ln1_bias, "fsdp", axis=0, tiled=True),
        lax.all_gather(qkv_weight, "fsdp", axis=0, tiled=True),
        lax.all_gather(qv_bias, "fsdp", axis=0, tiled=True),
        lax.all_gather(out_weight, "fsdp", axis=0, tiled=True),
        lax.all_gather(out_bias, "fsdp", axis=0, tiled=True),
        lax.all_gather(ln2_gain, "fsdp", axis=0, tiled=True),
        lax.all_gather(ln2_bias, "fsdp", axis=0, tiled=True),
        lax.all_gather(fc1_weight, "fsdp", axis=0, tiled=True),
        lax.all_gather(fc1_bias, "fsdp", axis=0, tiled=True),
        lax.all_gather(fc2_weight, "fsdp", axis=0, tiled=True),
        lax.all_gather(fc2_bias, "fsdp", axis=0, tiled=True),
    )
    totals, (unused_out, grad_blocks) = lax.scan(
        make_backward(again), start, (tok_blocks, dup_blocks, target_blocks)
    )
    shard_sums = (
        lax.psum_scatter(totals[0], "fsdp", scatter_dimension=0, tiled=True),
        lax.psum_scatter(totals[1], "fsdp", scatter_dimension=0, tiled=True),
        lax.psum_scatter(totals[2], "fsdp", scatter_dimension=0, tiled=True),
        lax.psum_scatter(totals[3], "fsdp", scatter_dimension=0, tiled=True),
        lax.psum_scatter(totals[4], "fsdp", scatter_dimension=0, tiled=True),
        lax.psum_scatter(totals[5], "fsdp", scatter_dimension=0, tiled=True),
        lax.psum_scatter(totals[6], "fsdp", scatter_dimension=0, tiled=True),
        lax.psum_scatter(totals[7], "fsdp", scatter_dimension=0, tiled=True),
        lax.psum_scatter(totals[8], "fsdp", scatter_dimension=0, tiled=True),
        lax.psum_scatter(totals[9], "fsdp", scatter_dimension=0, tiled=True),
        lax.psum_scatter(totals[10], "fsdp", scatter_dimension=0, tiled=True),
        lax.psum_scatter(totals[11], "fsdp", scatter_dimension=0, tiled=True),
    )
    summed = (
        lax.psum(shard_sums[0].astype(jnp.bfloat16), "dp").astype(jnp.float32),
        lax.psum(shard_sums[1].astype(jnp.bfloat16), "dp").astype(jnp.float32),
        lax.psum(shard_sums[2].astype(jnp.bfloat16), "dp").astype(jnp.float32),
        lax.psum(shard_sums[3].astype(jnp.bfloat16), "dp").astype(jnp.float32),
        lax.psum(shard_sums[4].astype(jnp.bfloat16), "dp").astype(jnp.float32),
        lax.psum(shard_sums[5].astype(jnp.bfloat16), "dp").astype(jnp.float32),
        lax.psum(shard_sums[6].astype(jnp.bfloat16), "dp").astype(jnp.float32),
        lax.psum(shard_sums[7].astype(jnp.bfloat16), "dp").astype(jnp.float32),
        lax.psum(shard_sums[8].astype(jnp.bfloat16), "dp").astype(jnp.float32),
        lax.psum(shard_sums[9].astype(jnp.bfloat16), "dp").astype(jnp.float32),
        lax.psum(shard_sums[10].astype(jnp.bfloat16), "dp").astype(jnp.float32),
        lax.psum(shard_sums[11].astype(jnp.bfloat16), "dp").astype(jnp.float32),
    )
    block_output = out_blocks.reshape(image_count, seq_len, feature_width)
    input_grad = grad_blocks.reshape(image_count, seq_len, feature_width)
    return (
        block_output,
        input_grad,
        summed[0],
        summed[1],
        summed[2],
        summed[3],
        summed[4],
        summed[5],
        summed[6],
        summed[7],
        summed[8],
        summed[9],
        summed[10],
        summed[11],
    )


def solution(mesh):
    return jax.shard_map(
        per_device,
        mesh=mesh,
        in_specs=(
            P(("fsdp", "dp"), None, None),
            P(("fsdp", "dp"), None),
            P(("fsdp", "dp"), None),
            P("fsdp"),
            P("fsdp"),
            P("fsdp", None),
            P("fsdp"),
            P("fsdp", None),
            P("fsdp"),
            P("fsdp"),
            P("fsdp"),
            P("fsdp", None),
            P("fsdp"),
            P("fsdp", None),
            P("fsdp"),
        ),
        out_specs=(
            P(("fsdp", "dp"), None, None),
            P(("fsdp", "dp"), None, None),
            P("fsdp"),
            P("fsdp"),
            P("fsdp", None),
            P("fsdp"),
            P("fsdp", None),
            P("fsdp"),
            P("fsdp"),
            P("fsdp"),
            P("fsdp", None),
            P("fsdp"),
            P("fsdp", None),
            P("fsdp"),
        ),
        check_vma=False,
    )
```

profile of v0, /device:TPU:0, one launch (start us, length us, event | category | flops | bytes accessed | tf_op | source)
XLA Modules:
  0.0 1305.0 jit_solution(16057559991316612417)
XLA Ops:
  18.2 78.8 %all-reduce.19 = (bf16[384]{0:T(512)(128)(2,1)S(1)}, bf16[384]{0:T(512)(128)(2,1)S(1)}, bf16[768]{0:T(1024)(128)(2,1)S(1)}, bf16[384]{0:T(512)(128)(2,1)}, bf16[...) all-reduce(bf16[384]{0:T(512)(128)(2,1)S(1)} %dynamic-update-slice,, ...), channel_id=1, replica_groups=mesh['fsdp'=16,'dp'=2] {'fsdp'}, use_global_device_ids=true, to_apply=%add | all-reduce | flops 4608 | bytes 18432
  97.1 37.7 %all_gather.51 = bf16[384,384]{1,0:T(8,128)(2,1)S(1)} all-gather(bf16[24,384]{1,0:T(8,128)(2,1)S(1)} %copy-done.80), channel_id=1, replica_groups=mesh['fsdp'=16,'dp'=2] {'fsdp'}, dimensions={0}, use_global_device_ids=true | all-gather | bytes 313344 | tf_op jit(solution)/shard_map/all_gather | solution.py:238
  134.8 44.4 %all_gather.49 = bf16[384,1152]{1,0:T(8,128)(2,1)} all-gather(bf16[24,1152]{1,0:T(8,128)(2,1)S(1)} %copy-done.75), channel_id=1, replica_groups=mesh['fsdp'=16,'dp'=2] {'fsdp'}, dimensions={0}, use_global_device_ids=true | all-gather | bytes 940032 | tf_op jit(solution)/shard_map/all_gather | solution.py:236
  179.1 421.0 %while.46 = (s32[]{:T(128)}, f32[384]{0:T(512)}, f32[384]{0:T(512)}, f32[384,1152]{1,0:T(8,128)}, f32[768]{0:T(1024)}, /*index=5*/f32[384,384]{1,0:T(8,128)}, f3...) while((s32[]{:T(128)}, f32[384]{0:T(512)}, ...), condition=%wide.region_29.30_spmd.clone, body=%wide.region_8.29_spmd.clone.sunk | while | flops 5561711616 | bytes 237182800 | solution.py:284
  206.3 3.7 reshape.402
  216.7 3.5 fusion.257
  221.0 3.3 fusion.258
  228.1 10.4 fusion.261
  242.3 6.1 convolution_add_fusion.18
  260.6 4.0 multiply_reduce_fusion.23
  270.6 4.5 copy.127
  275.1 4.8 convert_element_type.532
  279.9 3.4 multiply_reduce_fusion.24
  301.9 3.7 reshape.402
  312.3 3.5 fusion.257
  316.6 3.3 fusion.258
  323.8 10.4 fusion.261
  337.9 6.8 convolution_add_fusion.18
  356.9 4.0 multiply_reduce_fusion.23
  366.9 4.5 copy.127
  371.4 4.8 convert_element_type.532
  376.2 3.4 multiply_reduce_fusion.24
  385.1 3.9 convolution_add_fusion.15
  399.9 3.7 reshape.402
  410.3 3.5 fusion.257
  414.5 3.3 fusion.258
  421.7 10.4 fusion.261
  435.8 6.8 convolution_add_fusion.18
  454.8 4.0 multiply_reduce_fusion.23
  464.8 4.5 copy.127
  469.3 4.8 convert_element_type.532
  474.2 3.4 multiply_reduce_fusion.24
  483.0 3.9 convolution_add_fusion.15
  497.8 3.7 reshape.402
  508.2 3.5 fusion.257
  512.5 3.3 fusion.258
  519.6 10.4 fusion.261
  533.7 6.8 convolution_add_fusion.18
  552.7 3.9 multiply_reduce_fusion.23
  562.8 4.5 copy.127
  567.3 4.8 convert_element_type.532
  572.1 3.4 multiply_reduce_fusion.24
  581.0 3.9 convolution_add_fusion.15
  604.0 72.6 %all-reduce.18 = (bf16[384]{0:T(512)(128)(2,1)S(1)}, bf16[384]{0:T(512)(128)(2,1)S(1)}, bf16[768]{0:T(1024)(128)(2,1)S(1)}, bf16[384]{0:T(512)(128)(2,1)S(1)}, b...) all-reduce(f32[384]{0:T(512)S(1)} %copy-done.59, ...), channel_id=2, replica_groups=mesh['fsdp'=16,'dp'=2] {'fsdp'}, use_global_device_ids=true, to_apply=%region_30.31.clone | all-reduce | flops 4608 | bytes 27648
  681.4 38.0 %reduce-scatter.15.cloned.1.call-done = f32[24,384]{1,0:T(8,128)} async-done(((f32[384,384]{1,0:T(8,128)}), f32[24,384]{1,0:T(8,128)}) %reduce-scatter.15.cloned.1.call-update) | async-done | bytes 36880
  720.7 129.6 %reduce-scatter.13.cloned.1.call-done = f32[24,1152]{1,0:T(8,128)} async-done(((f32[384,1152]{1,0:T(8,128)}), f32[24,1152]{1,0:T(8,128)}) %reduce-scatter.13.cloned.1.call-update) | async-done | bytes 110608
  851.9 131.0 %reduce-scatter.9.cloned.1.call-done = f32[24,1536]{1,0:T(8,128)} async-done(((f32[384,1536]{1,0:T(8,128)}), f32[24,1536]{1,0:T(8,128)}) %reduce-scatter.9.cloned.1.call-update) | async-done | bytes 147472 | tf_op jit(solution)/shard_map/reduce_scatter | solution.py:296
  984.5 130.7 %reduce-scatter.11.cloned.1.call-done = f32[96,384]{1,0:T(8,128)} async-done(((f32[1536,384]{1,0:T(8,128)}), f32[96,384]{1,0:T(8,128)}) %reduce-scatter.11.cloned.1.call-update) | async-done | bytes 147472 | tf_op jit(solution)/shard_map/reduce_scatter | solution.py:298
  1116.8 160.3 %while.45 = (s32[]{:T(128)}, bf16[4,2,257,384]{3,2,1,0:T(8,128)(2,1)}, bf16[4,2,257,384]{3,2,1,0:T(8,128)(2,1)}, bf16[384]{0:T(512)(128)(2,1)S(1)}, bf16[384]{0:...) while((s32[]{:T(128)}, ...), condition=%wide.region_7.8_spmd, body=%wide.region_0.7_spmd.sunk | while | flops 2085303296 | bytes 45573328 | solution.py:269
  1124.6 3.7 reshape.400
  1134.7 3.5 fusion.220
  1146.0 10.0 fusion.223
  1164.7 3.7 reshape.400
  1174.8 3.5 fusion.220
  1186.1 10.0 fusion.223
  1204.8 3.7 reshape.400
  1214.9 3.5 fusion.220
  1219.1 3.2 fusion.221
  1226.2 10.0 fusion.223
  1244.8 3.7 reshape.400
  1254.9 3.5 fusion.220
  1259.2 3.2 fusion.221
  1266.2 10.0 fusion.223
  1277.1 4.3 copy.95
  (1138 shorter events, 319.7 us)
Async XLA Ops:
  7.2 8.5 copy-start.82
  7.2 9.1 copy-start.85
  7.2 9.3 copy-start.86
  7.2 9.5 copy-start.87
  7.2 9.7 copy-start.88
  7.2 10.0 copy-start.89
  7.3 10.2 copy-start.90
  7.3 10.5 copy-start.91
  7.3 10.7 copy-start.92
  7.3 89.8 %copy-start.80 = (bf16[24,384]{1,0:T(8,128)(2,1)S(1)}, bf16[24,384]{1,0:T(8,128)(2,1)}, u32[]{:S(2)}) copy-start(bf16[24,384]{1,0:T(8,128)(2,1)} %param.26) | copy-start | bytes 55300
  7.3 127.5 %copy-start.75 = (bf16[24,1152]{1,0:T(8,128)(2,1)S(1)}, bf16[24,1152]{1,0:T(8,128)(2,1)}, u32[]{:S(2)}) copy-start(bf16[24,1152]{1,0:T(8,128)(2,1)} %param.24) | copy-start | bytes 165892
  7.3 171.8 %all-gather.3.cloned.1.call-start = ((), (), s32[]{:S(2)}) async-start(), calls=%async_computation.4 | async-start | bytes 1253376 | tf_op jit(solution)/shard_map/all_gather | solution.py:242
  8.0 171.1 %all-gather.5.cloned.1.call-start = ((), (), s32[]{:S(2)}) async-start(), calls=%async_computation.5 | async-start | bytes 1253376 | tf_op jit(solution)/shard_map/all_gather | solution.py:244
  8.8 710.5 %reduce-scatter.15.cloned.1.call-start = ((), (), s32[]{:S(2)}) async-start(), calls=%async_computation.9 | async-start | bytes 626688
  197.8 8.5 copy-start.24
  197.8 8.5 copy-start.53
  197.8 8.5 copy-start.55
  197.8 30.3 %copy-start.36 = (bf16[1536]{0:T(1024)(128)(2,1)}, bf16[1536]{0:T(1024)(128)(2,1)S(1)}, u32[]{:S(2)}) copy-start(bf16[1536]{0:T(1024)(128)(2,1)S(1)} %get-tuple-element.1023) | copy-start | bytes 9220 | tf_op jit(solution)/shard_map/while
  225.3 13.2 %copy-start.7 = (bf16[514,384]{0,1:T(8,128)(2,1)}, bf16[514,384]{0,1:T(8,128)(2,1)S(1)}, u32[]{:S(2)}) copy-start(bf16[514,384]{0,1:T(8,128)(2,1)S(1)} %convert_element_type.528) | copy-start | bytes 1184260 | tf_op jit(solution)/shard_map/while
  227.5 11.1 copy-start.30
  228.1 10.4 copy-start.45
  270.5 9.4 copy-start.49
  270.5 9.4 copy-start.29
  270.6 9.4 copy-start.33
  270.6 9.3 copy-start.35
  293.4 8.5 copy-start.24
  293.5 8.5 copy-start.53
  293.5 8.5 copy-start.55
  293.5 30.3 %copy-start.36 = (bf16[1536]{0:T(1024)(128)(2,1)}, bf16[1536]{0:T(1024)(128)(2,1)S(1)}, u32[]{:S(2)}) copy-start(bf16[1536]{0:T(1024)(128)(2,1)S(1)} %get-tuple-element.1023) | copy-start | bytes 9220 | tf_op jit(solution)/shard_map/while
  321.0 13.2 %copy-start.7 = (bf16[514,384]{0,1:T(8,128)(2,1)}, bf16[514,384]{0,1:T(8,128)(2,1)S(1)}, u32[]{:S(2)}) copy-start(bf16[514,384]{0,1:T(8,128)(2,1)S(1)} %convert_element_type.528) | copy-start | bytes 1184260 | tf_op jit(solution)/shard_map/while
  323.1 11.1 copy-start.30
  323.8 10.4 copy-start.45
  366.8 9.4 copy-start.49
  366.9 9.4 copy-start.29
  366.9 9.4 copy-start.33
  366.9 9.3 copy-start.35
  391.4 8.5 copy-start.24
  391.4 8.5 copy-start.53
  391.4 8.5 copy-start.55
  391.4 30.3 %copy-start.36 = (bf16[1536]{0:T(1024)(128)(2,1)}, bf16[1536]{0:T(1024)(128)(2,1)S(1)}, u32[]{:S(2)}) copy-start(bf16[1536]{0:T(1024)(128)(2,1)S(1)} %get-tuple-element.1023) | copy-start | bytes 9220 | tf_op jit(solution)/shard_map/while
  418.9 13.2 %copy-start.7 = (bf16[514,384]{0,1:T(8,128)(2,1)}, bf16[514,384]{0,1:T(8,128)(2,1)S(1)}, u32[]{:S(2)}) copy-start(bf16[514,384]{0,1:T(8,128)(2,1)S(1)} %convert_element_type.528) | copy-start | bytes 1184260 | tf_op jit(solution)/shard_map/while
  421.0 11.1 copy-start.30
  421.7 10.4 copy-start.45
  464.8 9.4 copy-start.49
  464.8 9.4 copy-start.29
  464.8 9.4 copy-start.33
  464.8 9.3 copy-start.35
  489.3 8.5 copy-start.24
  489.3 8.5 copy-start.53
  489.3 8.5 copy-start.55
  489.3 30.3 %copy-start.36 = (bf16[1536]{0:T(1024)(128)(2,1)}, bf16[1536]{0:T(1024)(128)(2,1)S(1)}, u32[]{:S(2)}) copy-start(bf16[1536]{0:T(1024)(128)(2,1)S(1)} %get-tuple-element.1023) | copy-start | bytes 9220 | tf_op jit(solution)/shard_map/while
  516.8 13.2 %copy-start.7 = (bf16[514,384]{0,1:T(8,128)(2,1)}, bf16[514,384]{0,1:T(8,128)(2,1)S(1)}, u32[]{:S(2)}) copy-start(bf16[514,384]{0,1:T(8,128)(2,1)S(1)} %convert_element_type.528) | copy-start | bytes 1184260 | tf_op jit(solution)/shard_map/while
  519.0 11.1 copy-start.30
  519.6 10.4 copy-start.45
  562.7 9.4 copy-start.49
  562.7 9.4 copy-start.29
  562.7 9.4 copy-start.33
  562.7 9.3 copy-start.35
  600.1 250.1 %reduce-scatter.13.cloned.1.call-start = ((), (), s32[]{:S(2)}) async-start(), calls=%async_computation.8 | async-start | bytes 1880064
  600.7 516.1 %copy-start.79 = (bf16[384]{0:T(512)(128)(2,1)S(1)}, bf16[384]{0:T(512)(128)(2,1)}, u32[]{:S(2)}) copy-start(bf16[384]{0:T(512)(128)(2,1)} %get-tuple-element.898) | copy-start | bytes 2308
  600.7 382.2 %reduce-scatter.9.cloned.1.call-start = ((), (), s32[]{:S(2)}) async-start(), calls=%async_computation.6 | async-start | bytes 2506752 | tf_op jit(solution)/shard_map/reduce_scatter | solution.py:296
  601.3 513.9 %reduce-scatter.11.cloned.1.call-start = ((), (), s32[]{:S(2)}) async-start(), calls=%async_computation.7 | async-start | bytes 2506752 | tf_op jit(solution)/shard_map/reduce_scatter | solution.py:298
  601.9 680.9 %all-reduce.25.cloned.1.call-start = ((), (), s32[]{:S(2)}) async-start(), calls=%async_computation.10 | async-start | bytes 155648 | tf_op jit(solution)/shard_map/psum | solution.py:302
  851.8 443.0 %all-reduce.27.cloned.1.call-start = ((), (), s32[]{:S(2)}) async-start(), calls=%async_computation.11 | async-start | bytes 294912 | tf_op jit(solution)/shard_map/psum | solution.py:310
  (258 other events, 916.2 us)
Sparse Core Ops, SparseCore 0:
  10.9 58.9 all-gather.2
  72.7 55.6 all-gather.4
  600.3 119.0 reduce-scatter.14
  724.8 125.4 reduce-scatter.12
  856.4 126.5 reduce-scatter.8
  987.7 127.4 reduce-scatter.10
  1119.7 18.2 all-reduce.24
  1141.0 19.1 all-reduce.26
where the time goes:
time: 1310 us; the launch traced here: 1300 us
  waiting for transfers between devices  432 us (33%)
  matrix products  255 us (19%)
  blocking collectives  234 us (18%)
  local copies, waits for them, and re-layouts  197 us (15%)
  other arithmetic  132 us (10%)
  loops' own time  35.8 us (3%)
  between operations  18.6 us (1%)
    unnamed x10, waiting for transfers between devices  170 us
    unnamed x2, blocking collectives  151 us
    reduce_scatter x1, waiting for transfers between devices, per_device(): lax.psum_scatter(totals[8], 'fsdp', scatter_dimension=0, tiled=True)  131 us
    reduce_scatter x1, waiting for transfers between devices, per_device(): lax.psum_scatter(totals[10], 'fsdp', scatter_dimension=0, tiled=True)  131 us
    while x612, local copies, waits for them, and re-layouts  57 us
    all_gather x1, blocking collectives, per_device(): lax.all_gather(qkv_weight, 'fsdp', axis=0, tiled=True)  44.4 us
    dot_general x4, matrix products, block_forward(): jnp.dot(normed2, fc1_weight, preferred_element_type=jnp.float32)  41.6 us
    dot_general x4, matrix products, block_forward(): jnp.dot(activated_low, fc2_weight, preferred_element_type=jnp.float32)  40 us
  transfers between devices with their start and end apart: 8, of which 4 were waited for; matrix products, arithmetic and copies ran while one was open for 15% of the time, Pallas kernels for 0%

commit v1 on v0

v1 whole, which is shorter than its diff:
```python
import functools
import jax
import jax.numpy as jnp
from jax import lax
from jax.experimental import pallas as pl
from jax.experimental.pallas import tpu as pltpu
from jax.sharding import PartitionSpec as P

HEADS = 6
HD = 64
EPS = 1e-06
F32 = jnp.float32
BF16 = jnp.bfloat16

NN = (((1,), (0,)), ((), ()))
NT = (((1,), (1,)), ((), ()))


def mm(a, b, dims=NN):
    return lax.dot_general(a, b, dims, preferred_element_type=F32)


def normalise(v):
    mu = jnp.mean(v, 0, keepdims=True)
    c = v - mu
    r = lax.rsqrt(jnp.mean(c * c, 0, keepdims=True) + EPS)
    return c * r, r


def norm_back(dn, u, r, gain):
    e = dn * gain
    me = jnp.mean(e, 0, keepdims=True)
    meu = jnp.mean(e * u, 0, keepdims=True)
    return r * (e - me - u * meu)


def fold(v):
    lanes = v.shape[1]
    total = v[:, :128]
    for k in range(1, lanes // 128):
        total = total + v[:, 128 * k : 128 * (k + 1)]
    return total


def wide(col, lanes):
    if lanes == 128:
        return col
    return jnp.concatenate([col] * (lanes // 128), 1)


def gelu_pair(x):
    e = jnp.exp(x * x * -0.5)
    d = 1.0 + 0.231641888 * jnp.abs(x)
    t = pl.reciprocal(d, approx=True)
    t = t * (2.0 - d * t)
    poly = t * (0.127414796 + t * (-0.142248368 + t * (0.710706871 + t * (-0.726576014 + t * 0.530702715))))
    h = poly * e
    phi = jnp.where(x >= 0.0, 1.0 - h, h)
    return x * phi, phi + x * (e * 0.3989422804014327)


def rows_of(values):
    return jnp.concatenate(values, 0)


MESH_ID = pl.DeviceIdType.MESH
NZ = 4


def place():
    p = lax.axis_index("fsdp")
    c = lax.axis_index("dp")
    x = lax.rem(p, 2)
    y = lax.rem(lax.div(p, 2), 2)
    z = lax.div(p, 4)
    return x, y, z, c


def index_of(x, y, z):
    return (z * 2 + y) * 2 + x


def greet(x, y, z, c):
    barrier = pltpu.get_barrier_semaphore()
    pl.semaphore_signal(barrier, inc=1, device_id=(index_of(1 - x, y, z), c), device_id_type=MESH_ID)
    pl.semaphore_signal(barrier, inc=1, device_id=(index_of(x, 1 - y, z), c), device_id_type=MESH_ID)
    pl.semaphore_signal(barrier, inc=1, device_id=(index_of(x, y, z), 1 - c), device_id_type=MESH_ID)
    for step in range(1, NZ):
        other = lax.rem(z + step, NZ)
        pl.semaphore_signal(barrier, inc=1, device_id=(index_of(x, y, other), c), device_id_type=MESH_ID)
    pl.semaphore_wait(barrier, 3 + NZ - 1)


def remote(src, dst, sems, k, device):
    return pltpu.make_async_remote_copy(
        src_ref=src, dst_ref=dst, send_sem=sems.at[0, k], recv_sem=sems.at[1, k],
        device_id=device, device_id_type=MESH_ID,
    )


def gather_body(qkv, outw, fc1, fc2, vec, slots1, slots2, slots_v, sems1, sems2, semsv, sib):
    x, y, z, c = place()
    d = outw.shape[1]

    f = fc1[...].astype(F32)
    q = qkv[...].astype(F32)

    @pl.when(c == 0)
    def _():
        slots1[0, y, x, z] = jnp.concatenate([q[:, :d], q[:, d : 2 * d]], 0).astype(BF16)
        slots2[0, y, x, z] = jnp.concatenate([f[:, k * d : (k + 1) * d] for k in range(4)], 0).astype(BF16)

    @pl.when(c == 1)
    def _():
        slots1[1, y, x, z] = jnp.concatenate([q[:, 2 * d :], outw[...].astype(F32)], 0).astype(BF16)
        slots2[1, y, x, z] = fc2[...]

    slots_v[y, x, z] = vec[...]
    greet(x, y, z, c)

    def line(buf, sems):
        copies = []
        for step in range(1, NZ):
            other = lax.rem(z + step, NZ)
            copy = remote(buf.at[y, x, z], buf.at[y, x, z], sems, step - 1, (index_of(x, y, other), c))
            copy.start()
            copies.append(copy)
        return copies

    def across(buf, sems, first):
        copies = []
        if first == "x":
            copies.append(remote(buf.at[y, x], buf.at[y, x], sems, 3, (index_of(1 - x, y, z), c)))
            copies[-1].start()
            copies[-1].wait()
            copies.append(remote(buf.at[y], buf.at[y], sems, 4, (index_of(x, 1 - y, z), c)))
            copies[-1].start()
            copies[-1].wait()
        else:
            copies.append(remote(buf.at[y, x], buf.at[y, x], sems, 3, (index_of(x, 1 - y, z), c)))
            copies[-1].start()
            copies[-1].wait()
            pair = [
                remote(buf.at[k, x], buf.at[k, x], sems, 4 + k, (index_of(1 - x, y, z), c)) for k in range(2)
            ]
            for copy in pair:
                copy.start()
            for copy in pair:
                copy.wait()

    def path(group, first):
        one, two = slots1.at[group], slots2.at[group]
        flights = line(slots_v, semsv) + line(one, sems1) + line(two, sems2)
        for copy in flights[:3]:
            copy.wait()
        for copy in flights[3:6]:
            copy.wait()
        across(slots_v, semsv, first)
        across(one, sems1, first)
        swap = remote(one, one, sib, 0, (index_of(x, y, z), 1 - c))
        swap.start()
        for copy in flights[6:]:
            copy.wait()
        across(two, sems2, first)
        swap2 = remote(two, two, sib, 1, (index_of(x, y, z), 1 - c))
        swap2.start()
        swap.wait()
        swap2.wait()

    @pl.when(c == 0)
    def _():
        path(0, "x")

    @pl.when(c == 1)
    def _():
        path(1, "y")


def reduce_body(
    gqkv, gout, g1, g2, gvec,
    oqkv, oout, o1, o2, ovec,
    t1, t2, u1, u2, a1, a2, b1, b2, z1, z2, f1, f2, va, vz, sems1, sems2, semsv,
):
    x, y, z, c = place()
    d = gout.shape[1]
    rows = gout.shape[0] // 16

    def stage(buf, group, blocks):
        for p in range(16):
            part = [b[rows * p : rows * (p + 1)] for b in blocks]
            buf[group, (p // 2) % 2, p % 2, p // 4] = jnp.concatenate(part, 0).astype(BF16)

    q = gqkv[...].astype(F32)
    stage(t1, 0, [q[:, :d], q[:, d : 2 * d]])
    stage(t1, 1, [q[:, 2 * d :], gout[...].astype(F32)])
    f = g1[...].astype(F32)
    stage(t2, 0, [f[:, k * d : (k + 1) * d] for k in range(4)])
    for p in range(16):
        t2[1, (p // 2) % 2, p % 2, p // 4] = g2[4 * rows * p : 4 * rows * (p + 1), :]
    va[0] = gvec[...]
    greet(x, y, z, c)

    sibling = (index_of(x, y, z), 1 - c)
    xn = (index_of(1 - x, y, z), c)
    yn = (index_of(x, 1 - y, z), c)

    def add(dst, src):
        dst[...] = (dst[...].astype(F32) + src[...].astype(F32)).astype(BF16)

    def send_all(copies):
        for copy in copies:
            copy.start()
        return copies

    def wait_all(copies):
        for copy in copies:
            copy.wait()

    def z_copies(src, dst, sems, base):
        copies = []
        for step in range(1, NZ):
            other = lax.rem(z + step, NZ)
            copies.append(remote(src(other), dst.at[step - 1], sems, base + step - 1, (index_of(x, y, other), c)))
        return copies

    def path(group, order):
        units = ((t1.at[group], u1, a1, b1, z1, f1, sems1), (t2.at[group], u2, a2, b2, z2, f2, sems2))
        swaps = [
            send_all([remote(full.at[1 - group], got, sems, 0, sibling)])
            for full, got, sems in ((t1, u1, sems1), (t2, u2, sems2))
        ]
        for (buf, got, *_), copies in zip(units, swaps):
            wait_all(copies)
            add(buf, got)
        flights = []
        for buf, got, ra, rb, rz, fin, sems in units:
            if order == "yx":
                flights.append(send_all([remote(buf.at[1 - y], ra, sems, 1, yn)]))
            else:
                flights.append(
                    send_all([remote(buf.at[k, 1 - x], ra.at[k], sems, 1 + k, xn) for k in range(2)])
                )
        for (buf, got, ra, rb, rz, fin, sems), copies in zip(units, flights):
            wait_all(copies)
            if order == "yx":
                add(buf.at[y], ra)
            else:
                for k in range(2):
                    add(buf.at[k, x], ra.at[k])
        flights = []
        for buf, got, ra, rb, rz, fin, sems in units:
            if order == "yx":
                flights.append(send_all([remote(buf.at[y, 1 - x], rb, sems, 3, xn)]))
            else:
                flights.append(send_all([remote(buf.at[1 - y, x], rb, sems, 3, yn)]))
        for (buf, got, ra, rb, rz, fin, sems), copies in zip(units, flights):
            wait_all(copies)
            add(buf.at[y, x], rb)
        flights = []
        for buf, got, ra, rb, rz, fin, sems in units:
            flights.append(send_all(z_copies(lambda k, buf=buf: buf.at[y, x, k], rz, sems, 4)))
        flights2 = []
        for (buf, got, ra, rb, rz, fin, sems), copies in zip(units, flights):
            wait_all(copies)
            total = buf[y, x, z].astype(F32)
            for k in range(NZ - 1):
                total = total + rz[k].astype(F32)
            fin[group] = total
            flights2.append(send_all([remote(fin.at[group], fin.at[group], sems, 7, sibling)]))
        for copies in flights2:
            wait_all(copies)

    for k, device in enumerate((sibling, xn, yn)):
        copy = remote(va.at[2 * k], va.at[2 * k + 1], semsv, k, device)
        copy.start()
        copy.wait()
        va[2 * k + 2] = va[2 * k] + va[2 * k + 1]
    vz[z] = va[6]
    copies = [
        remote(vz.at[z], vz.at[z], semsv, 2 + step, (index_of(x, y, lax.rem(z + step, NZ)), c))
        for step in range(1, NZ)
    ]
    send_all(copies)
    wait_all(copies)
    ovec[...] = vz[0] + vz[1] + vz[2] + vz[3]

    @pl.when(c == 0)
    def _():
        path(0, "yx")

    @pl.when(c == 1)
    def _():
        path(1, "xy")

    oqkv[:, :d] = f1[0, :rows]
    oqkv[:, d : 2 * d] = f1[0, rows:]
    oqkv[:, 2 * d :] = f1[1, :rows]
    oout[...] = f1[1, rows:]
    for k in range(4):
        o1[:, k * d : (k + 1) * d] = f2[0, rows * k : rows * (k + 1)]
    o2[...] = f2[1]


def gather_call(qkv, outw, fc1, fc2, vec):
    rows, d = outw.shape
    dma = pltpu.SemaphoreType.DMA
    spec = pl.BlockSpec(memory_space=pltpu.VMEM)
    return pl.pallas_call(
        gather_body,
        out_shape=(
            jax.ShapeDtypeStruct((2, 2, 2, NZ, 2 * rows, d), BF16),
            jax.ShapeDtypeStruct((2, 2, 2, NZ, 4 * rows, d), BF16),
            jax.ShapeDtypeStruct((2, 2, NZ) + vec.shape, vec.dtype),
        ),
        in_specs=[spec] * 5,
        out_specs=(spec,) * 3,
        scratch_shapes=[dma((2, 6)), dma((2, 6)), dma((2, 6)), dma((2, 2))],
        compiler_params=pltpu.CompilerParams(collective_id=0, has_side_effects=True, vmem_limit_bytes=48 * 1024 * 1024),
        name="gather",
    )(qkv, outw, fc1, fc2, vec)


def reduce_call(gqkv, gout, g1, g2, gvec):
    d = gout.shape[1]
    rows = d // 16
    dma = pltpu.SemaphoreType.DMA
    vm = pltpu.VMEM
    spec = pl.BlockSpec(memory_space=pltpu.VMEM)

    def pair(lead, dtype=BF16):
        return [vm(lead + (2 * rows, d), dtype), vm(lead + (4 * rows, d), dtype)]

    return pl.pallas_call(
        reduce_body,
        out_shape=(
            jax.ShapeDtypeStruct((rows, 3 * d), F32),
            jax.ShapeDtypeStruct((rows, d), F32),
            jax.ShapeDtypeStruct((rows, 4 * d), F32),
            jax.ShapeDtypeStruct((4 * rows, d), F32),
            jax.ShapeDtypeStruct(gvec.shape, F32),
        ),
        in_specs=[spec] * 5,
        out_specs=(spec,) * 5,
        scratch_shapes=pair((2, 2, 2, NZ)) + pair((2, 2, NZ)) + pair((2, NZ)) + pair((NZ,)) + pair((NZ - 1,))
        + pair((2,), F32) + [vm((7,) + gvec.shape, F32), vm((NZ,) + gvec.shape, F32)]
        + [dma((2, 8)), dma((2, 8)), dma((2, 8))],
        compiler_params=pltpu.CompilerParams(collective_id=1, has_side_effects=True, vmem_limit_bytes=48 * 1024 * 1024),
        name="reduce",
    )(gqkv, gout, g1, g2, gvec)


LN1G, LN1B, BQKV, BOUT, LN2G, LN2B, BFC1, BFC2 = range(8)


def to_columns(vec, row, count):
    return jnp.broadcast_to(vec[row : row + 1, :count], (128, count)).T


def compute_body(
    tok, dup, tgt, vec, wqkv, wout, w1, w2,
    out, gin, gqkv, gout, g1, g2, gvec,
    xs, n1, qkv, att, n2, act, dpre, db2, db1, dos, dmid, probs,
    wqkv_t, wout_t, w1_t, w2_t,
    c_ln1g, c_ln1b, c_bqkv, c_bout, c_ln2g, c_ln2b, c_b1, c_b2,
    rl_s, ex_s, exq_s, rlx_s, exx_s, attx, dqkvx, a_g1, a_b1, a_g2, a_b2, tgt_t, stage, gin_sem,
):
    images, seq = dup.shape
    d = tok.shape[1]
    t = seq - 1
    x0 = images * t
    ff = w1.shape[1]
    w = x0 + 128
    dqkv = act.at[: 3 * d]

    blocks = d // 128

    def load_image(i):
        return jnp.concatenate([stage[b, pl.ds(i, t, stride=images), :] for b in range(blocks)], 1)

    def store_image(i, values):
        for b in range(blocks):
            stage[b, pl.ds(i, t, stride=images), :] = values[:, 128 * b : 128 * (b + 1)]

    def store_last(values):
        for b in range(blocks):
            stage[b, x0:, :] = values[:images, 128 * b : 128 * (b + 1)]

    def lanes_of(i):
        return pl.ds(pl.multiple_of(i * t, 128), t)

    extra_lanes = pl.ds(x0, 128)

    wqkv_t[...] = wqkv[...].T
    wout_t[...] = wout[...].T
    w1_t[...] = w1[...].T
    w2_t[...] = w2[...].T
    c_ln1g[...] = to_columns(vec, LN1G, d)
    c_ln1b[...] = to_columns(vec, LN1B, d)
    c_bqkv[...] = to_columns(vec, BQKV, 3 * d)
    c_bout[...] = to_columns(vec, BOUT, d)
    c_ln2g[...] = to_columns(vec, LN2G, d)
    c_ln2b[...] = to_columns(vec, LN2B, d)
    c_b1[...] = to_columns(vec, BFC1, ff)
    c_b2[...] = to_columns(vec, BFC2, d)
    tgt_t[...] = jnp.concatenate([tgt[...], jnp.zeros((128 - images, d), F32)], 0).T
    ones_row = jnp.where(lax.broadcasted_iota(jnp.int32, (16, w), 0) == 0, 1.0, 0.0).astype(BF16)
    n1[d : d + 16, :] = ones_row
    n2[d : d + 16, :] = ones_row
    att[d : d + 16, :] = ones_row
    act[ff : ff + 16, :] = ones_row
    attx[...] = jnp.zeros_like(attx)
    dqkvx[...] = jnp.zeros_like(dqkvx)
    for acc in (a_g1, a_b1, a_g2, a_b2):
        acc[...] = jnp.zeros_like(acc)

    def project(x_t, lanes, count):
        x = x_t.astype(F32)
        xs[:, lanes] = x_t
        u, r = normalise(x)
        n = (u * wide(c_ln1g[...], count) + wide(c_ln1b[...], count)).astype(BF16)
        n1[:d, lanes] = n
        for k in range(3):
            rows = slice(k * d, (k + 1) * d)
            y = mm(wqkv_t[rows, :], n) + wide(c_bqkv[rows, :], count)
            y = y.astype(BF16)
            if k == 0:
                y = y * jnp.asarray(HD**-0.5, BF16)
            qkv[rows, lanes] = y

    def project_image(i, carry):
        project(load_image(i).astype(BF16).T, lanes_of(i), t)
        return carry

    for b in range(blocks):
        stage[b] = tok[:, 128 * b : 128 * (b + 1)].astype(F32)

    lax.fori_loop(0, images, project_image, 0)
    last = jnp.concatenate([tok[x0:, :].astype(F32), jnp.zeros((128 - images, d), F32)], 0)
    project(last.astype(BF16).T, extra_lanes, 128)

    lane_ids = lax.broadcasted_iota(jnp.int32, (HD, 128), 1)

    def pick(ref, row, i):
        block = ref[row : row + HD, extra_lanes].astype(F32)
        return jnp.sum(jnp.where(lane_ids == i, block, 0.0), 1, keepdims=True)

    def attend_image(i, carry):
        lanes = lanes_of(i)
        for h in range(HEADS):
            r0 = h * HD
            q = qkv[r0 : r0 + HD, lanes]
            k = qkv[d + r0 : d + r0 + HD, lanes]
            v = qkv[2 * d + r0 : 2 * d + r0 + HD, lanes]
            qx, kx, vx = pick(qkv, r0, i), pick(qkv, d + r0, i), pick(qkv, 2 * d + r0, i)
            s = mm(k.T, q)
            sx = jnp.sum(q.astype(F32) * kx, 0, keepdims=True)
            top = jnp.maximum(jnp.max(s, 0, keepdims=True), sx)
            e = jnp.exp(s - top)
            ex = jnp.exp(sx - top)
            rl = 1.0 / (jnp.sum(e, 0, keepdims=True) + ex)
            e = e.astype(BF16)
            probs[i * HEADS + h] = e
            o = (mm(v, e) + vx * ex) * rl
            att[r0 : r0 + HD, lanes] = o.astype(BF16)
            rl_s[i, h : h + 1, :] = rl
            ex_s[i, h : h + 1, :] = ex
            sq = jnp.sum(k.astype(F32) * qx, 0, keepdims=True)
            sxx = jnp.sum(kx * qx, 0, keepdims=True)
            topx = jnp.maximum(jnp.max(sq, 1, keepdims=True), sxx)
            eq = jnp.exp(sq - topx)
            exx = jnp.exp(sxx - topx)
            rlx = 1.0 / (jnp.sum(eq, 1, keepdims=True) + exx)
            ox = (jnp.sum(v.astype(F32) * eq, 1, keepdims=True) + vx * exx) * rlx
            attx[r0 : r0 + HD, :] = jnp.where(lane_ids == i, ox, attx[r0 : r0 + HD, :])
            exq_s[i, h : h + 1, :] = eq
            rlx_s[i, h : h + 1, :] = jnp.broadcast_to(rlx, (1, 128))
            exx_s[i, h : h + 1, :] = jnp.broadcast_to(exx, (1, 128))
        return carry

    lax.fori_loop(0, images, attend_image, 0)
    att[:d, extra_lanes] = attx[...].astype(BF16)

    def feed(lanes, count, d_final):
        mid = xs[:, lanes].astype(F32) + mm(wout_t[...], att[:d, lanes]) + wide(c_bout[...], count)
        u, r = normalise(mid)
        n = (u * wide(c_ln2g[...], count) + wide(c_ln2b[...], count)).astype(BF16)
        n2[:d, lanes] = n
        db = d_final.astype(BF16)
        db2[:, lanes] = db
        for j in range(ff // 256):
            rows = slice(256 * j, 256 * (j + 1))
            pre = mm(w1_t[rows, :], n) + wide(c_b1[rows, :], count)
            da = mm(w2[rows, :], db)
            value, slope = gelu_pair(pre)
            act[rows, lanes] = value.astype(BF16)
            dpre[rows, lanes] = (slope * da).astype(BF16)
        final = mid + mm(w2_t[...], act[:ff, lanes]) + wide(c_b2[...], count)
        dn = mm(w1[...], dpre[:, lanes])
        a_g2[...] += fold(dn * u)
        a_b2[...] += fold(dn)
        dm = d_final + norm_back(dn, u, r, wide(c_ln2g[...], count))
        dmid[:, lanes] = dm
        low = dm.astype(BF16)
        db1[:, lanes] = low
        dos[:, lanes] = mm(wout[...], low).astype(BF16)
        return final.T

    def keep_row(row):
        first = lax.broadcasted_iota(jnp.int32, row.shape, 1) == 0
        return jnp.where(first, 1.0, 1.0 - row.astype(F32))

    def feed_image(i, carry):
        keep = keep_row(dup[pl.ds(i, 1), :])
        count = jnp.sum(keep, 1, keepdims=True)
        scale = seq * keep[:, :t] / count
        ids = lax.broadcasted_iota(jnp.int32, (d, 128), 1)
        target = jnp.sum(jnp.where(ids == i, tgt_t[...], 0.0), 1, keepdims=True)
        store_image(i, feed(lanes_of(i), t, target * scale))
        return carry

    lax.fori_loop(0, images, feed_image, 0)
    keep_all = keep_row(dup[...])
    scale_x = seq * keep_all[:, t:] / jnp.sum(keep_all, 1, keepdims=True)
    scale_x = jnp.broadcast_to(scale_x, (images, 128))
    scale_x = jnp.concatenate([scale_x, jnp.zeros((128 - images, 128), F32)], 0).T[:1, :]
    store_last(feed(extra_lanes, 128, tgt_t[...] * scale_x))
    for b in range(blocks):
        out[:, 128 * b : 128 * (b + 1)] = stage[b].astype(BF16)

    for j in range(ff // 256):
        rows = slice(256 * j, 256 * (j + 1))
        g = mm(n2[...], dpre[rows, :], NT)
        g1[:, rows] = g[:d].astype(BF16)
        gvec[BFC1 : BFC1 + 1, rows] = g[d : d + 1]
        g2[rows, :] = mm(act[rows, :], db2[...], NT).astype(BF16)
    g = mm(act[ff : ff + 16, :], db2[...], NT)
    gvec[BFC2 : BFC2 + 1, :d] = g[:1]

    def attend_back(i, carry):
        lanes = lanes_of(i)
        for h in range(HEADS):
            r0 = h * HD
            q = qkv[r0 : r0 + HD, lanes]
            k = qkv[d + r0 : d + r0 + HD, lanes]
            v = qkv[2 * d + r0 : 2 * d + r0 + HD, lanes]
            qx, kx, vx = pick(qkv, r0, i), pick(qkv, d + r0, i), pick(qkv, 2 * d + r0, i)
            rl = rl_s[i, h : h + 1, :]
            ex = ex_s[i, h : h + 1, :]
            do = dos[r0 : r0 + HD, lanes].astype(F32) * rl
            dot_o = jnp.sum(do * att[r0 : r0 + HD, lanes].astype(F32), 0, keepdims=True)
            dol = do.astype(BF16)
            p = probs[i * HEADS + h]
            ds = (p.astype(F32) * (mm(v.T, dol) - dot_o)).astype(BF16)
            dsx = ex * (jnp.sum(do * vx, 0, keepdims=True) - dot_o)
            dq = mm(k, ds) + kx * dsx
            dk = mm(q, ds, NT)
            dv = mm(dol, p, NT)
            qf = q.astype(F32)
            kf = k.astype(F32)
            vf = v.astype(F32)
            dkx = jnp.sum(qf * dsx, 1, keepdims=True)
            dvx = jnp.sum(do * ex, 1, keepdims=True)
            eq = exq_s[i, h : h + 1, :]
            rlx = rlx_s[i, h : h + 1, :1]
            exx = exx_s[i, h : h + 1, :1]
            dox = pick(dos, r0, i) * rlx
            dotx = jnp.sum(dox * pick(att, r0, i), 0, keepdims=True)
            dsq = eq * (jnp.sum(vf * dox, 0, keepdims=True) - dotx)
            dsxx = exx * (jnp.sum(vx * dox, 0, keepdims=True) - dotx)
            dqx = jnp.sum(kf * dsq, 1, keepdims=True) + kx * dsxx
            dk = dk + qx * dsq
            dv = dv + dox * eq
            dkx = dkx + qx * dsxx
            dvx = dvx + dox * exx
            scale = HD**-0.5
            for base, main, tail in ((0, dq * scale, dqx * scale), (d, dk, dkx), (2 * d, dv, dvx)):
                rows = slice(base + r0, base + r0 + HD)
                dqkv[rows, lanes] = main.astype(BF16)
                dqkvx[rows, :] = jnp.where(lane_ids == i, tail, dqkvx[rows, :])
        return carry

    lax.fori_loop(0, images, attend_back, 0)
    dqkv[:, extra_lanes] = dqkvx[...].astype(BF16)

    for k in range(3):
        rows = slice(k * d, (k + 1) * d)
        g = mm(n1[...], dqkv[rows, :], NT)
        gqkv[:, rows] = g[:d].astype(BF16)
        gvec[BQKV : BQKV + 1, rows] = g[d : d + 1]
    g = mm(att[...], db1[...], NT)
    gout[...] = g[:d].astype(BF16)
    gvec[BOUT : BOUT + 1, :d] = g[d : d + 1]

    def finish(lanes, count):
        u, r = normalise(xs[:, lanes].astype(F32))
        dn = mm(wqkv[...], dqkv[:, lanes])
        a_g1[...] += fold(dn * u)
        a_b1[...] += fold(dn)
        return (dmid[:, lanes] + norm_back(dn, u, r, wide(c_ln1g[...], count))).T

    def finish_image(i, carry):
        store_image(i, finish(lanes_of(i), t))
        return carry

    lax.fori_loop(0, images, finish_image, 0)
    store_last(finish(extra_lanes, 128))
    copies = [
        pltpu.make_async_copy(stage.at[b], gin.at[:, pl.ds(128 * b, 128)], gin_sem.at[b]) for b in range(blocks)
    ]
    for copy in copies:
        copy.start()

    for row, acc in ((LN1G, a_g1), (LN1B, a_b1), (LN2G, a_g2), (LN2B, a_b2)):
        gvec[row : row + 1, :d] = jnp.sum(acc[...].T, 0, keepdims=True)
    for copy in copies:
        copy.wait()


def compute(tok, dup, tgt, vec, wqkv, wout, w1, w2):
    images, seq = dup.shape
    d = tok.shape[1]
    ff = w1.shape[1]
    t = seq - 1
    w = images * t + 128
    vm = pltpu.VMEM
    scratch = [
        vm((d, w), BF16),
        vm((d + 16, w), BF16),
        vm((3 * d, w), BF16),
        vm((d + 16, w), BF16),
        vm((d + 16, w), BF16),
        vm((ff + 16, w), BF16),
        vm((ff, w), BF16),
        vm((d, w), BF16),
        vm((d, w), BF16),
        vm((d, w), BF16),
        vm((d, w), F32),
        vm((images * HEADS, t, t), BF16),
        vm((3 * d, d), BF16),
        vm((d, d), BF16),
        vm((ff, d), BF16),
        vm((d, ff), BF16),
        vm((d, 128), F32), vm((d, 128), F32), vm((3 * d, 128), F32), vm((d, 128), F32),
        vm((d, 128), F32), vm((d, 128), F32), vm((ff, 128), F32), vm((d, 128), F32),
        vm((images, 8, t), F32),
        vm((images, 8, t), F32),
        vm((images, 8, t), F32),
        vm((images, 8, 128), F32),
        vm((images, 8, 128), F32),
        vm((d, 128), F32),
        vm((3 * d, 128), F32),
        vm((d, 128), F32), vm((d, 128), F32), vm((d, 128), F32), vm((d, 128), F32),
        vm((d, 128), F32),
        vm((d // 128, images * seq, 128), F32),
        pltpu.SemaphoreType.DMA((d // 128,)),
    ]
    outs = (
        jax.ShapeDtypeStruct(tok.shape, BF16),
        jax.ShapeDtypeStruct(tok.shape, F32),
        jax.ShapeDtypeStruct((d, 3 * d), BF16),
        jax.ShapeDtypeStruct((d, d), BF16),
        jax.ShapeDtypeStruct((d, ff), BF16),
        jax.ShapeDtypeStruct((ff, d), BF16),
        jax.ShapeDtypeStruct((8, ff), F32),
    )
    spec = pl.BlockSpec(memory_space=pltpu.VMEM)
    return pl.pallas_call(
        compute_body,
        out_shape=outs,
        in_specs=[spec] * 8,
        out_specs=(spec, pl.BlockSpec(memory_space=pl.ANY)) + (spec,) * 5,
        scratch_shapes=scratch,
        compiler_params=pltpu.CompilerParams(vmem_limit_bytes=64 * 1024 * 1024),
        name="block",
    )(tok, dup, tgt, vec, wqkv, wout, w1, w2)

def gather_all(value):
    return lax.all_gather(value, "fsdp", axis=0, tiled=True)


def pack_rows(ln1_gain, ln1_bias, qv_bias, out_bias, ln2_gain, ln2_bias, fc1_bias, fc2_bias):
    n = ln1_gain.shape[0]
    rows = [ln1_gain, ln1_bias, qv_bias[:n], qv_bias[n:], out_bias, ln2_gain, ln2_bias, fc2_bias]
    rows += [fc1_bias[n * k : n * (k + 1)] for k in range(4)]
    table = jnp.stack(rows, 0)
    return jnp.pad(table, ((0, 4), (0, 128 - n)))


def vectors(full):
    ln1_gain, ln1_bias, qv_bias, out_bias, ln2_gain, ln2_bias, fc1_bias, fc2_bias = full
    d = ln1_gain.shape[0]
    bias = jnp.concatenate([qv_bias[:d], jnp.zeros((d,), qv_bias.dtype), qv_bias[d:]])
    rows = (ln1_gain, ln1_bias, bias, out_bias, ln2_gain, ln2_bias, fc1_bias, fc2_bias)
    width = fc1_bias.shape[0]
    return jnp.stack([jnp.pad(row.astype(F32), (0, width - row.shape[0])) for row in rows], 0)


def per_device(
    tokens, duplicate, targets,
    ln1_gain, ln1_bias, qkv_weight, qv_bias, out_weight, out_bias,
    ln2_gain, ln2_bias, fc1_weight, fc1_bias, fc2_weight, fc2_bias,
    block16,
):
    images, seq, d = tokens.shape
    small = (ln1_gain, ln1_bias, qv_bias, out_bias, ln2_gain, ln2_bias, fc1_bias, fc2_bias)
    rows = tokens.transpose(1, 0, 2).reshape(seq * images, d)
    if block16:
        n = d // 16
        slots1, slots2, slots_v = gather_call(
            qkv_weight, out_weight, fc1_weight, fc2_weight, pack_rows(*small).astype(BF16)
        )
        def whole(slots):
            return slots.transpose((2, 0, 1) + tuple(range(3, slots.ndim))).reshape((16,) + slots.shape[3:])

        g0, g1 = whole(slots1[0]), whole(slots1[1])
        wqkv = jnp.concatenate([g0[:, :n], g0[:, n:], g1[:, :n]], 2).reshape(d, 3 * d)
        wout = g1[:, n:].reshape(d, d)
        w1 = whole(slots2[0]).reshape(16, 4, n, d).transpose(0, 2, 1, 3).reshape(d, 4 * d)
        w2 = whole(slots2[1]).reshape(4 * d, d)
        table = whole(slots_v)[:, :12, :n]
        line = lambda k: table[:, k].reshape(d)
        qv = table[:, 2:4].reshape(2 * d)
        b1 = table[:, 8:12].reshape(4 * d)
        vec = vectors((line(0), line(1), qv, line(4), line(5), line(6), b1, line(7)))
    else:
        wqkv, wout, w1, w2 = map(gather_all, (qkv_weight, out_weight, fc1_weight, fc2_weight))
        vec = vectors(tuple(map(gather_all, small)))
    out, gin, gqkv, gout, g1, g2, gvec = compute(rows, duplicate, targets, vec, wqkv, wout, w1, w2)
    if block16:
        gqkv, gout, g1, g2, gvec = reduce_call(gqkv, gout, g1, g2, gvec)
        p = lax.axis_index("fsdp")
    else:
        def scatter(value):
            value = lax.psum_scatter(value.astype(F32), "fsdp", scatter_dimension=0, tiled=True)
            return lax.psum(value, "dp")

        gqkv, gout, g1, g2 = map(scatter, (gqkv, gout, g1, g2))
        gvec = lax.psum(gvec, ("fsdp", "dp"))
        p = lax.axis_index("fsdp")

    def shard(value, whole_size):
        count = whole_size // lax.axis_size("fsdp")
        return lax.dynamic_slice(value, (p * count,), (count,))

    qv_grad = jnp.concatenate([gvec[2, :d], gvec[2, 2 * d : 3 * d]])
    back = lambda v: v.reshape(seq, images, d).transpose(1, 0, 2)
    return (
        back(out), back(gin),
        shard(gvec[0], d), shard(gvec[1], d), gqkv, shard(qv_grad, 2 * d), gout, shard(gvec[3], d),
        shard(gvec[4], d), shard(gvec[5], d), g1, shard(gvec[6], 4 * d), g2, shard(gvec[7], d),
    )


def solution(mesh):
    block16 = mesh.shape["fsdp"] == 16 and mesh.shape["dp"] == 2
    both = ("fsdp", "dp")
    vector, matrix = P("fsdp"), P("fsdp", None)
    weights = (vector, vector, matrix, vector, matrix, vector, vector, vector, matrix, vector, matrix, vector)
    return jax.shard_map(
        functools.partial(per_device, block16=block16),
        mesh=mesh,
        in_specs=(P(both, None, None), P(both, None), P(both, None)) + weights,
        out_specs=(P(both, None, None), P(both, None, None)) + weights,
        check_vma=False,
    )
```

time: 1310 us -> 239 us (0.18)
  waiting for transfers between devices: 432 us -> 0 us
  matrix products: 255 us -> 0 us
  blocking collectives: 234 us -> 0 us
  Pallas kernels: 0 us -> 197 us
  local copies, waits for them, and re-layouts: 197 us -> 37.6 us
  other arithmetic: 132 us -> 2.38 us
  loops' own time: 35.8 us -> 0 us
  between operations: 18.6 us -> 0.85 us
    reduce_scatter x2 -> x0, waiting for transfers between devices: 262 us -> none  [the longest x1 131 us: per_device(): lax.psum_scatter(totals[8], 'fsdp', scatter_dimension=0, tiled=True)]
    dot_general x88 -> x0, matrix products: 255 us -> none  [the longest x4 41.6 us: block_forward(): jnp.dot(normed2, fc1_weight, preferred_element_type=jnp.float32)]
    pallas_call x0 -> x3, Pallas kernels: none -> 197 us  [the longest x1 94.6 us: compute(): pl.pallas_call(compute_body, out_shape=outs, in_specs=[spec] * 8, out_spe...]
    unnamed x10 -> x0, waiting for transfers between devices: 170 us -> none
    unnamed x2 -> x0, blocking collectives: 151 us -> none
    all_gather x2 -> x0, blocking collectives: 82.1 us -> none  [the longest x1 44.4 us: per_device(): lax.all_gather(qkv_weight, 'fsdp', axis=0, tiled=True)]
    convert_element_type x84 -> x0, other arithmetic: 57.1 us -> none  [the longest x4 8.55 us: block_forward(): normed1 = layer_norm(tok_rows, gain_one, shift_one).astype(jnp.bfloat16)]
    while x612 -> x0, local copies, waits for them, and re-layouts: 57 us -> none
  transfers between devices with their start and end apart: 8 -> 0, of which waited for: 4 -> 0; matrix products, arithmetic and copies ran while one was open for 15% -> 0% of each run, Pallas kernels for 0% -> 0%
where the time goes in v1:
time: 239 us; the launch traced here: 238 us
  Pallas kernels  197 us (82%)
  local copies, waits for them, and re-layouts  37.6 us (16%)
    pallas_call x1, Pallas kernels, compute(): pl.pallas_call(compute_body, out_shape=outs, in_specs=[spec] * 8, out_spe...  94.6 us
    pallas_call x1, Pallas kernels, reduce_call(): pl.pallas_call(reduce_body, out_shape=(jax.ShapeDtypeStruct((rows, 3 * d)...  53.1 us
    pallas_call x1, Pallas kernels, gather_call(): pl.pallas_call(gather_body, out_shape=(jax.ShapeDtypeStruct((2, 2, 2, NZ,...  49.6 us
    unnamed x25, local copies, waits for them, and re-layouts  13.2 us
    another operation x8, local copies, waits for them, and re-layouts, vectors(): jnp.stack([jnp.pad(row.astype(F32), (0, width - row.shape[0])) for row in...  5.68 us

profile of v1, /device:TPU:0, one launch (start us, length us, event | category | flops | bytes accessed | tf_op | source)
XLA Modules:
  0.0 238.1 jit_solution(7419758503724899944)
XLA Ops:
  0.6 0.9 slice_bitcast_fusion.4
  1.5 0.8 stack.85
  2.3 0.0 copy-start.4
  2.3 0.9 copy-done.4
  3.2 0.9 copy-done.5
  4.1 0.8 copy-done.6
  4.9 0.7 copy-done.8
  5.6 49.6 %gather.1 = (bf16[2,2,2,4,48,384]{5,4,3,2,1,0:T(8,128)(2,1)S(1)}, bf16[2,2,2,4,96,384]{5,4,3,2,1,0:T(8,128)(2,1)S(1)}, bf16[2,2,4,16,128]{4,3,2,1,0:T(8,128)(2,1)S(1)}) custom-call(bf16[24,1152]{1,0:T(8,128)(2,1)S(1)} %copy-done.6, bf16[24,384]{1,0:T(8,128)(2,1)S(1)} %copy-done.8, bf16[24,1536]{1,0:T(8,128)(2,1)S(1)} %copy-done.4, ...), custom_call_target="tpu_custom_call" | custom-call | tf_op jit(solution)/shard_map/gather/pallas_call | solution.py:308
  55.3 0.0 copy-start.9
  55.3 0.6 copy-done.9
  55.9 0.1 slice.123
  56.0 0.1 slice.125
  56.2 0.6 stack.88
  56.8 1.8 slice_reduce_fusion
  58.6 1.3 convert_element_type.47
  59.9 0.7 pad.35
  60.6 0.6 stack.86
  61.2 1.3 convert_element_type.48
  62.6 0.7 pad.36
  63.2 0.6 stack.87
  63.8 0.7 convert_element_type.49
  64.5 0.7 pad.38
  65.2 0.6 stack.89
  65.8 0.1 convert_element_type.50
  65.9 0.6 stack.90
  66.5 0.1 convert_element_type.51
  66.6 0.6 stack.91
  67.2 0.1 convert_element_type.53
  67.3 0.6 stack.92
  67.9 0.8 slice.155
  68.7 0.7 convert_element_type.52
  69.4 1.5 stack.93
  70.9 1.4 stack.94.vec
  72.2 0.1 slice_bitcast_fusion.3
  72.3 0.1 copy.32
  72.4 0.8 fusion.12
  73.2 0.1 copy.31
  73.2 0.1 fusion.13
  73.3 1.0 pad_maximum_fusion
  74.3 0.3 slice_bitcast_fusion
  74.6 0.1 copy.33
  74.8 0.5 copy.34
  75.2 1.2 copy.36
  76.4 1.2 copy.35
  77.6 94.6 %block.1 = (bf16[2056,384]{1,0:T(8,128)(2,1)}, f32[2056,384]{1,0:T(8,128)}, bf16[384,1152]{1,0:T(8,128)(2,1)}, bf16[384,384]{1,0:T(8,128)(2,1)}, bf16[384,1536]{...) custom-call(bf16[2056,384]{1,0:T(8,128)(2,1)} %bitcast.78, s32[8,257]{1,0:T(8,128)} %dup.1, ...), custom_call_target="tpu_custom_call" | custom-call | tf_op jit(solution)/shard_map/block/pallas_call | solution.py:667
  172.2 0.0 copy-start
  172.2 1.3 copy-done
  173.5 1.3 copy-done.1
  174.7 1.2 copy-done.2
  175.9 1.0 copy-done.3
  176.9 0.8 copy-done.7
  177.7 53.1 %reduce.17 = (f32[24,1152]{1,0:T(8,128)S(1)}, f32[24,384]{1,0:T(8,128)S(1)}, f32[24,1536]{1,0:T(8,128)S(1)}, f32[96,384]{1,0:T(8,128)S(1)}, f32[8,1536]{1,0:T(8,128)S(1)}) custom-call(bf16[384,1152]{1,0:T(8,128)(2,1)S(1)} %copy-done.2, bf16[384,384]{1,0:T(8,128)(2,1)S(1)} %copy-done.3, bf16[384,1536]{1,0:T(8,128)(2,1)S(1)} %copy-done, ...), custom_call_target="tpu_custom_call" | custom-call | tf_op jit(solution)/shard_map/reduce/pallas_call | solution.py:333
  230.8 0.6 dynamic_slice.42
  231.4 0.6 fusion.10
  232.0 0.6 fusion.11
  232.6 0.6 fusion.7
  233.2 0.6 fusion.8
  233.7 0.6 fusion.9
  234.3 0.6 fusion.6
  234.9 0.6 fusion.5
  235.5 0.6 copy.41
  236.1 0.6 copy.42
  236.7 0.7 copy.43
  237.4 0.7 copy.44
  (18 shorter events, 0.1 us)
Async XLA Ops:
  2.3 0.9 copy-start.4
  3.2 0.9 copy-start.5
  4.1 0.8 copy-start.6
  4.9 0.7 copy-start.8
  55.3 0.6 copy-start.9
  172.2 1.3 copy-start
  173.5 1.3 copy-start.1
  174.7 1.2 copy-start.2
  175.9 1.0 copy-start.3
  176.9 0.8 copy-start.7

commit v2 on v1

--- a/solution.py
+++ b/solution.py
@@ -61,292 +61,6 @@
 
 def rows_of(values):
     return jnp.concatenate(values, 0)
-
-
-MESH_ID = pl.DeviceIdType.MESH
-NZ = 4
-
-
-def place():
-    p = lax.axis_index("fsdp")
-    c = lax.axis_index("dp")
-    x = lax.rem(p, 2)
-    y = lax.rem(lax.div(p, 2), 2)
-    z = lax.div(p, 4)
-    return x, y, z, c
-
-
-def index_of(x, y, z):
-    return (z * 2 + y) * 2 + x
-
-
-def greet(x, y, z, c):
-    barrier = pltpu.get_barrier_semaphore()
-    pl.semaphore_signal(barrier, inc=1, device_id=(index_of(1 - x, y, z), c), device_id_type=MESH_ID)
-    pl.semaphore_signal(barrier, inc=1, device_id=(index_of(x, 1 - y, z), c), device_id_type=MESH_ID)
-    pl.semaphore_signal(barrier, inc=1, device_id=(index_of(x, y, z), 1 - c), device_id_type=MESH_ID)
-    for step in range(1, NZ):
-        other = lax.rem(z + step, NZ)
-        pl.semaphore_signal(barrier, inc=1, device_id=(index_of(x, y, other), c), device_id_type=MESH_ID)
-    pl.semaphore_wait(barrier, 3 + NZ - 1)
-
-
-def remote(src, dst, sems, k, device):
-    return pltpu.make_async_remote_copy(
-        src_ref=src, dst_ref=dst, send_sem=sems.at[0, k], recv_sem=sems.at[1, k],
-        device_id=device, device_id_type=MESH_ID,
-    )
-
-
-def gather_body(qkv, outw, fc1, fc2, vec, slots1, slots2, slots_v, sems1, sems2, semsv, sib):
-    x, y, z, c = place()
-    d = outw.shape[1]
-
-    f = fc1[...].astype(F32)
-    q = qkv[...].astype(F32)
-
-    @pl.when(c == 0)
-    def _():
-        slots1[0, y, x, z] = jnp.concatenate([q[:, :d], q[:, d : 2 * d]], 0).astype(BF16)
-        slots2[0, y, x, z] = jnp.concatenate([f[:, k * d : (k + 1) * d] for k in range(4)], 0).astype(BF16)
-
-    @pl.when(c == 1)
-    def _():
-        slots1[1, y, x, z] = jnp.concatenate([q[:, 2 * d :], outw[...].astype(F32)], 0).astype(BF16)
-        slots2[1, y, x, z] = fc2[...]
-
-    slots_v[y, x, z] = vec[...]
-    greet(x, y, z, c)
-
-    def line(buf, sems):
-        copies = []
-        for step in range(1, NZ):
-            other = lax.rem(z + step, NZ)
-            copy = remote(buf.at[y, x, z], buf.at[y, x, z], sems, step - 1, (index_of(x, y, other), c))
-            copy.start()
-            copies.append(copy)
-        return copies
-
-    def across(buf, sems, first):
-        copies = []
-        if first == "x":
-            copies.append(remote(buf.at[y, x], buf.at[y, x], sems, 3, (index_of(1 - x, y, z), c)))
-            copies[-1].start()
-            copies[-1].wait()
-            copies.append(remote(buf.at[y], buf.at[y], sems, 4, (index_of(x, 1 - y, z), c)))
-            copies[-1].start()
-            copies[-1].wait()
-        else:
-            copies.append(remote(buf.at[y, x], buf.at[y, x], sems, 3, (index_of(x, 1 - y, z), c)))
-            copies[-1].start()
-            copies[-1].wait()
-            pair = [
-                remote(buf.at[k, x], buf.at[k, x], sems, 4 + k, (index_of(1 - x, y, z), c)) for k in range(2)
-            ]
-            for copy in pair:
-                copy.start()
-            for copy in pair:
-                copy.wait()
-
-    def path(group, first):
-        one, two = slots1.at[group], slots2.at[group]
-        flights = line(slots_v, semsv) + line(one, sems1) + line(two, sems2)
-        for copy in flights[:3]:
-            copy.wait()
-        for copy in flights[3:6]:
-            copy.wait()
-        across(slots_v, semsv, first)
-        across(one, sems1, first)
-        swap = remote(one, one, sib, 0, (index_of(x, y, z), 1 - c))
-        swap.start()
-        for copy in flights[6:]:
-            copy.wait()
-        across(two, sems2, first)
-        swap2 = remote(two, two, sib, 1, (index_of(x, y, z), 1 - c))
-        swap2.start()
-        swap.wait()
-        swap2.wait()
-
-    @pl.when(c == 0)
-    def _():
-        path(0, "x")
-
-    @pl.when(c == 1)
-    def _():
-        path(1, "y")
-
-
-def reduce_body(
-    gqkv, gout, g1, g2, gvec,
-    oqkv, oout, o1, o2, ovec,
-    t1, t2, u1, u2, a1, a2, b1, b2, z1, z2, f1, f2, va, vz, sems1, sems2, semsv,
-):
-    x, y, z, c = place()
-    d = gout.shape[1]
-    rows = gout.shape[0] // 16
-
-    def stage(buf, group, blocks):
-        for p in range(16):
-            part = [b[rows * p : rows * (p + 1)] for b in blocks]
-            buf[group, (p // 2) % 2, p % 2, p // 4] = jnp.concatenate(part, 0).astype(BF16)
-
-    q = gqkv[...].astype(F32)
-    stage(t1, 0, [q[:, :d], q[:, d : 2 * d]])
-    stage(t1, 1, [q[:, 2 * d :], gout[...].astype(F32)])
-    f = g1[...].astype(F32)
-    stage(t2, 0, [f[:, k * d : (k + 1) * d] for k in range(4)])
-    for p in range(16):
-        t2[1, (p // 2) % 2, p % 2, p // 4] = g2[4 * rows * p : 4 * rows * (p + 1), :]
-    va[0] = gvec[...]
-    greet(x, y, z, c)
-
-    sibling = (index_of(x, y, z), 1 - c)
-    xn = (index_of(1 - x, y, z), c)
-    yn = (index_of(x, 1 - y, z), c)
-
-    def add(dst, src):
-        dst[...] = (dst[...].astype(F32) + src[...].astype(F32)).astype(BF16)
-
-    def send_all(copies):
-        for copy in copies:
-            copy.start()
-        return copies
-
-    def wait_all(copies):
-        for copy in copies:
-            copy.wait()
-
-    def z_copies(src, dst, sems, base):
-        copies = []
-        for step in range(1, NZ):
-            other = lax.rem(z + step, NZ)
-            copies.append(remote(src(other), dst.at[step - 1], sems, base + step - 1, (index_of(x, y, other), c)))
-        return copies
-
-    def path(group, order):
-        units = ((t1.at[group], u1, a1, b1, z1, f1, sems1), (t2.at[group], u2, a2, b2, z2, f2, sems2))
-        swaps = [
-            send_all([remote(full.at[1 - group], got, sems, 0, sibling)])
-            for full, got, sems in ((t1, u1, sems1), (t2, u2, sems2))
-        ]
-        for (buf, got, *_), copies in zip(units, swaps):
-            wait_all(copies)
-            add(buf, got)
-        flights = []
-        for buf, got, ra, rb, rz, fin, sems in units:
-            if order == "yx":
-                flights.append(send_all([remote(buf.at[1 - y], ra, sems, 1, yn)]))
-            else:
-                flights.append(
-                    send_all([remote(buf.at[k, 1 - x], ra.at[k], sems, 1 + k, xn) for k in range(2)])
-                )
-        for (buf, got, ra, rb, rz, fin, sems), copies in zip(units, flights):
-            wait_all(copies)
-            if order == "yx":
-                add(buf.at[y], ra)
-            else:
-                for k in range(2):
-                    add(buf.at[k, x], ra.at[k])
-        flights = []
-        for buf, got, ra, rb, rz, fin, sems in units:
-            if order == "yx":
-                flights.append(send_all([remote(buf.at[y, 1 - x], rb, sems, 3, xn)]))
-            else:
-                flights.append(send_all([remote(buf.at[1 - y, x], rb, sems, 3, yn)]))
-        for (buf, got, ra, rb, rz, fin, sems), copies in zip(units, flights):
-            wait_all(copies)
-            add(buf.at[y, x], rb)
-        flights = []
-        for buf, got, ra, rb, rz, fin, sems in units:
-            flights.append(send_all(z_copies(lambda k, buf=buf: buf.at[y, x, k], rz, sems, 4)))
-        flights2 = []
-        for (buf, got, ra, rb, rz, fin, sems), copies in zip(units, flights):
-            wait_all(copies)
-            total = buf[y, x, z].astype(F32)
-            for k in range(NZ - 1):
-                total = total + rz[k].astype(F32)
-            fin[group] = total
-            flights2.append(send_all([remote(fin.at[group], fin.at[group], sems, 7, sibling)]))
-        for copies in flights2:
-            wait_all(copies)
-
-    for k, device in enumerate((sibling, xn, yn)):
-        copy = remote(va.at[2 * k], va.at[2 * k + 1], semsv, k, device)
-        copy.start()
-        copy.wait()
-        va[2 * k + 2] = va[2 * k] + va[2 * k + 1]
-    vz[z] = va[6]
-    copies = [
-        remote(vz.at[z], vz.at[z], semsv, 2 + step, (index_of(x, y, lax.rem(z + step, NZ)), c))
-        for step in range(1, NZ)
-    ]
-    send_all(copies)
-    wait_all(copies)
-    ovec[...] = vz[0] + vz[1] + vz[2] + vz[3]
-
-    @pl.when(c == 0)
-    def _():
-        path(0, "yx")
-
-    @pl.when(c == 1)
-    def _():
-        path(1, "xy")
-
-    oqkv[:, :d] = f1[0, :rows]
-    oqkv[:, d : 2 * d] = f1[0, rows:]
-    oqkv[:, 2 * d :] = f1[1, :rows]
-    oout[...] = f1[1, rows:]
-    for k in range(4):
-        o1[:, k * d : (k + 1) * d] = f2[0, rows * k : rows * (k + 1)]
-    o2[...] = f2[1]
-
-
-def gather_call(qkv, outw, fc1, fc2, vec):
-    rows, d = outw.shape
-    dma = pltpu.SemaphoreType.DMA
-    spec = pl.BlockSpec(memory_space=pltpu.VMEM)
-    return pl.pallas_call(
-        gather_body,
-        out_shape=(
-            jax.ShapeDtypeStruct((2, 2, 2, NZ, 2 * rows, d), BF16),
-            jax.ShapeDtypeStruct((2, 2, 2, NZ, 4 * rows, d), BF16),
-            jax.ShapeDtypeStruct((2, 2, NZ) + vec.shape, vec.dtype),
-        ),
-        in_specs=[spec] * 5,
-        out_specs=(spec,) * 3,
-        scratch_shapes=[dma((2, 6)), dma((2, 6)), dma((2, 6)), dma((2, 2))],
-        compiler_params=pltpu.CompilerParams(collective_id=0, has_side_effects=True, vmem_limit_bytes=48 * 1024 * 1024),
-        name="gather",
-    )(qkv, outw, fc1, fc2, vec)
-
-
-def reduce_call(gqkv, gout, g1, g2, gvec):
-    d = gout.shape[1]
-    rows = d // 16
-    dma = pltpu.SemaphoreType.DMA
-    vm = pltpu.VMEM
-    spec = pl.BlockSpec(memory_space=pltpu.VMEM)
-
-    def pair(lead, dtype=BF16):
-        return [vm(lead + (2 * rows, d), dtype), vm(lead + (4 * rows, d), dtype)]
-
-    return pl.pallas_call(
-        reduce_body,
-        out_shape=(
-            jax.ShapeDtypeStruct((rows, 3 * d), F32),
-            jax.ShapeDtypeStruct((rows, d), F32),
-            jax.ShapeDtypeStruct((rows, 4 * d), F32),
-            jax.ShapeDtypeStruct((4 * rows, d), F32),
-            jax.ShapeDtypeStruct(gvec.shape, F32),
-        ),
-        in_specs=[spec] * 5,
-        out_specs=(spec,) * 5,
-        scratch_shapes=pair((2, 2, 2, NZ)) + pair((2, 2, NZ)) + pair((2, NZ)) + pair((NZ,)) + pair((NZ - 1,))
-        + pair((2,), F32) + [vm((7,) + gvec.shape, F32), vm((NZ,) + gvec.shape, F32)]
-        + [dma((2, 8)), dma((2, 8)), dma((2, 8))],
-        compiler_params=pltpu.CompilerParams(collective_id=1, has_side_effects=True, vmem_limit_bytes=48 * 1024 * 1024),
-        name="reduce",
-    )(gqkv, gout, g1, g2, gvec)
 
 
 LN1G, LN1B, BQKV, BOUT, LN2G, LN2B, BFC1, BFC2 = range(8)
@@ -674,16 +388,758 @@
         name="block",
     )(tok, dup, tgt, vec, wqkv, wout, w1, w2)
 
+MESH_ID = pl.DeviceIdType.MESH
+NZ = 4
+
+
+class Place:
+    def __init__(self):
+        p = lax.axis_index("fsdp")
+        self.p = p
+        self.c = lax.axis_index("dp")
+        self.x = lax.rem(p, 2)
+        self.y = lax.rem(lax.div(p, 2), 2)
+        self.z = lax.div(p, 4)
+        self.a = self.y + self.c * (self.x - self.y)
+        self.b = self.x + self.c * (self.y - self.x)
+
+    def device(self, x, y, z):
+        return ((z * 2 + y) * 2 + x, self.c)
+
+    def along_a(self):
+        c = self.c
+        return self.device(self.x + c * (1 - 2 * self.x), self.y + (1 - c) * (1 - 2 * self.y), self.z)
+
+    def along_b(self):
+        c = self.c
+        return self.device(self.x + (1 - c) * (1 - 2 * self.x), self.y + c * (1 - 2 * self.y), self.z)
+
+    def along_z(self, step):
+        return lax.rem(self.z + step, NZ)
+
+    def sibling(self):
+        return (self.p, 1 - self.c)
+
+
+def slot_of(p, group):
+    x, y, z = p % 2, (p // 2) % 2, p // 4
+    a, b = (y, x) if group == 0 else (x, y)
+    return (a * 2 + b) * NZ + z
+
+
+def greet(at):
+    barrier = pltpu.get_barrier_semaphore()
+    others = [at.along_a(), at.along_b(), at.sibling()]
+    others += [at.device(at.x, at.y, at.along_z(step)) for step in range(1, NZ)]
+    for device in others:
+        pl.semaphore_signal(barrier, inc=1, device_id=device, device_id_type=MESH_ID)
+    pl.semaphore_wait(barrier, len(others))
+
+
+def remote(src, dst, sems, k, device):
+    return pltpu.make_async_remote_copy(
+        src_ref=src, dst_ref=dst, send_sem=sems.at[0, k], recv_sem=sems.at[1, k],
+        device_id=device, device_id_type=MESH_ID,
+    )
+
+
+def span(start, size):
+    return pl.ds(pl.multiple_of(start, size), size)
+
+
+class Gather:
+    def __init__(self, at, buf, r, sems, swap):
+        self.at, self.buf, self.r, self.sems, self.shared = at, buf, r, sems, swap
+
+    def part(self, rows, k, device):
+        piece = self.buf.at[rows]
+        return remote(piece, piece, self.sems, k, device)
+
+    def line(self):
+        at, r = self.at, self.r
+        rows = span(((at.a * 2 + at.b) * NZ + at.z) * r, r)
+        return [
+            self.part(rows, step - 1, at.device(at.x, at.y, at.along_z(step))) for step in range(1, NZ)
+        ]
+
+    def over_b(self):
+        at, r = self.at, self.r
+        return [self.part(span((at.a * 2 + at.b) * NZ * r, NZ * r), 3, at.along_b())]
+
+    def over_a(self):
+        at, r = self.at, self.r
+        return [self.part(span(at.a * 2 * NZ * r, 2 * NZ * r), 4, at.along_a())]
+
+    def swap(self):
+        return [remote(self.buf, self.buf, self.sems, 5, self.at.sibling())] if self.shared else []
+
+    def go(self, step):
+        steps = (self.line, self.over_b, self.over_a, self.swap)
+        if step > 0:
+            for copy in steps[step - 1]():
+                copy.wait()
+        if step < 4:
+            for copy in steps[step]():
+                copy.start()
+
+
+class Reduce:
+    def __init__(self, at, full, got, from_a, from_b, from_z, total, r, sems):
+        self.at, self.full, self.got = at, full, got
+        self.from_a, self.from_b, self.from_z, self.total = from_a, from_b, from_z, total
+        self.r, self.sems = r, sems
+
+    def first(self):
+        return [remote(self.full.at[1 - self.at.c], self.got, self.sems, 0, self.at.sibling())]
+
+    def over_a(self):
+        at, r = self.at, self.r
+        rows = span((1 - at.a) * 2 * NZ * r, 2 * NZ * r)
+        return [remote(self.full.at[at.c, rows], self.from_a, self.sems, 1, at.along_a())]
+
+    def over_b(self):
+        at, r = self.at, self.r
+        rows = span((at.a * 2 + 1 - at.b) * NZ * r, NZ * r)
+        return [remote(self.full.at[at.c, rows], self.from_b, self.sems, 2, at.along_b())]
+
+    def line(self):
+        at, r = self.at, self.r
+        copies = []
+        for step in range(1, NZ):
+            other = at.along_z(step)
+            rows = span(((at.a * 2 + at.b) * NZ + other) * r, r)
+            copies.append(
+                remote(self.full.at[at.c, rows], self.from_z.at[pl.ds((step - 1) * r, r)], self.sems, 2 + step, at.device(at.x, at.y, other))
+            )
+        return copies
+
+    def last(self):
+        piece = self.total.at[self.at.c]
+        return [remote(piece, piece, self.sems, 6, self.at.sibling())]
+
+    def add(self, rows, values):
+        ref = self.full.at[self.at.c, rows]
+        ref[...] = (ref[...].astype(F32) + values.astype(F32)).astype(ref.dtype)
+
+    def go(self, step):
+        at, r = self.at, self.r
+        steps = (self.first, self.over_a, self.over_b, self.line, self.last)
+        if step > 0:
+            for copy in steps[step - 1]():
+                copy.wait()
+        if step == 1:
+            for half in range(2):
+                rows = pl.ds(half * 2 * NZ * r, 2 * NZ * r)
+                self.add(rows, self.got[rows, :])
+        elif step == 2:
+            self.add(span(at.a * 2 * NZ * r, 2 * NZ * r), self.from_a[...])
+        elif step == 3:
+            self.add(span((at.a * 2 + at.b) * NZ * r, NZ * r), self.from_b[...])
+        elif step == 4:
+            total = self.full[at.c, span(((at.a * 2 + at.b) * NZ + at.z) * r, r), :].astype(F32)
+            for k in range(NZ - 1):
+                total = total + self.from_z[k * r : (k + 1) * r, :].astype(F32)
+            self.total[at.c] = total
+        if step < 5:
+            for copy in steps[step]():
+                copy.start()
+
+
+V_LN1G, V_LN1B, V_QV, V_BOUT, V_LN2G, V_LN2B, V_BFC2, V_BFC1 = 0, 1, 2, 4, 5, 6, 7, 8
+
+
+def block_body(
+    tok, dup, tgt, s_ln1g, s_ln1b, s_qkv, s_qvb, s_out, s_bout, s_ln2g, s_ln2b, s_fc1, s_b1, s_fc2, s_b2,
+    out, gin, oqkv, oout, o1, o2, ovec,
+    tokb, stage, xs, n1, qkv, att, n2, act, dpre, db2, db1, dos, dmid, probs,
+    wqkv, wout, w1, w2_t, wt_a, wf,
+    c_ln1g, c_ln1b, c_bqkv, c_bout, c_ln2g, c_ln2b, c_b1, c_b2,
+    stat_s, rl_s, ex_s, exq_s, rlx_s, exx_s, attx, dqkvx, a_g2, a_b2, tgt_t, gvec, allc,
+    sv, tv, uv, av, bv, zv, f1, f2, fv,
+    loc_sem, gsem1, gsem2, gsemv, rsem1, rsem2, rsemv, ready,
+):
+    images, seq = dup.shape
+    d = tok.shape[1]
+    t = seq - 1
+    x0 = images * t
+    ff = w1.shape[1]
+    w = x0 + 128
+    shard = d // 16
+    blocks = d // 128
+    at = Place()
+
+    def lanes_of(i):
+        return pl.ds(pl.multiple_of(i * t, 128), t)
+
+    extra_lanes = pl.ds(x0, 128)
+
+    def load_image(i):
+        return jnp.concatenate([stage[b, pl.ds(i, t, stride=images), :] for b in range(blocks)], 1)
+
+    def store_image(i, values):
+        for b in range(blocks):
+            stage[b, pl.ds(i, t, stride=images), :] = values[:, 128 * b : 128 * (b + 1)]
+
+    def store_last(values):
+        for b in range(blocks):
+            stage[b, x0:, :] = values[:images, 128 * b : 128 * (b + 1)]
+
+    tok_copy = pltpu.make_async_copy(tok, tokb, loc_sem.at[0])
+    tok_copy.start()
+
+    own = span(((at.a * 2 + at.b) * NZ + at.z) * 16, 16)
+    table = jnp.zeros((16, 128), F32)
+    sv[own, :] = table
+    base = ((at.a * 2 + at.b) * NZ + at.z) * 16
+    flat = [s_ln1g[...], s_ln1b[...], s_qvb[:shard], s_qvb[shard:], s_bout[...], s_ln2g[...], s_ln2b[...], s_b2[...]]
+    flat += [s_b1[shard * k : shard * (k + 1)] for k in range(4)]
+    for k, line in enumerate(flat):
+        sv[pl.ds(base + k, 1), :shard] = line.astype(F32).reshape(1, shard)
+    halves = (pl.ds(0, d), pl.ds(d, d))
+    mine = pl.ds(pl.multiple_of(at.c * d, 128), d)
+    own1 = span(((at.a * 2 + at.b) * NZ + at.z) * 2 * shard, 2 * shard)
+    own2 = span(((at.a * 2 + at.b) * NZ + at.z) * 4 * shard, 4 * shard)
+    slots1 = act.at[: 16 * 2 * shard]
+    slots2 = dpre
+
+    @pl.when(at.c == 0)
+    def _():
+        q = s_qkv[...].astype(F32)
+        f = s_fc1[...].astype(F32)
+        slots1[own1, halves[0]] = jnp.concatenate([q[:, :d], q[:, d : 2 * d]], 0).astype(BF16)
+        slots2[own2, halves[0]] = jnp.concatenate([f[:, k * d : (k + 1) * d] for k in range(4)], 0).astype(BF16)
+
+    @pl.when(at.c == 1)
+    def _():
+        q = s_qkv[...].astype(F32)
+        slots1[own1, halves[1]] = jnp.concatenate([q[:, 2 * d :], s_out[...].astype(F32)], 0).astype(BF16)
+        slots2[own2, halves[1]] = s_fc2[...]
+
+    greet(at)
+    gather_v = Gather(at, sv, 16, gsemv, False)
+    gather1 = Gather(at, slots1.at[:, mine], 2 * shard, gsem1, True)
+    gather2 = Gather(at, slots2.at[:, mine], 4 * shard, gsem2, True)
+    gather_v.go(0)
+    gather1.go(0)
+
+    tok_copy.wait()
+    for b in range(blocks):
+        stage[b] = tokb[:, 128 * b : 128 * (b + 1)].astype(F32)
+
+    def statistics(x):
+        mu = jnp.mean(x, 0, keepdims=True)
+        c = x - mu
+        return mu, lax.rsqrt(jnp.mean(c * c, 0, keepdims=True) + EPS)
+
+    def turn(i, carry):
+        x = load_image(i).astype(BF16).T
+        xs[:, lanes_of(i)] = x
+        mu, r = statistics(x.astype(F32))
+        stat_s[i, 0:1, :] = mu
+        stat_s[i, 1:2, :] = r
+        return carry
+
+    gather_v.go(1)
+    gather1.go(1)
+    gather2.go(0)
+    lax.fori_loop(0, images // 2, turn, 0)
+    gather_v.go(2)
+    gather1.go(2)
+    lax.fori_loop(images // 2, images, turn, 0)
+    last = jnp.concatenate([tokb[x0:, :].astype(F32), jnp.zeros((128 - images, d), F32)], 0)
+    x = last.astype(BF16).T
+    xs[:, extra_lanes] = x
+    mu, r = statistics(x.astype(F32))
+    stat_s[images, 0:1, :128] = mu
+    stat_s[images, 1:2, :128] = r
+    tgt_t[...] = jnp.concatenate([tgt[...], jnp.zeros((128 - images, d), F32)], 0).T
+    ones_row = jnp.where(lax.broadcasted_iota(jnp.int32, (16, w), 0) == 0, 1.0, 0.0).astype(BF16)
+    n1[d : d + 16, :] = ones_row
+    n2[d : d + 16, :] = ones_row
+    att[d : d + 16, :] = ones_row
+    attx[...] = jnp.zeros_like(attx)
+    dqkvx[...] = jnp.zeros_like(dqkvx)
+    a_g2[...] = jnp.zeros_like(a_g2)
+    a_b2[...] = jnp.zeros_like(a_b2)
+    gather_v.go(3)
+    gather1.go(3)
+
+    def slot_v(p):
+        px, py, pz = p % 2, (p // 2) % 2, p // 4
+        pa = py + at.c * (px - py)
+        pb = px + at.c * (py - px)
+        return sv[span(((pa * 2 + pb) * NZ + pz) * 16, 16), :]
+
+    for half in range(2):
+        allc[half] = jnp.concatenate([slot_v(p) for p in range(8 * half, 8 * half + 8)], 0).T
+
+    def column(ref, entries):
+        runs = []
+        ids = lax.broadcasted_iota(jnp.int32, (shard, 128), 1)
+        for p, k in entries:
+            runs.append(jnp.where(ids == 16 * (p % 8) + k, allc[p // 8, :shard, :], 0.0))
+        block = jnp.sum(jnp.concatenate(runs, 0), 1, keepdims=True)
+        ref[...] = jnp.broadcast_to(block, (len(entries) * shard, 128))
+
+    every = range(16)
+    column(c_ln1g, [(p, V_LN1G) for p in every])
+    column(c_ln1b, [(p, V_LN1B) for p in every])
+    column(c_bqkv.at[:d], [(p, V_QV + k) for p in range(8) for k in range(2)])
+    c_bqkv[d : 2 * d, :] = jnp.zeros((d, 128), F32)
+    column(c_bqkv.at[2 * d :], [(p, V_QV + k) for p in range(8, 16) for k in range(2)])
+    column(c_bout, [(p, V_BOUT) for p in every])
+    column(c_ln2g, [(p, V_LN2G) for p in every])
+    column(c_ln2b, [(p, V_LN2B) for p in every])
+    column(c_b2, [(p, V_BFC2) for p in every])
+    column(c_b1, [(p, V_BFC1 + k) for p in every for k in range(4)])
+
+    gather1.go(4)
+    gather2.go(1)
+
+    def unpack(slots, group, r, k):
+        part = slots[:, halves[group]]
+        runs = []
+        for p in every:
+            s = slot_of(p, group)
+            runs.append(slots[r * s : r * (s + 1), halves[group]].astype(F32)[k * shard : (k + 1) * shard])
+        return jnp.concatenate(runs, 0).astype(BF16)
+
+    for k in range(4):
+        block = unpack(slots1, k // 2, 2 * shard, k % 2)
+        if k < 3:
+            wqkv[:, k * d : (k + 1) * d] = block
+        else:
+            wout[...] = block
+        wt_a[k // 2, (k % 2) * d : (k % 2 + 1) * d, :] = block.T
+
+    def project(lanes, count, mu, r):
+        u = (xs[:, lanes].astype(F32) - mu) * r
+        n = (u * wide(c_ln1g[...], count) + wide(c_ln1b[...], count)).astype(BF16)
+        n1[:d, lanes] = n
+        for k in range(3):
+            rows = slice(k * d, (k + 1) * d)
+            y = mm(wt_a[k // 2, (k % 2) * d : (k % 2 + 1) * d, :], n) + wide(c_bqkv[rows, :], count)
+            y = y.astype(BF16)
+            if k == 0:
+                y = y * jnp.asarray(HD**-0.5, BF16)
+            qkv[rows, lanes] = y
+
+    def project_image(i, carry):
+        project(lanes_of(i), t, stat_s[i, 0:1, :], stat_s[i, 1:2, :])
+        return carry
+
+    lax.fori_loop(0, images, project_image, 0)
+    project(extra_lanes, 128, stat_s[images, 0:1, :128], stat_s[images, 1:2, :128])
+    gather2.go(2)
+
+    lane_ids = lax.broadcasted_iota(jnp.int32, (HD, 128), 1)
+
+    def pick(ref, row, i):
+        block = ref[row : row + HD, extra_lanes].astype(F32)
+        return jnp.sum(jnp.where(lane_ids == i, block, 0.0), 1, keepdims=True)
+
+    def attend_image(i, carry):
+        lanes = lanes_of(i)
+        for h in range(HEADS):
+            r0 = h * HD
+            q = qkv[r0 : r0 + HD, lanes]
+            k = qkv[d + r0 : d + r0 + HD, lanes]
+            v = qkv[2 * d + r0 : 2 * d + r0 + HD, lanes]
+            qx, kx, vx = pick(qkv, r0, i), pick(qkv, d + r0, i), pick(qkv, 2 * d + r0, i)
+            s = mm(k.T, q)
+            sx = jnp.sum(q.astype(F32) * kx, 0, keepdims=True)
+            top = jnp.maximum(jnp.max(s, 0, keepdims=True), sx)
+            e = jnp.exp(s - top)
+            ex = jnp.exp(sx - top)
+            rl = 1.0 / (jnp.sum(e, 0, keepdims=True) + ex)
+            e = e.astype(BF16)
+            probs[i * HEADS + h] = e
+            o = (mm(v, e) + vx * ex) * rl
+            att[r0 : r0 + HD, lanes] = o.astype(BF16)
+            rl_s[i, h : h + 1, :] = rl
+            ex_s[i, h : h + 1, :] = ex
+            sq = jnp.sum(k.astype(F32) * qx, 0, keepdims=True)
+            sxx = jnp.sum(kx * qx, 0, keepdims=True)
+            topx = jnp.maximum(jnp.max(sq, 1, keepdims=True), sxx)
+            eq = jnp.exp(sq - topx)
+            exx = jnp.exp(sxx - topx)
+            rlx = 1.0 / (jnp.sum(eq, 1, keepdims=True) + exx)
+            ox = (jnp.sum(v.astype(F32) * eq, 1, keepdims=True) + vx * exx) * rlx
+            attx[r0 : r0 + HD, :] = jnp.where(lane_ids == i, ox, attx[r0 : r0 + HD, :])
+            exq_s[i, h : h + 1, :] = eq
+            rlx_s[i, h : h + 1, :] = jnp.broadcast_to(rlx, (1, 128))
+            exx_s[i, h : h + 1, :] = jnp.broadcast_to(exx, (1, 128))
+
+        @pl.when(i == images // 2)
+        def _():
+            gather2.go(3)
+
+        return carry
+
+    lax.fori_loop(0, images, attend_image, 0)
+    att[:d, extra_lanes] = attx[...].astype(BF16)
+    gather2.go(4)
+    for k in range(4):
+        block = unpack(slots2, 0, 4 * shard, k)
+        w1[:, k * d : (k + 1) * d] = block
+        wf[0, k * d : (k + 1) * d, :] = block.T
+    for p in every:
+        s = slot_of(p, 1)
+        wf[1, 4 * shard * p : 4 * shard * (p + 1), :] = slots2[4 * shard * s : 4 * shard * (s + 1), halves[1]]
+    w2_t[...] = wf[1].T
+    act[ff : ff + 16, :] = ones_row
+
+    def feed(lanes, count, d_final):
+        mid = xs[:, lanes].astype(F32) + mm(wt_a[1, d:, :], att[:d, lanes]) + wide(c_bout[...], count)
+        u, r = normalise(mid)
+        n = (u * wide(c_ln2g[...], count) + wide(c_ln2b[...], count)).astype(BF16)
+        n2[:d, lanes] = n
+        db = d_final.astype(BF16)
+        db2[:, lanes] = db
+        for j in range(ff // 256):
+            rows = slice(256 * j, 256 * (j + 1))
+            pre = mm(wf[0, rows, :], n) + wide(c_b1[rows, :], count)
+            da = mm(wf[1, rows, :], db)
+            value, slope = gelu_pair(pre)
+            act[rows, lanes] = value.astype(BF16)
+            dpre[rows, lanes] = (slope * da).astype(BF16)
+        final = mid + mm(w2_t[...], act[:ff, lanes]) + wide(c_b2[...], count)
+        dn = mm(w1[...], dpre[:, lanes])
+        a_g2[...] += fold(dn * u)
+        a_b2[...] += fold(dn)
+        dm = d_final + norm_back(dn, u, r, wide(c_ln2g[...], count))
+        dmid[:, lanes] = dm
+        low = dm.astype(BF16)
+        db1[:, lanes] = low
+        dos[:, lanes] = mm(wout[...], low).astype(BF16)
+        return final.T
+
+    def keep_row(row):
+        first = lax.broadcasted_iota(jnp.int32, row.shape, 1) == 0
+        return jnp.where(first, 1.0, 1.0 - row.astype(F32))
+
+    def feed_image(i, carry):
+        keep = keep_row(dup[pl.ds(i, 1), :])
+        count = jnp.sum(keep, 1, keepdims=True)
+        scale = seq * keep[:, :t] / count
+        ids = lax.broadcasted_iota(jnp.int32, (d, 128), 1)
+        target = jnp.sum(jnp.where(ids == i, tgt_t[...], 0.0), 1, keepdims=True)
+        store_image(i, feed(lanes_of(i), t, target * scale))
+        return carry
+
+    lax.fori_loop(0, images, feed_image, 0)
+    keep_all = keep_row(dup[...])
+    scale_x = seq * keep_all[:, t:] / jnp.sum(keep_all, 1, keepdims=True)
+    scale_x = jnp.broadcast_to(scale_x, (images, 128))
+    scale_x = jnp.concatenate([scale_x, jnp.zeros((128 - images, 128), F32)], 0).T[:1, :]
+    store_last(feed(extra_lanes, 128, tgt_t[...] * scale_x))
+    for b in range(blocks):
+        tokb[:, 128 * b : 128 * (b + 1)] = stage[b].astype(BF16)
+    out_copy = pltpu.make_async_copy(tokb, out, loc_sem.at[0])
+    out_copy.start()
+
+    for j in range(2):
+        rows = slice(2 * d * j, 2 * d * (j + 1))
+        g = mm(n2[...], dpre[rows, :], NT)
+        gvec[BFC1 : BFC1 + 1, rows] = g[d : d + 1]
+        for k in range(2):
+            part = g[:d, d * k : d * (k + 1)].astype(BF16)
+            for p in every:
+                start = 4 * shard * slot_of(p, 0) + shard * (2 * j + k)
+                wf[0, start : start + shard, :] = part[shard * p : shard * (p + 1)]
+    for j in range(ff // 256):
+        rows = slice(256 * j, 256 * (j + 1))
+        g = mm(act[rows, :], db2[...], NT).astype(BF16)
+        step = 4 * shard
+        lo = 256 * j
+        while lo < 256 * (j + 1):
+            p = lo // step
+            hi = min(256 * (j + 1), (p + 1) * step)
+            start = step * slot_of(p, 1) + lo - p * step
+            wf[1, start : start + hi - lo, :] = g[lo - 256 * j : hi - 256 * j]
+            lo = hi
+    g = mm(act[ff : ff + 16, :], db2[...], NT)
+    gvec[BFC2 : BFC2 + 1, :d] = g[:1]
+
+    partners = [at.sibling(), at.along_a(), at.along_b()]
+    partners += [at.device(at.x, at.y, at.along_z(step)) for step in range(1, NZ)]
+    for k, device in enumerate(partners):
+        pl.semaphore_signal(ready.at[min(k, 3)], inc=1, device_id=device, device_id_type=MESH_ID)
+
+    def area(row, count, column):
+        return dpre.at[row : row + count, d * column : d * (column + 1)]
+
+    r2, r1 = 4 * shard, 2 * shard
+    reduce2 = Reduce(
+        at, wf, area(0, 16 * r2, 0), area(0, 8 * r2, 1), area(8 * r2, 4 * r2, 1), area(12 * r2, 3 * r2, 1), f2, r2, rsem2
+    )
+    reduce1 = Reduce(
+        at, wt_a, area(0, 16 * r1, 2), area(16 * r1, 8 * r1, 2), area(24 * r1, 4 * r1, 2), area(28 * r1, 3 * r1, 2), f1, r1, rsem1
+    )
+    pl.semaphore_wait(ready.at[0], 1)
+    reduce2.go(0)
+
+    def attend_back(i, carry):
+        lanes = lanes_of(i)
+        for h in range(HEADS):
+            r0 = h * HD
+            q = qkv[r0 : r0 + HD, lanes]
+            k = qkv[d + r0 : d + r0 + HD, lanes]
+            v = qkv[2 * d + r0 : 2 * d + r0 + HD, lanes]
+            qx, kx, vx = pick(qkv, r0, i), pick(qkv, d + r0, i), pick(qkv, 2 * d + r0, i)
+            rl = rl_s[i, h : h + 1, :]
+            ex = ex_s[i, h : h + 1, :]
+            do = dos[r0 : r0 + HD, lanes].astype(F32) * rl
+            dot_o = jnp.sum(do * att[r0 : r0 + HD, lanes].astype(F32), 0, keepdims=True)
+            dol = do.astype(BF16)
+            p = probs[i * HEADS + h]
+            ds = (p.astype(F32) * (mm(v.T, dol) - dot_o)).astype(BF16)
+            dsx = ex * (jnp.sum(do * vx, 0, keepdims=True) - dot_o)
+            dq = mm(k, ds) + kx * dsx
+            dk = mm(q, ds, NT)
+            dv = mm(dol, p, NT)
+            qf = q.astype(F32)
+            kf = k.astype(F32)
+            vf = v.astype(F32)
+            dkx = jnp.sum(qf * dsx, 1, keepdims=True)
+            dvx = jnp.sum(do * ex, 1, keepdims=True)
+            eq = exq_s[i, h : h + 1, :]
+            rlx = rlx_s[i, h : h + 1, :1]
+            exx = exx_s[i, h : h + 1, :1]
+            dox = pick(dos, r0, i) * rlx
+            dotx = jnp.sum(dox * pick(att, r0, i), 0, keepdims=True)
+            dsq = eq * (jnp.sum(vf * dox, 0, keepdims=True) - dotx)
+            dsxx = exx * (jnp.sum(vx * dox, 0, keepdims=True) - dotx)
+            dqx = jnp.sum(kf * dsq, 1, keepdims=True) + kx * dsxx
+            dk = dk + qx * dsq
+            dv = dv + dox * eq
+            dkx = dkx + qx * dsxx
+            dvx = dvx + dox * exx
+            scale = HD**-0.5
+            for base, main, tail in ((0, dq * scale, dqx * scale), (d, dk, dkx), (2 * d, dv, dvx)):
+                rows = slice(base + r0, base + r0 + HD)
+                qkv[rows, lanes] = main.astype(BF16)
+                dqkvx[rows, :] = jnp.where(lane_ids == i, tail, dqkvx[rows, :])
+
+        for step, when in ((1, 1), (2, 3), (3, 5), (4, 7)):
+
+            @pl.when(i == when)
+            def _(step=step):
+                if step < 4:
+                    pl.semaphore_wait(ready.at[step], 1 if step < 3 else NZ - 1)
+                reduce2.go(step)
+
+        return carry
+
+    lax.fori_loop(0, images, attend_back, 0)
+    qkv[:, extra_lanes] = dqkvx[...].astype(BF16)
+
+    scale1 = jnp.zeros((d, 128), F32)
+    shift1 = jnp.zeros((d, 128), F32)
+    gain1, bias1 = c_ln1g[:, :1], c_ln1b[:, :1]
+
+    def put(group, k, part):
+        part = part.astype(BF16)
+        for p in every:
+            start = 2 * shard * slot_of(p, group) + shard * k
+            wt_a[group, start : start + shard, :] = part[shard * p : shard * (p + 1)]
+
+    for k in range(3):
+        rows = slice(k * d, (k + 1) * d)
+        g = mm(n1[...], qkv[rows, :], NT)
+        sums = g[d : d + 1]
+        gvec[BQKV : BQKV + 1, rows] = sums
+        weight = wqkv[:, rows].astype(F32)
+        scale1 = scale1 + fold(weight * (g[:d] - bias1 * sums))
+        shift1 = shift1 + fold(weight * sums)
+        put(k // 2, k % 2, g[:d])
+    g = mm(att[...], db1[...], NT)
+    put(1, 1, g[:d])
+    gvec[BOUT : BOUT + 1, :d] = g[d : d + 1]
+    scale1 = scale1 * (1.0 / c_ln1g[...])
+    for row, acc in ((LN1G, scale1), (LN1B, shift1), (LN2G, a_g2[...]), (LN2B, a_b2[...])):
+        gvec[row : row + 1, :d] = jnp.sum(acc.T, 0, keepdims=True)
+    tv[...] = jnp.zeros_like(tv)
+    for p in every:
+        s0 = 8 * slot_of(p, 0)
+        tv[0, s0 : s0 + 8, :shard] = gvec[:, shard * p : shard * (p + 1)]
+        s1 = 8 * slot_of(p, 1)
+        lo = 2 * shard * p if p < 8 else 2 * d + 2 * shard * (p - 8)
+        parts = [gvec[BQKV : BQKV + 1, lo + shard * k : lo + shard * (k + 1)] for k in range(2)]
+        lo = 4 * shard * p
+        parts += [gvec[BFC1 : BFC1 + 1, lo + shard * k : lo + shard * (k + 1)] for k in range(4)]
+        tv[1, s1 : s1 + 6, :shard] = jnp.concatenate(parts, 0)
+
+    reduce_v = Reduce(at, tv, uv, av, bv, zv, fv, 8, rsemv)
+    reduce1.go(0)
+    reduce_v.go(0)
+    reduce2.go(5)
+
+    def finish(lanes, count, mu, r):
+        u = (xs[:, lanes].astype(F32) - mu) * r
+        dn = mm(wqkv[...], qkv[:, lanes])
+        return (dmid[:, lanes] + norm_back(dn, u, r, wide(c_ln1g[...], count))).T
+
+    def finish_image(i, carry):
+        store_image(i, finish(lanes_of(i), t, stat_s[i, 0:1, :], stat_s[i, 1:2, :]))
+        for step, when in ((1, 2), (2, 6)):
+
+            @pl.when(i == when)
+            def _(step=step):
+                reduce_v.go(step)
+                reduce1.go(step)
+
+        return carry
+
+    lax.fori_loop(0, images, finish_image, 0)
+    store_last(finish(extra_lanes, 128, stat_s[images, 0:1, :128], stat_s[images, 1:2, :128]))
+    copies = [
+        pltpu.make_async_copy(stage.at[b], gin.at[:, pl.ds(128 * b, 128)], loc_sem.at[1 + b]) for b in range(blocks)
+    ]
+    for copy in copies:
+        copy.start()
+    o1[...] = jnp.concatenate([f2[0, shard * k : shard * (k + 1)] for k in range(4)], 1)
+    o2[...] = f2[1]
+    for step in (3, 4, 5):
+        reduce_v.go(step)
+        reduce1.go(step)
+    oqkv[:, :d] = f1[0, :shard]
+    oqkv[:, d : 2 * d] = f1[0, shard:]
+    oqkv[:, 2 * d :] = f1[1, :shard]
+    oout[...] = f1[1, shard:]
+    ovec[...] = fv[...]
+    for copy in copies:
+        copy.wait()
+    out_copy.wait()
+
+
+def block_call(tok, dup, tgt, weights):
+    images, seq = dup.shape
+    d = tok.shape[1]
+    n = d // 16
+    ff = 4 * d
+    t = seq - 1
+    w = images * t + 128
+    vm = pltpu.VMEM
+    dma = pltpu.SemaphoreType.DMA
+    sd = jax.ShapeDtypeStruct
+    scratch = [
+        vm((seq * images, d), BF16),
+        vm((d // 128, seq * images, 128), F32),
+        vm((d, w), BF16),
+        vm((d + 16, w), BF16),
+        vm((3 * d, w), BF16),
+        vm((d + 16, w), BF16),
+        vm((d + 16, w), BF16),
+        vm((ff + 16, w), BF16),
+        vm((ff, w), BF16),
+        vm((d, w), BF16),
+        vm((d, w), BF16),
+        vm((d, w), BF16),
+        vm((d, w), F32),
+        vm((images * HEADS, t, t), BF16),
+        vm((d, 3 * d), BF16),
+        vm((d, d), BF16),
+        vm((d, ff), BF16),
+        vm((d, ff), BF16),
+        vm((2, 2 * d, d), BF16),
+        vm((2, ff, d), BF16),
+        vm((d, 128), F32), vm((d, 128), F32), vm((3 * d, 128), F32), vm((d, 128), F32),
+        vm((d, 128), F32), vm((d, 128), F32), vm((ff, 128), F32), vm((d, 128), F32),
+        vm((images + 1, 8, t), F32),
+        vm((images, 8, t), F32),
+        vm((images, 8, t), F32),
+        vm((images, 8, t), F32),
+        vm((images, 8, 128), F32),
+        vm((images, 8, 128), F32),
+        vm((d, 128), F32),
+        vm((3 * d, 128), F32),
+        vm((d, 128), F32), vm((d, 128), F32),
+        vm((d, 128), F32),
+        vm((8, ff), F32),
+        vm((2, 128, 128), F32),
+        vm((256, 128), F32),
+        vm((2, 128, 128), F32),
+    ]
+    for slots in (16, 8, 4):
+        scratch += [vm((slots * 8, 128), F32)]
+    scratch += [vm((24, 128), F32)]
+    scratch += [vm((2, 2 * n, d), F32), vm((2, 4 * n, d), F32), vm((2, 8, 128), F32)]
+    scratch += [dma((4,))] + [dma((2, 7))] * 6 + [pltpu.SemaphoreType.REGULAR((4,))]
+    spec = pl.BlockSpec(memory_space=pltpu.VMEM)
+    any_spec = pl.BlockSpec(memory_space=pl.ANY)
+    return pl.pallas_call(
+        block_body,
+        out_shape=(
+            sd(tok.shape, BF16), sd(tok.shape, F32),
+            sd((n, 3 * d), F32), sd((n, d), F32), sd((n, ff), F32), sd((4 * n, d), F32), sd((2, 8, 128), F32),
+        ),
+        in_specs=[any_spec] + [spec] * 14,
+        out_specs=(any_spec, any_spec) + (spec,) * 5,
+        scratch_shapes=scratch,
+        compiler_params=pltpu.CompilerParams(
+            collective_id=0, has_side_effects=True, vmem_limit_bytes=64 * 1024 * 1024
+        ),
+        name="block16",
+    )(tok, dup, tgt, *weights)
+
+
+def deliver_body(out, gin, gqkv, gout, g1, g2, gv, *refs):
+    o_out, o_gin, o_ln1g, o_ln1b, o_qkv, o_qvb, o_w, o_bout, o_ln2g, o_ln2b, o_fc1, o_b1, o_fc2, o_b2 = refs[:14]
+    buf_out, buf_gin, sems = refs[14:]
+    n = gqkv.shape[0]
+    pieces = []
+    for k, (src, buf, dst) in enumerate(((out, buf_out, o_out), (gin, buf_gin, o_gin))):
+        count = 1 + 3 * k
+        size = (src.shape[0] // count) // 16 * 16
+        for m in range(count):
+            rows = pl.ds(m * size, size if m < count - 1 else src.shape[0] - m * size)
+            s = k + m
+            pieces.append((
+                pltpu.make_async_copy(src.at[rows], buf.at[rows], sems.at[0, s]),
+                pltpu.make_async_copy(buf.at[rows], dst.at[rows], sems.at[1, s]),
+            ))
+    for load, store in pieces:
+        load.start()
+    o_qkv[...] = gqkv[...]
+    o_w[...] = gout[...]
+    o_fc1[...] = g1[...]
+    o_fc2[...] = g2[...]
+    for ref, row in ((o_ln1g, LN1G), (o_ln1b, LN1B), (o_bout, BOUT), (o_ln2g, LN2G), (o_ln2b, LN2B), (o_b2, BFC2)):
+        ref[...] = gv[0, row, :n]
+    o_qvb[...] = jnp.concatenate([gv[1, k, :n] for k in range(2)], 0)
+    o_b1[...] = jnp.concatenate([gv[1, 2 + k, :n] for k in range(4)], 0)
+    for load, store in pieces:
+        load.wait()
+        store.start()
+    for load, store in pieces:
+        store.wait()
+
+
+def deliver_call(out, gin, gqkv, gout, g1, g2, gv):
+    n, d = gout.shape
+    sd = jax.ShapeDtypeStruct
+    spec = pl.BlockSpec(memory_space=pltpu.VMEM)
+    any_spec = pl.BlockSpec(memory_space=pl.ANY)
+    vec = sd((n,), F32)
+    return pl.pallas_call(
+        deliver_body,
+        out_shape=(
+            sd(out.shape, BF16), sd(gin.shape, F32), vec, vec, sd((n, 3 * d), F32), sd((2 * n,), F32),
+            sd((n, d), F32), vec, vec, vec, sd((n, 4 * d), F32), sd((4 * n,), F32), sd((4 * n, d), F32), vec,
+        ),
+        in_specs=[any_spec, any_spec] + [spec] * 5,
+        out_specs=(any_spec, any_spec) + (spec,) * 12,
+        scratch_shapes=[
+            pltpu.VMEM(out.shape, BF16), pltpu.VMEM(gin.shape, F32), pltpu.SemaphoreType.DMA((2, 6)),
+        ],
+        compiler_params=pltpu.CompilerParams(vmem_limit_bytes=24 * 1024 * 1024),
+        name="deliver",
+    )(out, gin, gqkv, gout, g1, g2, gv)
+
+
 def gather_all(value):
     return lax.all_gather(value, "fsdp", axis=0, tiled=True)
-
-
-def pack_rows(ln1_gain, ln1_bias, qv_bias, out_bias, ln2_gain, ln2_bias, fc1_bias, fc2_bias):
-    n = ln1_gain.shape[0]
-    rows = [ln1_gain, ln1_bias, qv_bias[:n], qv_bias[n:], out_bias, ln2_gain, ln2_bias, fc2_bias]
-    rows += [fc1_bias[n * k : n * (k + 1)] for k in range(4)]
-    table = jnp.stack(rows, 0)
-    return jnp.pad(table, ((0, 4), (0, 128 - n)))
 
 
 def vectors(full):
@@ -695,55 +1151,36 @@
     return jnp.stack([jnp.pad(row.astype(F32), (0, width - row.shape[0])) for row in rows], 0)
 
 
-def per_device(
-    tokens, duplicate, targets,
-    ln1_gain, ln1_bias, qkv_weight, qv_bias, out_weight, out_bias,
-    ln2_gain, ln2_bias, fc1_weight, fc1_bias, fc2_weight, fc2_bias,
-    block16,
-):
+def per_device(tokens, duplicate, targets, *weights, block16):
     images, seq, d = tokens.shape
+    rows = tokens.transpose(1, 0, 2).reshape(seq * images, d)
+    back = lambda v: v.reshape(seq, images, d).transpose(1, 0, 2)
+    if block16:
+        results = deliver_call(*block_call(rows, duplicate, targets, weights))
+        return (back(results[0]), back(results[1])) + tuple(results[2:])
+
+    (
+        ln1_gain, ln1_bias, qkv_weight, qv_bias, out_weight, out_bias,
+        ln2_gain, ln2_bias, fc1_weight, fc1_bias, fc2_weight, fc2_bias,
+    ) = weights
     small = (ln1_gain, ln1_bias, qv_bias, out_bias, ln2_gain, ln2_bias, fc1_bias, fc2_bias)
-    rows = tokens.transpose(1, 0, 2).reshape(seq * images, d)
-    if block16:
-        n = d // 16
-        slots1, slots2, slots_v = gather_call(
-            qkv_weight, out_weight, fc1_weight, fc2_weight, pack_rows(*small).astype(BF16)
-        )
-        def whole(slots):
-            return slots.transpose((2, 0, 1) + tuple(range(3, slots.ndim))).reshape((16,) + slots.shape[3:])
-
-        g0, g1 = whole(slots1[0]), whole(slots1[1])
-        wqkv = jnp.concatenate([g0[:, :n], g0[:, n:], g1[:, :n]], 2).reshape(d, 3 * d)
-        wout = g1[:, n:].reshape(d, d)
-        w1 = whole(slots2[0]).reshape(16, 4, n, d).transpose(0, 2, 1, 3).reshape(d, 4 * d)
-        w2 = whole(slots2[1]).reshape(4 * d, d)
-        table = whole(slots_v)[:, :12, :n]
-        line = lambda k: table[:, k].reshape(d)
-        qv = table[:, 2:4].reshape(2 * d)
-        b1 = table[:, 8:12].reshape(4 * d)
-        vec = vectors((line(0), line(1), qv, line(4), line(5), line(6), b1, line(7)))
-    else:
-        wqkv, wout, w1, w2 = map(gather_all, (qkv_weight, out_weight, fc1_weight, fc2_weight))
-        vec = vectors(tuple(map(gather_all, small)))
+    wqkv, wout, w1, w2 = map(gather_all, (qkv_weight, out_weight, fc1_weight, fc2_weight))
+    vec = vectors(tuple(map(gather_all, small)))
     out, gin, gqkv, gout, g1, g2, gvec = compute(rows, duplicate, targets, vec, wqkv, wout, w1, w2)
-    if block16:
-        gqkv, gout, g1, g2, gvec = reduce_call(gqkv, gout, g1, g2, gvec)
-        p = lax.axis_index("fsdp")
-    else:
-        def scatter(value):
-            value = lax.psum_scatter(value.astype(F32), "fsdp", scatter_dimension=0, tiled=True)
-            return lax.psum(value, "dp")
-
-        gqkv, gout, g1, g2 = map(scatter, (gqkv, gout, g1, g2))
-        gvec = lax.psum(gvec, ("fsdp", "dp"))
-        p = lax.axis_index("fsdp")
+
+    def scatter(value):
+        value = lax.psum_scatter(value.astype(F32), "fsdp", scatter_dimension=0, tiled=True)
+        return lax.psum(value, "dp")
+
+    gqkv, gout, g1, g2 = map(scatter, (gqkv, gout, g1, g2))
+    gvec = lax.psum(gvec, ("fsdp", "dp"))
+    p = lax.axis_index("fsdp")
 
     def shard(value, whole_size):
         count = whole_size // lax.axis_size("fsdp")
         return lax.dynamic_slice(value, (p * count,), (count,))
 
     qv_grad = jnp.concatenate([gvec[2, :d], gvec[2, 2 * d : 3 * d]])
-    back = lambda v: v.reshape(seq, images, d).transpose(1, 0, 2)
     return (
         back(out), back(gin),
         shard(gvec[0], d), shard(gvec[1], d), gqkv, shard(qv_grad, 2 * d), gout, shard(gvec[3], d),

time: 239 us -> 146 us (0.61)
  Pallas kernels: 197 us -> 138 us
  local copies, waits for them, and re-layouts: 37.6 us -> 7.47 us
    pallas_call x3 -> x2, Pallas kernels: 197 us -> 138 us  [the longest x1 134 us: block_call(): pl.pallas_call(block_body, out_shape=(sd(tok.shape, BF16), sd(tok.shape,...]
    another operation x10 -> x0, local copies, waits for them, and re-layouts: 7.35 us -> none  [the longest x8 5.68 us: vectors(): jnp.stack([jnp.pad(row.astype(F32), (0, width - row.shape[0])) for row in...]
    unnamed x25 -> x14, local copies, waits for them, and re-layouts: 13.2 us -> 7.47 us
    dynamic_slice x8 -> x0, local copies, waits for them, and re-layouts: 4.66 us -> none  [shard(): return lax.dynamic_slice(value, (p * count,), (count,))]
    convert_element_type x7 -> x0, local copies, waits for them, and re-layouts: 4.32 us -> none  [vectors(): row.astype(F32)]
    slice x9 -> x0, local copies, waits for them, and re-layouts: 3.69 us -> none  [the longest x1 1.84 us: per_device(): line = lambda k: table[:, k].reshape(d)]
where the time goes in v2:
time: 146 us
  Pallas kernels  138 us (95%)
  local copies, waits for them, and re-layouts  7.47 us (5%)
    pallas_call x1, Pallas kernels, block_call(): pl.pallas_call(block_body, out_shape=(sd(tok.shape, BF16), sd(tok.shape,...  134 us
    unnamed x14, local copies, waits for them, and re-layouts  7.47 us
    pallas_call x1, Pallas kernels, deliver_call(): pl.pallas_call(deliver_body, out_shape=(sd(out.shape, BF16), sd(gin.shape...  3.5 us

profile of v2, /device:TPU:0, one launch (start us, length us, event | category | flops | bytes accessed | tf_op | source)
XLA Modules:
  0.0 146.0 jit_solution(8200064563474357970)
XLA Ops:
  0.7 134.2 %block16.1 = (bf16[2056,384]{1,0:T(8,128)(2,1)}, f32[2056,384]{1,0:T(8,128)}, f32[24,1152]{1,0:T(8,128)}, f32[24,384]{1,0:T(8,128)}, f32[24,1536]{1,0:T(8,128)},...) custom-call(bf16[2056,384]{1,0:T(8,128)(2,1)} %bitcast.9, s32[8,257]{1,0:T(8,128)} %dup.1, f32[8,384]{1,0:T(8,128)} %tgt.1, ...), custom_call_target="tpu_custom_call" | custom-call | tf_op jit(solution)/shard_map/block16/pallas_call | solution.py:1071
  134.9 0.0 copy-start
  134.9 1.9 %copy-done = f32[2056,384]{1,0:T(8,128)S(1)} copy-done((f32[2056,384]{1,0:T(8,128)S(1)}, f32[2056,384]{1,0:T(8,128)}, u32[]{:S(2)}) %copy-start) | copy-done | bytes 3158040
  136.8 0.0 copy-start.1
  136.8 1.4 copy-done.1
  138.2 0.0 copy-start.2
  138.2 0.9 copy-done.2
  139.1 0.0 copy-start.3
  139.1 0.9 copy-done.3
  140.0 0.0 copy-start.4
  140.0 0.9 copy-done.4
  140.9 0.0 copy-start.5
  140.9 0.8 copy-done.5
  141.7 0.0 copy-start.6
  141.7 0.7 copy-done.6
  142.4 3.5 %deliver.1 = (bf16[2056,384]{1,0:T(8,128)(2,1)}, f32[2056,384]{1,0:T(8,128)}, f32[24]{0:T(128)}, f32[24]{0:T(128)}, f32[24,1152]{1,0:T(8,128)}, /*index=5*/f32[4...) custom-call(bf16[2056,384]{1,0:T(8,128)(2,1)S(1)} %copy-done.1, ...), custom_call_target="tpu_custom_call" | custom-call | tf_op jit(solution)/shard_map/deliver/pallas_call | solution.py:1125
Async XLA Ops:
  134.9 1.9 %copy-start = (f32[2056,384]{1,0:T(8,128)S(1)}, f32[2056,384]{1,0:T(8,128)}, u32[]{:S(2)}) copy-start(f32[2056,384]{1,0:T(8,128)} %get-tuple-element.36.gin) | copy-start | bytes 9474052
  136.8 1.4 copy-start.1
  138.2 0.9 copy-start.2
  139.1 0.9 copy-start.3
  140.0 0.9 copy-start.4
  140.9 0.8 copy-start.5
  141.7 0.7 copy-start.6

commit v3 on v2

--- a/solution.py
+++ b/solution.py
@@ -49,18 +49,11 @@
 
 
 def gelu_pair(x):
-    e = jnp.exp(x * x * -0.5)
-    d = 1.0 + 0.231641888 * jnp.abs(x)
-    t = pl.reciprocal(d, approx=True)
-    t = t * (2.0 - d * t)
-    poly = t * (0.127414796 + t * (-0.142248368 + t * (0.710706871 + t * (-0.726576014 + t * 0.530702715))))
-    h = poly * e
-    phi = jnp.where(x >= 0.0, 1.0 - h, h)
-    return x * phi, phi + x * (e * 0.3989422804014327)
-
-
-def rows_of(values):
-    return jnp.concatenate(values, 0)
+    z = x * 0.7071067811865476
+    bell = jnp.exp(-(z * z))
+    tail = lax.erf(z)
+    half = 0.5 * x
+    return half + half * tail, 0.5 + (0.5 * tail + (x * 0.3989422804014327) * bell)
 
 
 LN1G, LN1B, BQKV, BOUT, LN2G, LN2B, BFC1, BFC2 = range(8)
@@ -104,6 +97,9 @@
 
     extra_lanes = pl.ds(x0, 128)
 
+    tok_copy = pltpu.make_async_copy(tok, out, gin_sem.at[0])
+    tok_copy.start()
+    tok_copy.wait()
     wqkv_t[...] = wqkv[...].T
     wout_t[...] = wout[...].T
     w1_t[...] = w1[...].T
@@ -146,10 +142,10 @@
         return carry
 
     for b in range(blocks):
-        stage[b] = tok[:, 128 * b : 128 * (b + 1)].astype(F32)
+        stage[b] = out[:, 128 * b : 128 * (b + 1)].astype(F32)
 
     lax.fori_loop(0, images, project_image, 0)
-    last = jnp.concatenate([tok[x0:, :].astype(F32), jnp.zeros((128 - images, d), F32)], 0)
+    last = jnp.concatenate([out[x0:, :].astype(F32), jnp.zeros((128 - images, d), F32)], 0)
     project(last.astype(BF16).T, extra_lanes, 128)
 
     lane_ids = lax.broadcasted_iota(jnp.int32, (HD, 128), 1)
@@ -381,7 +377,7 @@
     return pl.pallas_call(
         compute_body,
         out_shape=outs,
-        in_specs=[spec] * 8,
+        in_specs=[pl.BlockSpec(memory_space=pl.ANY)] + [spec] * 7,
         out_specs=(spec, pl.BlockSpec(memory_space=pl.ANY)) + (spec,) * 5,
         scratch_shapes=scratch,
         compiler_params=pltpu.CompilerParams(vmem_limit_bytes=64 * 1024 * 1024),
@@ -390,6 +386,7 @@
 
 MESH_ID = pl.DeviceIdType.MESH
 NZ = 4
+PAD = 16
 
 
 class Place:
@@ -554,7 +551,7 @@
     tokb, stage, xs, n1, qkv, att, n2, act, dpre, db2, db1, dos, dmid, probs,
     wqkv, wout, w1, w2_t, wt_a, wf,
     c_ln1g, c_ln1b, c_bqkv, c_bout, c_ln2g, c_ln2b, c_b1, c_b2,
-    stat_s, rl_s, ex_s, exq_s, rlx_s, exx_s, attx, dqkvx, a_g2, a_b2, tgt_t, gvec, allc,
+    stat_s, rl_s, exq, qxn, kxn, vxn, oxn, attx, dqkvx, a_g2, a_b2, tgt_t, gvec, allc,
     sv, tv, uv, av, bv, zv, f1, f2, fv,
     loc_sem, gsem1, gsem2, gsemv, rsem1, rsem2, rsemv, ready,
 ):
@@ -732,43 +729,63 @@
     project(extra_lanes, 128, stat_s[images, 0:1, :128], stat_s[images, 1:2, :128])
     gather2.go(2)
 
-    lane_ids = lax.broadcasted_iota(jnp.int32, (HD, 128), 1)
-
-    def pick(ref, row, i):
-        block = ref[row : row + HD, extra_lanes].astype(F32)
-        return jnp.sum(jnp.where(lane_ids == i, block, 0.0), 1, keepdims=True)
+    last = pl.ds(x0, PAD)
+    tail = t + PAD
+
+    def split(values, ref):
+        rows = values.T[:PAD]
+        for h in range(HEADS):
+            ref[h] = rows[:, h * HD : (h + 1) * HD].astype(BF16)
+
+    for k, ref in enumerate((qxn, kxn, vxn)):
+        split(qkv[k * d : (k + 1) * d, extra_lanes].astype(F32), ref)
+
+    def heads_of(base, lanes, h):
+        r0 = base + h * HD
+        return jnp.concatenate([qkv[r0 : r0 + HD, lanes], qkv[r0 : r0 + HD, last]], 1)
 
     def attend_image(i, carry):
         lanes = lanes_of(i)
-        for h in range(HEADS):
-            r0 = h * HD
-            q = qkv[r0 : r0 + HD, lanes]
-            k = qkv[d + r0 : d + r0 + HD, lanes]
-            v = qkv[2 * d + r0 : 2 * d + r0 + HD, lanes]
-            qx, kx, vx = pick(qkv, r0, i), pick(qkv, d + r0, i), pick(qkv, 2 * d + r0, i)
-            s = mm(k.T, q)
-            sx = jnp.sum(q.astype(F32) * kx, 0, keepdims=True)
-            top = jnp.maximum(jnp.max(s, 0, keepdims=True), sx)
-            e = jnp.exp(s - top)
-            ex = jnp.exp(sx - top)
-            rl = 1.0 / (jnp.sum(e, 0, keepdims=True) + ex)
+        own_row = lax.broadcasted_iota(jnp.int32, (PAD, t), 0) == i
+        lane = lax.broadcasted_iota(jnp.int32, (PAD, tail), 1)
+        own_key = (lane < t) | (lane == t + i)
+        own_query = lax.broadcasted_iota(jnp.int32, (PAD, tail), 0) == i
+
+        def score(h):
+            q = qkv[h * HD : (h + 1) * HD, lanes]
+            k = heads_of(d, lanes, h)
+            s = mm(jnp.concatenate([k[:, :t].T, kxn[h]], 0), q)
+            return s, mm(qxn[h], k)
+
+        def share(h, s, sq):
+            s = jnp.concatenate([s[:t], jnp.where(own_row, s[t:], -1e30)], 0)
+            e = jnp.exp(s - jnp.max(s, 0, keepdims=True))
+            rl = 1.0 / jnp.sum(e, 0, keepdims=True)
             e = e.astype(BF16)
             probs[i * HEADS + h] = e
-            o = (mm(v, e) + vx * ex) * rl
-            att[r0 : r0 + HD, lanes] = o.astype(BF16)
             rl_s[i, h : h + 1, :] = rl
-            ex_s[i, h : h + 1, :] = ex
-            sq = jnp.sum(k.astype(F32) * qx, 0, keepdims=True)
-            sxx = jnp.sum(kx * qx, 0, keepdims=True)
-            topx = jnp.maximum(jnp.max(sq, 1, keepdims=True), sxx)
-            eq = jnp.exp(sq - topx)
-            exx = jnp.exp(sxx - topx)
-            rlx = 1.0 / (jnp.sum(eq, 1, keepdims=True) + exx)
-            ox = (jnp.sum(v.astype(F32) * eq, 1, keepdims=True) + vx * exx) * rlx
-            attx[r0 : r0 + HD, :] = jnp.where(lane_ids == i, ox, attx[r0 : r0 + HD, :])
-            exq_s[i, h : h + 1, :] = eq
-            rlx_s[i, h : h + 1, :] = jnp.broadcast_to(rlx, (1, 128))
-            exx_s[i, h : h + 1, :] = jnp.broadcast_to(exx, (1, 128))
+            sq = jnp.where(own_key, sq, -1e30)
+            eq = jnp.exp(sq - jnp.max(sq, 1, keepdims=True))
+            eq = eq * (1.0 / jnp.sum(eq, 1, keepdims=True))
+            eq = jnp.where(own_query, eq, 0.0).astype(BF16)
+            exq[i * HEADS + h] = eq
+            return e, rl, eq
+
+        def mix(h, e, rl, eq):
+            v = heads_of(2 * d, lanes, h)
+            rows = slice(h * HD, (h + 1) * HD)
+            att[rows, lanes] = (mm(v, e) * rl).astype(BF16)
+            attx[rows, :PAD] += mm(v, eq, NT)
+
+        ready_scores = [score(0)]
+        shares = []
+        for h in range(HEADS):
+            if h + 1 < HEADS:
+                ready_scores.append(score(h + 1))
+            shares.append(share(h, *ready_scores[h]))
+            if h >= 1:
+                mix(h - 1, *shares[h - 1])
+        mix(HEADS - 1, *shares[HEADS - 1])
 
         @pl.when(i == images // 2)
         def _():
@@ -879,49 +896,57 @@
     pl.semaphore_wait(ready.at[0], 1)
     reduce2.go(0)
 
+    split(dos[:, extra_lanes].astype(F32), oxn)
+
     def attend_back(i, carry):
         lanes = lanes_of(i)
+
+        def slopes(h):
+            rows = slice(h * HD, (h + 1) * HD)
+            v = heads_of(2 * d, lanes, h)
+            do = dos[rows, lanes].astype(F32) * rl_s[i, h : h + 1, :]
+            dot_o = jnp.sum(do * att[rows, lanes].astype(F32), 0, keepdims=True)
+            dol = do.astype(BF16)
+            dp = mm(jnp.concatenate([v[:, :t].T, vxn[h]], 0), dol)
+            return dol, dot_o, dp, mm(oxn[h], v)
+
+        def scores_back(h, dol, dot_o, dp, dpq):
+            p = probs[i * HEADS + h]
+            ds = (p.astype(F32) * (dp - dot_o)).astype(BF16)
+            eq = exq[i * HEADS + h]
+            eqf = eq.astype(F32)
+            dsq = eqf * (dpq - jnp.sum(eqf * dpq, 1, keepdims=True))
+            return dol, p, ds, eq, dsq.astype(BF16)
+
+        def heads_back(h, dol, p, ds, eq, dsq):
+            rows = slice(h * HD, (h + 1) * HD)
+            q = qkv[rows, lanes]
+            k = heads_of(d, lanes, h)
+            scale = HD**-0.5
+            dq = mm(k, ds) * scale
+            dqx = mm(k, dsq, NT) * scale
+            dk = mm(q, ds, NT) + mm(qkv[rows, last], dsq)
+            dv = mm(dol, p, NT) + mm(dos[rows, last], eq)
+            dqkvx[rows, :PAD] += dqx
+            for base, value in ((d, dk), (2 * d, dv)):
+                dqkvx[base + h * HD : base + (h + 1) * HD, :PAD] += value[:, t:]
+            return dq, dk, dv
+
+        def keep_heads(h, dq, dk, dv):
+            for base, value in ((0, dq), (d, dk), (2 * d, dv)):
+                qkv[base + h * HD : base + (h + 1) * HD, lanes] = value[:, :t].astype(BF16)
+
+        first = [slopes(0)]
+        second = []
         for h in range(HEADS):
-            r0 = h * HD
-            q = qkv[r0 : r0 + HD, lanes]
-            k = qkv[d + r0 : d + r0 + HD, lanes]
-            v = qkv[2 * d + r0 : 2 * d + r0 + HD, lanes]
-            qx, kx, vx = pick(qkv, r0, i), pick(qkv, d + r0, i), pick(qkv, 2 * d + r0, i)
-            rl = rl_s[i, h : h + 1, :]
-            ex = ex_s[i, h : h + 1, :]
-            do = dos[r0 : r0 + HD, lanes].astype(F32) * rl
-            dot_o = jnp.sum(do * att[r0 : r0 + HD, lanes].astype(F32), 0, keepdims=True)
-            dol = do.astype(BF16)
-            p = probs[i * HEADS + h]
-            ds = (p.astype(F32) * (mm(v.T, dol) - dot_o)).astype(BF16)
-            dsx = ex * (jnp.sum(do * vx, 0, keepdims=True) - dot_o)
-            dq = mm(k, ds) + kx * dsx
-            dk = mm(q, ds, NT)
-            dv = mm(dol, p, NT)
-            qf = q.astype(F32)
-            kf = k.astype(F32)
-            vf = v.astype(F32)
-            dkx = jnp.sum(qf * dsx, 1, keepdims=True)
-            dvx = jnp.sum(do * ex, 1, keepdims=True)
-            eq = exq_s[i, h : h + 1, :]
-            rlx = rlx_s[i, h : h + 1, :1]
-            exx = exx_s[i, h : h + 1, :1]
-            dox = pick(dos, r0, i) * rlx
-            dotx = jnp.sum(dox * pick(att, r0, i), 0, keepdims=True)
-            dsq = eq * (jnp.sum(vf * dox, 0, keepdims=True) - dotx)
-            dsxx = exx * (jnp.sum(vx * dox, 0, keepdims=True) - dotx)
-            dqx = jnp.sum(kf * dsq, 1, keepdims=True) + kx * dsxx
-            dk = dk + qx * dsq
-            dv = dv + dox * eq
-            dkx = dkx + qx * dsxx
-            dvx = dvx + dox * exx
-            scale = HD**-0.5
-            for base, main, tail in ((0, dq * scale, dqx * scale), (d, dk, dkx), (2 * d, dv, dvx)):
-                rows = slice(base + r0, base + r0 + HD)
-                qkv[rows, lanes] = main.astype(BF16)
-                dqkvx[rows, :] = jnp.where(lane_ids == i, tail, dqkvx[rows, :])
-
-        for step, when in ((1, 1), (2, 3), (3, 5), (4, 7)):
+            if h + 1 < HEADS:
+                first.append(slopes(h + 1))
+            second.append(scores_back(h, *first[h]))
+            if h >= 1:
+                keep_heads(h - 1, *heads_back(h - 1, *second[h - 1]))
+        keep_heads(HEADS - 1, *heads_back(HEADS - 1, *second[HEADS - 1]))
+
+        for step, when in ((1, 1), (2, 5), (3, 7)):
 
             @pl.when(i == when)
             def _(step=step):
@@ -973,7 +998,7 @@
     reduce_v = Reduce(at, tv, uv, av, bv, zv, fv, 8, rsemv)
     reduce1.go(0)
     reduce_v.go(0)
-    reduce2.go(5)
+    reduce2.go(4)
 
     def finish(lanes, count, mu, r):
         u = (xs[:, lanes].astype(F32) - mu) * r
@@ -998,6 +1023,7 @@
     ]
     for copy in copies:
         copy.start()
+    reduce2.go(5)
     o1[...] = jnp.concatenate([f2[0, shard * k : shard * (k + 1)] for k in range(4)], 1)
     o2[...] = f2[1]
     for step in (3, 4, 5):
@@ -1037,7 +1063,7 @@
         vm((d, w), BF16),
         vm((d, w), BF16),
         vm((d, w), F32),
-        vm((images * HEADS, t, t), BF16),
+        vm((images * HEADS, t + PAD, t), BF16),
         vm((d, 3 * d), BF16),
         vm((d, d), BF16),
         vm((d, ff), BF16),
@@ -1048,10 +1074,9 @@
         vm((d, 128), F32), vm((d, 128), F32), vm((ff, 128), F32), vm((d, 128), F32),
         vm((images + 1, 8, t), F32),
         vm((images, 8, t), F32),
-        vm((images, 8, t), F32),
-        vm((images, 8, t), F32),
-        vm((images, 8, 128), F32),
-        vm((images, 8, 128), F32),
+        vm((images * HEADS, PAD, t + PAD), BF16),
+        vm((HEADS, PAD, HD), BF16), vm((HEADS, PAD, HD), BF16),
+        vm((HEADS, PAD, HD), BF16), vm((HEADS, PAD, HD), BF16),
         vm((d, 128), F32),
         vm((3 * d, 128), F32),
         vm((d, 128), F32), vm((d, 128), F32),
@@ -1133,7 +1158,7 @@
         scratch_shapes=[
             pltpu.VMEM(out.shape, BF16), pltpu.VMEM(gin.shape, F32), pltpu.SemaphoreType.DMA((2, 6)),
         ],
-        compiler_params=pltpu.CompilerParams(vmem_limit_bytes=24 * 1024 * 1024),
+        compiler_params=pltpu.CompilerParams(vmem_limit_bytes=64 * 1024 * 1024),
         name="deliver",
     )(out, gin, gqkv, gout, g1, g2, gv)
 

time: 146 us -> 127 us (0.87)
  Pallas kernels: 138 us -> 126 us
  local copies, waits for them, and re-layouts: 7.47 us -> 0 us
    pallas_call x1, Pallas kernels: 134 us -> 121 us  [block_call(): pl.pallas_call(block_body, out_shape=(sd(tok.shape, BF16), sd(tok.shape,...]
    unnamed x14 -> x0, local copies, waits for them, and re-layouts: 7.47 us -> none
    pallas_call x1, Pallas kernels: 3.5 us -> 5.57 us  [deliver_call(): pl.pallas_call(deliver_body, out_shape=(sd(out.shape, BF16), sd(gin.shape...]
where the time goes in v3:
time: 127 us
  Pallas kernels  126 us (99%)
    pallas_call x1, Pallas kernels, block_call(): pl.pallas_call(block_body, out_shape=(sd(tok.shape, BF16), sd(tok.shape,...  121 us
    pallas_call x1, Pallas kernels, deliver_call(): pl.pallas_call(deliver_body, out_shape=(sd(out.shape, BF16), sd(gin.shape...  5.57 us

profile of v3, /device:TPU:0, one launch (start us, length us, event | category | flops | bytes accessed | tf_op | source)
XLA Modules:
  0.0 127.0 jit_solution(15194611987150282563)
XLA Ops:
  0.7 120.5 %block16.1 = (bf16[2056,384]{1,0:T(8,128)(2,1)}, f32[2056,384]{1,0:T(8,128)}, f32[24,1152]{1,0:T(8,128)}, f32[24,384]{1,0:T(8,128)}, f32[24,1536]{1,0:T(8,128)},...) custom-call(bf16[2056,384]{1,0:T(8,128)(2,1)} %bitcast.9, s32[8,257]{1,0:T(8,128)} %dup.1, f32[8,384]{1,0:T(8,128)} %tgt.1, ...), custom_call_target="tpu_custom_call" | custom-call | tf_op jit(solution)/shard_map/block16/pallas_call | solution.py:1096
  121.2 5.6 %deliver.1 = (bf16[2056,384]{1,0:T(8,128)(2,1)}, f32[2056,384]{1,0:T(8,128)}, f32[24]{0:T(128)}, f32[24]{0:T(128)}, f32[24,1152]{1,0:T(8,128)}, /*index=5*/f32[4...) custom-call(bf16[2056,384]{1,0:T(8,128)(2,1)} %get-tuple-element.35., ...), custom_call_target="tpu_custom_call" | custom-call | tf_op jit(solution)/shard_map/deliver/pallas_call | solution.py:1150

commit v4 on v3

--- a/solution.py
+++ b/solution.py
@@ -386,7 +386,11 @@
 
 MESH_ID = pl.DeviceIdType.MESH
 NZ = 4
-PAD = 16
+UNITS = 2
+UNITS1 = 1
+UNITS2 = 2
+CHUNK = 2
+FFB = 128
 
 
 class Place:
@@ -549,11 +553,11 @@
     tok, dup, tgt, s_ln1g, s_ln1b, s_qkv, s_qvb, s_out, s_bout, s_ln2g, s_ln2b, s_fc1, s_b1, s_fc2, s_b2,
     out, gin, oqkv, oout, o1, o2, ovec,
     tokb, stage, xs, n1, qkv, att, n2, act, dpre, db2, db1, dos, dmid, probs,
-    wqkv, wout, w1, w2_t, wt_a, wf,
-    c_ln1g, c_ln1b, c_bqkv, c_bout, c_ln2g, c_ln2b, c_b1, c_b2,
-    stat_s, rl_s, exq, qxn, kxn, vxn, oxn, attx, dqkvx, a_g2, a_b2, tgt_t, gvec, allc,
-    sv, tv, uv, av, bv, zv, f1, f2, fv,
-    loc_sem, gsem1, gsem2, gsemv, rsem1, rsem2, rsemv, ready,
+    wqkv, wout, wout_t, w1, w2_t, wt_a, wf,
+    c_ln1g, c_ln1b, c_q, c_v, c_bout, c_ln2g, c_ln2b, c_b1, c_b2,
+    stat_s, rl_s, ex_s, pq_s, pxq_s, attx, dqkvx, a_g1, a_b1, a_g2, a_b2, tgt_t, gvec, allc, vec_s,
+    tail_s, tv, uv, av, bv, zv, f_a, f_b, f_c, f_d, f_v,
+    loc_sem, gsem0, gsem1, gsem2, gsem3, rsem_a, rsem_b, rsem_c, rsem_d, rsem_v, ready,
 ):
     images, seq = dup.shape
     d = tok.shape[1]
@@ -561,12 +565,16 @@
     x0 = images * t
     ff = w1.shape[1]
     w = x0 + 128
-    shard = d // 16
+    n = d // 16
     blocks = d // 128
     at = Place()
-
-    def lanes_of(i):
-        return pl.ds(pl.multiple_of(i * t, 128), t)
+    every = range(16)
+    pairs = HEADS // 2
+    mine = pl.ds(pl.multiple_of(at.c * d, 128), d)
+    own = (at.a * 2 + at.b) * NZ + at.z
+
+    def lanes_of(i, count=1):
+        return pl.ds(pl.multiple_of(i * t, 128), t * count)
 
     extra_lanes = pl.ds(x0, 128)
 
@@ -584,40 +592,50 @@
     tok_copy = pltpu.make_async_copy(tok, tokb, loc_sem.at[0])
     tok_copy.start()
 
-    own = span(((at.a * 2 + at.b) * NZ + at.z) * 16, 16)
-    table = jnp.zeros((16, 128), F32)
-    sv[own, :] = table
-    base = ((at.a * 2 + at.b) * NZ + at.z) * 16
-    flat = [s_ln1g[...], s_ln1b[...], s_qvb[:shard], s_qvb[shard:], s_bout[...], s_ln2g[...], s_ln2b[...], s_b2[...]]
-    flat += [s_b1[shard * k : shard * (k + 1)] for k in range(4)]
+    r0, r2, r3 = n + 8, 2 * n, 2 * n + 16
+    slots0 = act.at[: 16 * r0, :d]
+    slots1 = act.at[16 * r0 : 32 * r0]
+    slots2 = act.at[: 16 * r2]
+    slots3 = dpre.at[: 16 * r3]
+    group = [pl.ds(k * d, d) for k in range(4)]
+    later_mine = pl.ds(pl.multiple_of((2 + at.c) * d, 128), d)
+    q = s_qkv[...].astype(F32)
+
+    def pair_of(p):
+        return jnp.concatenate([q[:, d * k + 128 * p : d * k + 128 * (p + 1)] for k in range(3)], 1)
+
+    vec_s[...] = jnp.zeros_like(vec_s)
+    flat = [s_ln1g[...], s_ln1b[...], s_qvb[:n], s_qvb[n:], s_bout[...], s_ln2g[...], s_ln2b[...], s_b2[...]]
+    flat += [s_b1[n * k : n * (k + 1)] for k in range(4)]
     for k, line in enumerate(flat):
-        sv[pl.ds(base + k, 1), :shard] = line.astype(F32).reshape(1, shard)
-    halves = (pl.ds(0, d), pl.ds(d, d))
-    mine = pl.ds(pl.multiple_of(at.c * d, 128), d)
-    own1 = span(((at.a * 2 + at.b) * NZ + at.z) * 2 * shard, 2 * shard)
-    own2 = span(((at.a * 2 + at.b) * NZ + at.z) * 4 * shard, 4 * shard)
-    slots1 = act.at[: 16 * 2 * shard]
-    slots2 = dpre
+        lo = 128 * (k // 8)
+        vec_s[k % 8 : k % 8 + 1, lo : lo + n] = line.astype(F32).reshape(1, n)
+    slots0[span(own * r0, r0), :] = jnp.concatenate([pair_of(0), vec_s[...]], 0).astype(BF16)
+    own1, own2, own3 = (span(own * r, r) for r in (r0, r2, r3))
+    w_out = s_out[...].astype(F32)
+    blank = jnp.zeros((8, d), F32)
 
     @pl.when(at.c == 0)
     def _():
-        q = s_qkv[...].astype(F32)
         f = s_fc1[...].astype(F32)
-        slots1[own1, halves[0]] = jnp.concatenate([q[:, :d], q[:, d : 2 * d]], 0).astype(BF16)
-        slots2[own2, halves[0]] = jnp.concatenate([f[:, k * d : (k + 1) * d] for k in range(4)], 0).astype(BF16)
+        slots1[own1, group[0]] = jnp.concatenate([pair_of(1), blank], 0).astype(BF16)
+        slots2[own2, group[2]] = jnp.concatenate([f[:, :d], f[:, d : 2 * d]], 0).astype(BF16)
+        parts = [f[:, 2 * d : 3 * d], f[:, 3 * d :], w_out[:16]]
+        slots3[own3, group[0]] = jnp.concatenate(parts, 0).astype(BF16)
 
     @pl.when(at.c == 1)
     def _():
-        q = s_qkv[...].astype(F32)
-        slots1[own1, halves[1]] = jnp.concatenate([q[:, 2 * d :], s_out[...].astype(F32)], 0).astype(BF16)
-        slots2[own2, halves[1]] = s_fc2[...]
+        slots1[own1, group[1]] = jnp.concatenate([pair_of(2), blank], 0).astype(BF16)
+        slots2[own2, group[3]] = s_fc2[:r2]
+        parts = [s_fc2[r2:].astype(F32), w_out[16:], blank]
+        slots3[own3, group[1]] = jnp.concatenate(parts, 0).astype(BF16)
 
     greet(at)
-    gather_v = Gather(at, sv, 16, gsemv, False)
-    gather1 = Gather(at, slots1.at[:, mine], 2 * shard, gsem1, True)
-    gather2 = Gather(at, slots2.at[:, mine], 4 * shard, gsem2, True)
-    gather_v.go(0)
-    gather1.go(0)
+    g0 = Gather(at, slots0, r0, gsem0, False)
+    g1 = Gather(at, slots1.at[:, mine], r0, gsem1, True)
+    g2 = Gather(at, slots2.at[:, later_mine], r2, gsem2, True)
+    g3 = Gather(at, slots3.at[:, mine], r3, gsem3, True)
+    g0.go(0)
 
     tok_copy.wait()
     for b in range(blocks):
@@ -636,12 +654,8 @@
         stat_s[i, 1:2, :] = r
         return carry
 
-    gather_v.go(1)
-    gather1.go(1)
-    gather2.go(0)
     lax.fori_loop(0, images // 2, turn, 0)
-    gather_v.go(2)
-    gather1.go(2)
+    g1.go(0)
     lax.fori_loop(images // 2, images, turn, 0)
     last = jnp.concatenate([tokb[x0:, :].astype(F32), jnp.zeros((128 - images, d), F32)], 0)
     x = last.astype(BF16).T
@@ -654,173 +668,208 @@
     n1[d : d + 16, :] = ones_row
     n2[d : d + 16, :] = ones_row
     att[d : d + 16, :] = ones_row
-    attx[...] = jnp.zeros_like(attx)
-    dqkvx[...] = jnp.zeros_like(dqkvx)
-    a_g2[...] = jnp.zeros_like(a_g2)
-    a_b2[...] = jnp.zeros_like(a_b2)
-    gather_v.go(3)
-    gather1.go(3)
-
-    def slot_v(p):
+    for ref in (attx, dqkvx, a_g1, a_b1, a_g2, a_b2):
+        ref[...] = jnp.zeros_like(ref)
+    g2.go(0)
+    g0.go(1)
+    g0.go(2)
+    g3.go(0)
+    g1.go(1)
+    g0.go(3)
+    g1.go(2)
+    g2.go(1)
+
+    def slot_of_chip(p):
         px, py, pz = p % 2, (p // 2) % 2, p // 4
         pa = py + at.c * (px - py)
         pb = px + at.c * (py - px)
-        return sv[span(((pa * 2 + pb) * NZ + pz) * 16, 16), :]
-
+        return slots0[span(((pa * 2 + pb) * NZ + pz) * r0, r0), :].astype(F32)
+
+    first = [slot_of_chip(p) for p in every]
     for half in range(2):
-        allc[half] = jnp.concatenate([slot_v(p) for p in range(8 * half, 8 * half + 8)], 0).T
+        rows = [s[n:, 128 * half : 128 * (half + 1)] for s in first]
+        allc[half] = jnp.concatenate(rows, 0).T
+    lane_ids = lax.broadcasted_iota(jnp.int32, (n, 128), 1)
+    ones = jnp.ones((128, 128), BF16)
 
     def column(ref, entries):
-        runs = []
-        ids = lax.broadcasted_iota(jnp.int32, (shard, 128), 1)
-        for p, k in entries:
-            runs.append(jnp.where(ids == 16 * (p % 8) + k, allc[p // 8, :shard, :], 0.0))
-        block = jnp.sum(jnp.concatenate(runs, 0), 1, keepdims=True)
-        ref[...] = jnp.broadcast_to(block, (len(entries) * shard, 128))
-
-    every = range(16)
+        runs = [jnp.where(lane_ids == 8 * p + k % 8, allc[k // 8, :n, :], 0.0) for p, k in entries]
+        ref[...] = mm(jnp.concatenate(runs, 0).astype(BF16), ones)
+
     column(c_ln1g, [(p, V_LN1G) for p in every])
     column(c_ln1b, [(p, V_LN1B) for p in every])
-    column(c_bqkv.at[:d], [(p, V_QV + k) for p in range(8) for k in range(2)])
-    c_bqkv[d : 2 * d, :] = jnp.zeros((d, 128), F32)
-    column(c_bqkv.at[2 * d :], [(p, V_QV + k) for p in range(8, 16) for k in range(2)])
+    column(c_q, [(p, V_QV + k) for p in range(8) for k in range(2)])
+    column(c_v, [(p, V_QV + k) for p in range(8, 16) for k in range(2)])
+
+    def put_pair(p, block):
+        block = block.astype(BF16)
+        wqkv[:, p * d : (p + 1) * d] = block
+        wt_a[p // 2, (p % 2) * d : (p % 2 + 1) * d, :] = block.T
+
+    put_pair(0, jnp.concatenate([s[:n] for s in first], 0))
+
+    def unpack(slots, which, lanes, r, lo, hi):
+        runs = []
+        for p in every:
+            s = slot_of(p, which)
+            runs.append(slots[r * s : r * (s + 1), lanes].astype(F32)[lo:hi])
+        return runs
+
+    def project(p, lanes, count, mu=None, r=None):
+        if p == 0:
+            u = (xs[:, lanes].astype(F32) - mu) * r
+            y = (u * wide(c_ln1g[...], count) + wide(c_ln1b[...], count)).astype(BF16)
+            n1[:d, lanes] = y
+        else:
+            y = n1[:d, lanes]
+        y = mm(wt_a[p // 2, (p % 2) * d : (p % 2 + 1) * d, :], y)
+        heads = slice(128 * p, 128 * (p + 1))
+        query = (y[:128] + wide(c_q[heads, :], count)).astype(BF16) * jnp.asarray(HD**-0.5, BF16)
+        value = (y[256:] + wide(c_v[heads, :], count)).astype(BF16)
+        qkv[p * d : (p + 1) * d, lanes] = jnp.concatenate([query, y[128:256].astype(BF16), value], 0)
+
+    def rows_of(part, h):
+        row = (h // 2) * d + part * 128 + (h % 2) * HD
+        return slice(row, row + HD)
+
+    head_lanes = lax.broadcasted_iota(jnp.int32, (HD, 128), 1)
+
+    def pick(ref, rows, i):
+        return jnp.sum(jnp.where(head_lanes == i, ref[rows, extra_lanes].astype(F32), 0.0), 1, keepdims=True)
+
+    def row_dot(a, column):
+        return jnp.sum(a.astype(F32) * column, 0, keepdims=True)
+
+    def column_dot(a, row):
+        return jnp.sum(a.astype(F32) * row, 1, keepdims=True)
+
+    def place_column(ref, rows, i, column):
+        ref[rows, :] = jnp.where(head_lanes == i, column, ref[rows, :])
+
+    def score(i, h):
+        q, k = (qkv[rows_of(part, h), lanes_of(i)] for part in range(2))
+        qx, kx = (pick(qkv, rows_of(part, h), i) for part in range(2))
+        return mm(k.T, q), row_dot(q, kx), row_dot(k, qx), jnp.sum(qx * kx, 0, keepdims=True)
+
+    def share(i, h, s, sx, sq, sxq):
+        top = jnp.maximum(jnp.max(s, 0, keepdims=True), sx)
+        e = jnp.exp(s - top)
+        ex = jnp.exp(sx - top)
+        rl = 1.0 / (jnp.sum(e, 0, keepdims=True) + ex)
+        e = e.astype(BF16)
+        probs[i * HEADS + h] = e
+        rl_s[i, h : h + 1, :] = rl
+        ex_s[i, h : h + 1, :] = ex
+        top = jnp.maximum(jnp.max(sq, 1, keepdims=True), sxq)
+        eq = jnp.exp(sq - top)
+        exq = jnp.exp(sxq - top)
+        rlq = 1.0 / (jnp.sum(eq, 1, keepdims=True) + exq)
+        pq = eq * rlq
+        pxq = exq * rlq
+        pq_s[i, h : h + 1, :] = pq
+        pxq_s[i, h : h + 1, :] = jnp.broadcast_to(pxq, (1, 128))
+        return e, ex, rl, pq, pxq
+
+    def mix(i, h, e, ex, rl, pq, pxq):
+        v = qkv[rows_of(2, h), lanes_of(i)]
+        vx = pick(qkv, rows_of(2, h), i)
+        rows = slice(h * HD, (h + 1) * HD)
+        att[rows, lanes_of(i)] = ((mm(v, e) + vx * ex) * rl).astype(BF16)
+        place_column(attx, rows, i, column_dot(v, pq) + vx * pxq)
+
+    def attend(units):
+        scores = [score(*units[0])]
+        shares = []
+        for k, unit in enumerate(units):
+            if k + 1 < len(units):
+                scores.append(score(*units[k + 1]))
+            shares.append(share(*unit, *scores[k]))
+            if k >= 1:
+                mix(*units[k - 1], *shares[k - 1])
+        mix(*units[-1], *shares[-1])
+
+    def forward_pair(p, steps):
+        if p == 0:
+
+            def project_image(i, carry):
+                project(0, lanes_of(i), t, stat_s[i, 0:1, :], stat_s[i, 1:2, :])
+                return carry
+
+            lax.fori_loop(0, images, project_image, 0)
+            project(0, extra_lanes, 128, stat_s[images, 0:1, :128], stat_s[images, 1:2, :128])
+        else:
+
+            def project_images(i, carry):
+                project(p, lanes_of(2 * i, 2), 2 * t)
+                return carry
+
+            lax.fori_loop(0, images // 2, project_images, 0)
+            project(p, extra_lanes, 128)
+        for step in steps[0]:
+            step()
+
+        def attend_images(i, carry):
+            attend([(UNITS * i + k, 2 * p + h) for k in range(UNITS) for h in range(2)])
+            for when in range(images // UNITS):
+
+                @pl.when(i == when)
+                def _(when=when):
+                    for step in steps[1 + when]:
+                        step()
+
+            return carry
+
+        lax.fori_loop(0, images // UNITS, attend_images, 0)
+
+    def later(item, step):
+        return lambda: item.go(step)
+
+    forward_pair(0, [[later(g3, 1)], [], [later(g1, 3), later(g2, 2)], [], []])
+    g1.go(4)
+    for k in range(2):
+        put_pair(1 + k, jnp.concatenate(unpack(slots1, k, group[k], r0, 0, n), 0))
+    forward_pair(1, [[], [later(g3, 2)], [], [later(g2, 3)], []])
+    forward_pair(2, [[], [later(g3, 3)], [], [], [later(g2, 4)]])
+    att[:d, extra_lanes] = attx[...].astype(BF16)
     column(c_bout, [(p, V_BOUT) for p in every])
     column(c_ln2g, [(p, V_LN2G) for p in every])
     column(c_ln2b, [(p, V_LN2B) for p in every])
     column(c_b2, [(p, V_BFC2) for p in every])
     column(c_b1, [(p, V_BFC1 + k) for p in every for k in range(4)])
-
-    gather1.go(4)
-    gather2.go(1)
-
-    def unpack(slots, group, r, k):
-        part = slots[:, halves[group]]
-        runs = []
-        for p in every:
-            s = slot_of(p, group)
-            runs.append(slots[r * s : r * (s + 1), halves[group]].astype(F32)[k * shard : (k + 1) * shard])
-        return jnp.concatenate(runs, 0).astype(BF16)
-
+    g3.go(4)
+    runs = zip(unpack(slots3, 0, group[0], r3, r2, r3), unpack(slots3, 1, group[1], r3, r2, r2 + 8))
+    block = jnp.concatenate([part for run in runs for part in run], 0).astype(BF16)
+    wout[...] = block
+    wout_t[...] = block.T
     for k in range(4):
-        block = unpack(slots1, k // 2, 2 * shard, k % 2)
-        if k < 3:
-            wqkv[:, k * d : (k + 1) * d] = block
-        else:
-            wout[...] = block
-        wt_a[k // 2, (k % 2) * d : (k % 2 + 1) * d, :] = block.T
-
-    def project(lanes, count, mu, r):
-        u = (xs[:, lanes].astype(F32) - mu) * r
-        n = (u * wide(c_ln1g[...], count) + wide(c_ln1b[...], count)).astype(BF16)
-        n1[:d, lanes] = n
-        for k in range(3):
-            rows = slice(k * d, (k + 1) * d)
-            y = mm(wt_a[k // 2, (k % 2) * d : (k % 2 + 1) * d, :], n) + wide(c_bqkv[rows, :], count)
-            y = y.astype(BF16)
-            if k == 0:
-                y = y * jnp.asarray(HD**-0.5, BF16)
-            qkv[rows, lanes] = y
-
-    def project_image(i, carry):
-        project(lanes_of(i), t, stat_s[i, 0:1, :], stat_s[i, 1:2, :])
-        return carry
-
-    lax.fori_loop(0, images, project_image, 0)
-    project(extra_lanes, 128, stat_s[images, 0:1, :128], stat_s[images, 1:2, :128])
-    gather2.go(2)
-
-    last = pl.ds(x0, PAD)
-    tail = t + PAD
-
-    def split(values, ref):
-        rows = values.T[:PAD]
-        for h in range(HEADS):
-            ref[h] = rows[:, h * HD : (h + 1) * HD].astype(BF16)
-
-    for k, ref in enumerate((qxn, kxn, vxn)):
-        split(qkv[k * d : (k + 1) * d, extra_lanes].astype(F32), ref)
-
-    def heads_of(base, lanes, h):
-        r0 = base + h * HD
-        return jnp.concatenate([qkv[r0 : r0 + HD, lanes], qkv[r0 : r0 + HD, last]], 1)
-
-    def attend_image(i, carry):
-        lanes = lanes_of(i)
-        own_row = lax.broadcasted_iota(jnp.int32, (PAD, t), 0) == i
-        lane = lax.broadcasted_iota(jnp.int32, (PAD, tail), 1)
-        own_key = (lane < t) | (lane == t + i)
-        own_query = lax.broadcasted_iota(jnp.int32, (PAD, tail), 0) == i
-
-        def score(h):
-            q = qkv[h * HD : (h + 1) * HD, lanes]
-            k = heads_of(d, lanes, h)
-            s = mm(jnp.concatenate([k[:, :t].T, kxn[h]], 0), q)
-            return s, mm(qxn[h], k)
-
-        def share(h, s, sq):
-            s = jnp.concatenate([s[:t], jnp.where(own_row, s[t:], -1e30)], 0)
-            e = jnp.exp(s - jnp.max(s, 0, keepdims=True))
-            rl = 1.0 / jnp.sum(e, 0, keepdims=True)
-            e = e.astype(BF16)
-            probs[i * HEADS + h] = e
-            rl_s[i, h : h + 1, :] = rl
-            sq = jnp.where(own_key, sq, -1e30)
-            eq = jnp.exp(sq - jnp.max(sq, 1, keepdims=True))
-            eq = eq * (1.0 / jnp.sum(eq, 1, keepdims=True))
-            eq = jnp.where(own_query, eq, 0.0).astype(BF16)
-            exq[i * HEADS + h] = eq
-            return e, rl, eq
-
-        def mix(h, e, rl, eq):
-            v = heads_of(2 * d, lanes, h)
-            rows = slice(h * HD, (h + 1) * HD)
-            att[rows, lanes] = (mm(v, e) * rl).astype(BF16)
-            attx[rows, :PAD] += mm(v, eq, NT)
-
-        ready_scores = [score(0)]
-        shares = []
-        for h in range(HEADS):
-            if h + 1 < HEADS:
-                ready_scores.append(score(h + 1))
-            shares.append(share(h, *ready_scores[h]))
-            if h >= 1:
-                mix(h - 1, *shares[h - 1])
-        mix(HEADS - 1, *shares[HEADS - 1])
-
-        @pl.when(i == images // 2)
-        def _():
-            gather2.go(3)
-
-        return carry
-
-    lax.fori_loop(0, images, attend_image, 0)
-    att[:d, extra_lanes] = attx[...].astype(BF16)
-    gather2.go(4)
-    for k in range(4):
-        block = unpack(slots2, 0, 4 * shard, k)
+        slots, lanes, r = (slots2, group[2], r2) if k < 2 else (slots3, group[0], r3)
+        block = jnp.concatenate(unpack(slots, 0, lanes, r, (k % 2) * n, (k % 2 + 1) * n), 0).astype(BF16)
         w1[:, k * d : (k + 1) * d] = block
         wf[0, k * d : (k + 1) * d, :] = block.T
     for p in every:
         s = slot_of(p, 1)
-        wf[1, 4 * shard * p : 4 * shard * (p + 1), :] = slots2[4 * shard * s : 4 * shard * (s + 1), halves[1]]
+        for k, (slots, lanes, r) in enumerate(((slots2, group[3], r2), (slots3, group[1], r3))):
+            start = 4 * n * p + r2 * k
+            wf[1, start : start + r2, :] = slots[r * s : r * s + r2, lanes]
     w2_t[...] = wf[1].T
     act[ff : ff + 16, :] = ones_row
 
+    def middle(lanes, count):
+        return xs[:, lanes].astype(F32) + mm(wout_t[...], att[:d, lanes]) + wide(c_bout[...], count)
+
     def feed(lanes, count, d_final):
-        mid = xs[:, lanes].astype(F32) + mm(wt_a[1, d:, :], att[:d, lanes]) + wide(c_bout[...], count)
-        u, r = normalise(mid)
-        n = (u * wide(c_ln2g[...], count) + wide(c_ln2b[...], count)).astype(BF16)
-        n2[:d, lanes] = n
+        u, r = normalise(middle(lanes, count))
+        y = (u * wide(c_ln2g[...], count) + wide(c_ln2b[...], count)).astype(BF16)
+        n2[:d, lanes] = y
         db = d_final.astype(BF16)
         db2[:, lanes] = db
-        for j in range(ff // 256):
-            rows = slice(256 * j, 256 * (j + 1))
-            pre = mm(wf[0, rows, :], n) + wide(c_b1[rows, :], count)
+        for j in range(ff // FFB):
+            rows = slice(FFB * j, FFB * (j + 1))
+            pre = mm(wf[0, rows, :], y) + wide(c_b1[rows, :], count)
             da = mm(wf[1, rows, :], db)
             value, slope = gelu_pair(pre)
             act[rows, lanes] = value.astype(BF16)
             dpre[rows, lanes] = (slope * da).astype(BF16)
-        final = mid + mm(w2_t[...], act[:ff, lanes]) + wide(c_b2[...], count)
         dn = mm(w1[...], dpre[:, lanes])
         a_g2[...] += fold(dn * u)
         a_b2[...] += fold(dn)
@@ -829,211 +878,266 @@
         low = dm.astype(BF16)
         db1[:, lanes] = low
         dos[:, lanes] = mm(wout[...], low).astype(BF16)
-        return final.T
 
     def keep_row(row):
-        first = lax.broadcasted_iota(jnp.int32, row.shape, 1) == 0
-        return jnp.where(first, 1.0, 1.0 - row.astype(F32))
-
-    def feed_image(i, carry):
+        position = lax.broadcasted_iota(jnp.int32, row.shape, 1) == 0
+        return jnp.where(position, 1.0, 1.0 - row.astype(F32))
+
+    def cotangent(i):
         keep = keep_row(dup[pl.ds(i, 1), :])
-        count = jnp.sum(keep, 1, keepdims=True)
-        scale = seq * keep[:, :t] / count
+        scale = seq * keep[:, :t] / jnp.sum(keep, 1, keepdims=True)
         ids = lax.broadcasted_iota(jnp.int32, (d, 128), 1)
-        target = jnp.sum(jnp.where(ids == i, tgt_t[...], 0.0), 1, keepdims=True)
-        store_image(i, feed(lanes_of(i), t, target * scale))
+        return jnp.sum(jnp.where(ids == i, tgt_t[...], 0.0), 1, keepdims=True) * scale
+
+    def feed_images(k, carry):
+        d_final = jnp.concatenate([cotangent(CHUNK * k + m) for m in range(CHUNK)], 1)
+        feed(lanes_of(CHUNK * k, CHUNK), CHUNK * t, d_final)
         return carry
 
-    lax.fori_loop(0, images, feed_image, 0)
+    lax.fori_loop(0, images // CHUNK, feed_images, 0)
     keep_all = keep_row(dup[...])
     scale_x = seq * keep_all[:, t:] / jnp.sum(keep_all, 1, keepdims=True)
     scale_x = jnp.broadcast_to(scale_x, (images, 128))
     scale_x = jnp.concatenate([scale_x, jnp.zeros((128 - images, 128), F32)], 0).T[:1, :]
-    store_last(feed(extra_lanes, 128, tgt_t[...] * scale_x))
+    feed(extra_lanes, 128, tgt_t[...] * scale_x)
+
+    def put(buf, which, parts, lo=0, step=None):
+        for p in every:
+            slot = jnp.concatenate([part[n * p + a : n * p + b] for part, a, b in parts], 0).astype(BF16)
+            start = step * slot_of(p, which) + lo
+            buf[which, start : start + slot.shape[0], :] = slot
+
+    for j in range(ff // 256):
+        rows = slice(256 * j, 256 * (j + 1))
+        g = mm(act[rows, :], db2[...], NT).astype(BF16)
+        for lo in range(256 * j, 256 * (j + 1), 16):
+            p, off = lo // (4 * n), lo % (4 * n)
+            buf, r = (wf, r2) if off < r2 else (wt_a, r3)
+            start = r * slot_of(p, 1) + off % r2
+            buf[1, start : start + 16, :] = g[lo - 256 * j : lo - 256 * j + 16]
+    g = mm(act[ff : ff + 16, :], db2[...], NT)
+    gvec[BFC2 : BFC2 + 1, :d] = g[:1]
+
+    def reducer(full, total, r, sems, width, places):
+        refs = []
+        for (row, lane), count in zip(places, (16, 8, 4, 3)):
+            refs.append(dpre.at[row : row + count * r, lane : lane + width])
+        return Reduce(at, full, *refs, total, r, sems)
+
+    ra = reducer(wf.at[:, : 16 * r2], f_a, r2, rsem_a, d, [(k * r2, 0) for k in (0, 16, 24, 28)])
+    rb = reducer(wt_a, f_b, r3, rsem_b, d, [(0, d), (16 * r3, d), (0, 2 * d), (4 * r3, 2 * d)])
+    rc = reducer(
+        wf.at[:, 16 * r2 : 16 * r2 + 16 * r0], f_c, r0, rsem_c, d, [(k * r0, 3 * d) for k in (0, 16, 24, 28)]
+    )
+    rd = reducer(tail_s, f_d, r2, rsem_d, 128, [(k * r2, 4 * d) for k in (0, 16, 24, 28)])
+    rv = Reduce(at, tv, uv, av, bv, zv, f_v, 8, rsem_v)
+    gw = mm(att[...], db1[...], NT)
+    gvec[BOUT : BOUT + 1, :d] = gw[d : d + 1]
+    gw = gw[:d]
+    for j in range(2):
+        rows = slice(2 * d * j, 2 * d * (j + 1))
+        g = mm(n2[...], dpre[rows, :], NT)
+        gvec[BFC1 : BFC1 + 1, rows] = g[d : d + 1]
+        parts = [(g[:d, :d], 0, n), (g[:d, d:], 0, n)]
+        if j == 0:
+            put(wf, 0, parts, step=r2)
+        else:
+            put(wt_a, 0, parts + [(gw, 0, 16)], step=r3)
+    for p in every:
+        start = r3 * slot_of(p, 1) + r2
+        wt_a[1, start : start + 16, :] = jnp.concatenate([gw[n * p + 16 : n * (p + 1)], blank], 0).astype(BF16)
+
+    partners = [at.sibling(), at.along_a(), at.along_b()]
+    partners += [at.device(at.x, at.y, at.along_z(step)) for step in range(1, NZ)]
+    for k, device in enumerate(partners):
+        pl.semaphore_signal(ready.at[min(k, 3)], inc=1, device_id=device, device_id_type=MESH_ID)
+    pl.semaphore_wait(ready.at[0], 1)
+    ra.go(0)
+    rb.go(0)
+
+    def allowed(k):
+        return lambda: pl.semaphore_wait(ready.at[k], 1 if k < 3 else NZ - 1)
+
+    def slopes(i, h):
+        rows = slice(h * HD, (h + 1) * HD)
+        v = qkv[rows_of(2, h), lanes_of(i)]
+        vx = pick(qkv, rows_of(2, h), i)
+        do = dos[rows, lanes_of(i)].astype(F32) * rl_s[i, h : h + 1, :]
+        doq = pick(dos, rows, i)
+        dot_o = jnp.sum(do * att[rows, lanes_of(i)].astype(F32), 0, keepdims=True)
+        dol = do.astype(BF16)
+        dp = mm(v.T, dol)
+        return dol, dot_o, dp, row_dot(do, vx), doq, row_dot(v, doq), jnp.sum(vx * doq, 0, keepdims=True)
+
+    def scores_back(i, h, dol, dot_o, dp, dpx, doq, dpq, dpxq):
+        p = probs[i * HEADS + h]
+        ex = ex_s[i, h : h + 1, :]
+        ds = (p.astype(F32) * (dp - dot_o)).astype(BF16)
+        dsx = ex * (dpx - dot_o)
+        pq = pq_s[i, h : h + 1, :]
+        pxq = pxq_s[i, h : h + 1, :1]
+        total = jnp.sum(pq * dpq, 1, keepdims=True) + pxq * dpxq
+        return dol, p, ex, ds, dsx, doq, pq, pxq, pq * (dpq - total), pxq * (dpxq - total)
+
+    def heads_back(i, h, dol, p, ex, ds, dsx, doq, pq, pxq, dsq, dsxq):
+        q, k = (qkv[rows_of(part, h), lanes_of(i)] for part in range(2))
+        qx, kx = (pick(qkv, rows_of(part, h), i) for part in range(2))
+        scale = HD**-0.5
+        dq = (mm(k, ds) + kx * dsx) * scale
+        dk = mm(q, ds, NT) + qx * dsq
+        dv = mm(dol, p, NT) + doq * pq
+        place_column(dqkvx, rows_of(0, h), i, (column_dot(k, dsq) + kx * dsxq) * scale)
+        place_column(dqkvx, rows_of(1, h), i, column_dot(q, dsx) + qx * dsxq)
+        place_column(dqkvx, rows_of(2, h), i, column_dot(dol, ex) + doq * pxq)
+        for part, value in enumerate((dq, dk, dv)):
+            qkv[rows_of(part, h), lanes_of(i)] = value.astype(BF16)
+
+    def attend_back(units):
+        one = [slopes(*units[0])]
+        two = []
+        for k, unit in enumerate(units):
+            if k + 1 < len(units):
+                one.append(slopes(*units[k + 1]))
+            two.append(scores_back(*unit, *one[k]))
+            if k >= 1:
+                heads_back(*units[k - 1], *two[k - 1])
+        heads_back(*units[-1], *two[-1])
+
+    def run_steps(i, steps):
+        for when, todo in steps:
+
+            @pl.when(i == when)
+            def _(todo=todo):
+                for step in todo:
+                    step()
+
+    def back_first(i, carry):
+        attend_back([(UNITS1 * i + k, h) for k in range(UNITS1) for h in range(4)])
+        run_steps(i, (
+            (2, [allowed(1), later(ra, 1)]),
+            (3, [later(rb, 1)]),
+            (7, [allowed(2), later(ra, 2)]),
+        ))
+        return carry
+
+    lax.fori_loop(0, images // UNITS1, back_first, 0)
+    qkv[: 2 * d, extra_lanes] = dqkvx[: 2 * d, :].astype(BF16)
+
+    gain1, bias1 = c_ln1g[:, :1], c_ln1b[:, :1]
+
+    def weight_sums(first_pair, count):
+        rows = slice(first_pair * d, (first_pair + count) * d)
+        g = mm(n1[...], qkv[rows, :], NT)
+        sums = g[d : d + 1]
+        weight = wqkv[:, rows].astype(F32)
+        a_g1[...] += fold(weight * (g[:d] - bias1 * sums))
+        a_b1[...] += fold(weight * sums)
+        for m in range(count):
+            p = first_pair + m
+            gvec[BQKV : BQKV + 1, 128 * p : 128 * (p + 1)] = sums[:, m * d : m * d + 128]
+            gvec[BQKV : BQKV + 1, 2 * d + 128 * p : 2 * d + 128 * (p + 1)] = sums[:, m * d + 256 : (m + 1) * d]
+        return g[:d]
+
+    g = weight_sums(0, 2)
+    for p in range(2):
+        put(wf, p, [(g[:, p * d : (p + 1) * d], 0, n)], 16 * r2, r0)
+    rc.go(0)
+
+    def back_second(i, carry):
+        attend_back([(UNITS2 * i + k, h) for k in range(UNITS2) for h in range(4, 6)])
+        run_steps(i, (
+            (0, [allowed(3), later(ra, 3), later(rb, 2)]),
+            (1, [later(rc, 1)]),
+            (3, [later(rb, 3)]),
+        ))
+        return carry
+
+    lax.fori_loop(0, images // UNITS2, back_second, 0)
+    qkv[2 * d :, extra_lanes] = dqkvx[2 * d :, :].astype(BF16)
+    g = weight_sums(2, 1)
+    put(tail_s, 0, [(g[:, :128], 0, n), (g[:, 128:256], 0, n)], step=r2)
+    put(tail_s, 1, [(g[:, 256:], 0, n), (jnp.zeros((d, 128), F32), 0, n)], step=r2)
+    scale1 = a_g1[...] * (1.0 / c_ln1g[...])
+    for row, acc in ((LN1G, scale1), (LN1B, a_b1[...]), (LN2G, a_g2[...]), (LN2B, a_b2[...])):
+        gvec[row : row + 1, :d] = jnp.sum(acc.T, 0, keepdims=True)
+    tv[...] = jnp.zeros_like(tv)
+    for p in every:
+        s0 = 8 * slot_of(p, 0)
+        tv[0, s0 : s0 + 8, :n] = gvec[:, n * p : n * (p + 1)]
+        s1 = 8 * slot_of(p, 1)
+        lo = 2 * n * p if p < 8 else 2 * d + 2 * n * (p - 8)
+        parts = [gvec[BQKV : BQKV + 1, lo + n * k : lo + n * (k + 1)] for k in range(2)]
+        lo = 4 * n * p
+        parts += [gvec[BFC1 : BFC1 + 1, lo + n * k : lo + n * (k + 1)] for k in range(4)]
+        tv[1, s1 : s1 + 6, :n] = jnp.concatenate(parts, 0)
+    rd.go(0)
+    rv.go(0)
+    ra.go(4)
+
+    def finals(lanes, count):
+        return middle(lanes, count) + mm(w2_t[...], act[:ff, lanes]) + wide(c_b2[...], count)
+
+    def final_images(k, carry):
+        final = finals(lanes_of(CHUNK * k, CHUNK), CHUNK * t)
+        for m in range(CHUNK):
+            store_image(CHUNK * k + m, final[:, m * t : (m + 1) * t].T)
+        run_steps(k * CHUNK, (
+            (2, [later(rc, 2), later(rd, 1), later(rv, 1)]),
+            (6, [later(rb, 4), later(rc, 3)]),
+        ))
+        return carry
+
+    lax.fori_loop(0, images // CHUNK, final_images, 0)
+    store_last(finals(extra_lanes, 128).T)
     for b in range(blocks):
         tokb[:, 128 * b : 128 * (b + 1)] = stage[b].astype(BF16)
     out_copy = pltpu.make_async_copy(tokb, out, loc_sem.at[0])
     out_copy.start()
 
-    for j in range(2):
-        rows = slice(2 * d * j, 2 * d * (j + 1))
-        g = mm(n2[...], dpre[rows, :], NT)
-        gvec[BFC1 : BFC1 + 1, rows] = g[d : d + 1]
-        for k in range(2):
-            part = g[:d, d * k : d * (k + 1)].astype(BF16)
-            for p in every:
-                start = 4 * shard * slot_of(p, 0) + shard * (2 * j + k)
-                wf[0, start : start + shard, :] = part[shard * p : shard * (p + 1)]
-    for j in range(ff // 256):
-        rows = slice(256 * j, 256 * (j + 1))
-        g = mm(act[rows, :], db2[...], NT).astype(BF16)
-        step = 4 * shard
-        lo = 256 * j
-        while lo < 256 * (j + 1):
-            p = lo // step
-            hi = min(256 * (j + 1), (p + 1) * step)
-            start = step * slot_of(p, 1) + lo - p * step
-            wf[1, start : start + hi - lo, :] = g[lo - 256 * j : hi - 256 * j]
-            lo = hi
-    g = mm(act[ff : ff + 16, :], db2[...], NT)
-    gvec[BFC2 : BFC2 + 1, :d] = g[:1]
-
-    partners = [at.sibling(), at.along_a(), at.along_b()]
-    partners += [at.device(at.x, at.y, at.along_z(step)) for step in range(1, NZ)]
-    for k, device in enumerate(partners):
-        pl.semaphore_signal(ready.at[min(k, 3)], inc=1, device_id=device, device_id_type=MESH_ID)
-
-    def area(row, count, column):
-        return dpre.at[row : row + count, d * column : d * (column + 1)]
-
-    r2, r1 = 4 * shard, 2 * shard
-    reduce2 = Reduce(
-        at, wf, area(0, 16 * r2, 0), area(0, 8 * r2, 1), area(8 * r2, 4 * r2, 1), area(12 * r2, 3 * r2, 1), f2, r2, rsem2
-    )
-    reduce1 = Reduce(
-        at, wt_a, area(0, 16 * r1, 2), area(16 * r1, 8 * r1, 2), area(24 * r1, 4 * r1, 2), area(28 * r1, 3 * r1, 2), f1, r1, rsem1
-    )
-    pl.semaphore_wait(ready.at[0], 1)
-    reduce2.go(0)
-
-    split(dos[:, extra_lanes].astype(F32), oxn)
-
-    def attend_back(i, carry):
-        lanes = lanes_of(i)
-
-        def slopes(h):
-            rows = slice(h * HD, (h + 1) * HD)
-            v = heads_of(2 * d, lanes, h)
-            do = dos[rows, lanes].astype(F32) * rl_s[i, h : h + 1, :]
-            dot_o = jnp.sum(do * att[rows, lanes].astype(F32), 0, keepdims=True)
-            dol = do.astype(BF16)
-            dp = mm(jnp.concatenate([v[:, :t].T, vxn[h]], 0), dol)
-            return dol, dot_o, dp, mm(oxn[h], v)
-
-        def scores_back(h, dol, dot_o, dp, dpq):
-            p = probs[i * HEADS + h]
-            ds = (p.astype(F32) * (dp - dot_o)).astype(BF16)
-            eq = exq[i * HEADS + h]
-            eqf = eq.astype(F32)
-            dsq = eqf * (dpq - jnp.sum(eqf * dpq, 1, keepdims=True))
-            return dol, p, ds, eq, dsq.astype(BF16)
-
-        def heads_back(h, dol, p, ds, eq, dsq):
-            rows = slice(h * HD, (h + 1) * HD)
-            q = qkv[rows, lanes]
-            k = heads_of(d, lanes, h)
-            scale = HD**-0.5
-            dq = mm(k, ds) * scale
-            dqx = mm(k, dsq, NT) * scale
-            dk = mm(q, ds, NT) + mm(qkv[rows, last], dsq)
-            dv = mm(dol, p, NT) + mm(dos[rows, last], eq)
-            dqkvx[rows, :PAD] += dqx
-            for base, value in ((d, dk), (2 * d, dv)):
-                dqkvx[base + h * HD : base + (h + 1) * HD, :PAD] += value[:, t:]
-            return dq, dk, dv
-
-        def keep_heads(h, dq, dk, dv):
-            for base, value in ((0, dq), (d, dk), (2 * d, dv)):
-                qkv[base + h * HD : base + (h + 1) * HD, lanes] = value[:, :t].astype(BF16)
-
-        first = [slopes(0)]
-        second = []
-        for h in range(HEADS):
-            if h + 1 < HEADS:
-                first.append(slopes(h + 1))
-            second.append(scores_back(h, *first[h]))
-            if h >= 1:
-                keep_heads(h - 1, *heads_back(h - 1, *second[h - 1]))
-        keep_heads(HEADS - 1, *heads_back(HEADS - 1, *second[HEADS - 1]))
-
-        for step, when in ((1, 1), (2, 5), (3, 7)):
-
-            @pl.when(i == when)
-            def _(step=step):
-                if step < 4:
-                    pl.semaphore_wait(ready.at[step], 1 if step < 3 else NZ - 1)
-                reduce2.go(step)
-
-        return carry
-
-    lax.fori_loop(0, images, attend_back, 0)
-    qkv[:, extra_lanes] = dqkvx[...].astype(BF16)
-
-    scale1 = jnp.zeros((d, 128), F32)
-    shift1 = jnp.zeros((d, 128), F32)
-    gain1, bias1 = c_ln1g[:, :1], c_ln1b[:, :1]
-
-    def put(group, k, part):
-        part = part.astype(BF16)
-        for p in every:
-            start = 2 * shard * slot_of(p, group) + shard * k
-            wt_a[group, start : start + shard, :] = part[shard * p : shard * (p + 1)]
-
-    for k in range(3):
-        rows = slice(k * d, (k + 1) * d)
-        g = mm(n1[...], qkv[rows, :], NT)
-        sums = g[d : d + 1]
-        gvec[BQKV : BQKV + 1, rows] = sums
-        weight = wqkv[:, rows].astype(F32)
-        scale1 = scale1 + fold(weight * (g[:d] - bias1 * sums))
-        shift1 = shift1 + fold(weight * sums)
-        put(k // 2, k % 2, g[:d])
-    g = mm(att[...], db1[...], NT)
-    put(1, 1, g[:d])
-    gvec[BOUT : BOUT + 1, :d] = g[d : d + 1]
-    scale1 = scale1 * (1.0 / c_ln1g[...])
-    for row, acc in ((LN1G, scale1), (LN1B, shift1), (LN2G, a_g2[...]), (LN2B, a_b2[...])):
-        gvec[row : row + 1, :d] = jnp.sum(acc.T, 0, keepdims=True)
-    tv[...] = jnp.zeros_like(tv)
-    for p in every:
-        s0 = 8 * slot_of(p, 0)
-        tv[0, s0 : s0 + 8, :shard] = gvec[:, shard * p : shard * (p + 1)]
-        s1 = 8 * slot_of(p, 1)
-        lo = 2 * shard * p if p < 8 else 2 * d + 2 * shard * (p - 8)
-        parts = [gvec[BQKV : BQKV + 1, lo + shard * k : lo + shard * (k + 1)] for k in range(2)]
-        lo = 4 * shard * p
-        parts += [gvec[BFC1 : BFC1 + 1, lo + shard * k : lo + shard * (k + 1)] for k in range(4)]
-        tv[1, s1 : s1 + 6, :shard] = jnp.concatenate(parts, 0)
-
-    reduce_v = Reduce(at, tv, uv, av, bv, zv, fv, 8, rsemv)
-    reduce1.go(0)
-    reduce_v.go(0)
-    reduce2.go(4)
-
     def finish(lanes, count, mu, r):
         u = (xs[:, lanes].astype(F32) - mu) * r
         dn = mm(wqkv[...], qkv[:, lanes])
-        return (dmid[:, lanes] + norm_back(dn, u, r, wide(c_ln1g[...], count))).T
-
-    def finish_image(i, carry):
-        store_image(i, finish(lanes_of(i), t, stat_s[i, 0:1, :], stat_s[i, 1:2, :]))
-        for step, when in ((1, 2), (2, 6)):
-
-            @pl.when(i == when)
-            def _(step=step):
-                reduce_v.go(step)
-                reduce1.go(step)
-
+        return dmid[:, lanes] + norm_back(dn, u, r, wide(c_ln1g[...], count))
+
+    def finish_images(k, carry):
+        mu, r = (
+            jnp.concatenate([stat_s[CHUNK * k + m, row : row + 1, :] for m in range(CHUNK)], 1) for row in range(2)
+        )
+        grad = finish(lanes_of(CHUNK * k, CHUNK), CHUNK * t, mu, r)
+        for m in range(CHUNK):
+            store_image(CHUNK * k + m, grad[:, m * t : (m + 1) * t].T)
+        run_steps(k * CHUNK, (
+            (0, [later(rd, 2), later(rv, 2)]),
+            (6, [later(rd, 3), later(rv, 3)]),
+        ))
         return carry
 
-    lax.fori_loop(0, images, finish_image, 0)
-    store_last(finish(extra_lanes, 128, stat_s[images, 0:1, :128], stat_s[images, 1:2, :128]))
+    lax.fori_loop(0, images // CHUNK, finish_images, 0)
+    store_last(finish(extra_lanes, 128, stat_s[images, 0:1, :128], stat_s[images, 1:2, :128]).T)
     copies = [
         pltpu.make_async_copy(stage.at[b], gin.at[:, pl.ds(128 * b, 128)], loc_sem.at[1 + b]) for b in range(blocks)
     ]
     for copy in copies:
         copy.start()
-    reduce2.go(5)
-    o1[...] = jnp.concatenate([f2[0, shard * k : shard * (k + 1)] for k in range(4)], 1)
-    o2[...] = f2[1]
-    for step in (3, 4, 5):
-        reduce_v.go(step)
-        reduce1.go(step)
-    oqkv[:, :d] = f1[0, :shard]
-    oqkv[:, d : 2 * d] = f1[0, shard:]
-    oqkv[:, 2 * d :] = f1[1, :shard]
-    oout[...] = f1[1, shard:]
-    ovec[...] = fv[...]
+    rc.go(4)
+    ra.go(5)
+    rb.go(5)
+    o1[...] = jnp.concatenate([f[0, n * k : n * (k + 1)] for f in (f_a, f_b) for k in range(2)], 1)
+    o2[:r2] = f_a[1]
+    o2[r2:] = f_b[1, :r2]
+    oout[:16] = f_b[0, r2:]
+    oout[16:] = f_b[1, r2 : r2 + 8]
+    rd.go(4)
+    rv.go(4)
+    rc.go(5)
+    for k in range(3):
+        for p in range(2):
+            oqkv[:, d * k + 128 * p : d * k + 128 * (p + 1)] = f_c[p, :n, 128 * k : 128 * (k + 1)]
+    rd.go(5)
+    rv.go(5)
+    for k in range(3):
+        oqkv[:, d * k + 256 : d * (k + 1)] = f_d[k // 2, (k % 2) * n : (k % 2 + 1) * n]
+    ovec[...] = f_v[...]
     for copy in copies:
         copy.wait()
     out_copy.wait()
@@ -1049,6 +1153,7 @@
     vm = pltpu.VMEM
     dma = pltpu.SemaphoreType.DMA
     sd = jax.ShapeDtypeStruct
+    column = vm((d, 128), F32)
     scratch = [
         vm((seq * images, d), BF16),
         vm((d // 128, seq * images, 128), F32),
@@ -1063,34 +1168,32 @@
         vm((d, w), BF16),
         vm((d, w), BF16),
         vm((d, w), F32),
-        vm((images * HEADS, t + PAD, t), BF16),
+        vm((images * HEADS, t, t), BF16),
         vm((d, 3 * d), BF16),
-        vm((d, d), BF16),
+        vm((d, d), BF16), vm((d, d), BF16),
         vm((d, ff), BF16),
         vm((d, ff), BF16),
-        vm((2, 2 * d, d), BF16),
+        vm((2, 32 * n + 256, d), BF16),
         vm((2, ff, d), BF16),
-        vm((d, 128), F32), vm((d, 128), F32), vm((3 * d, 128), F32), vm((d, 128), F32),
-        vm((d, 128), F32), vm((d, 128), F32), vm((ff, 128), F32), vm((d, 128), F32),
+        column, column, column, column, column, column, column, vm((ff, 128), F32), column,
         vm((images + 1, 8, t), F32),
         vm((images, 8, t), F32),
-        vm((images * HEADS, PAD, t + PAD), BF16),
-        vm((HEADS, PAD, HD), BF16), vm((HEADS, PAD, HD), BF16),
-        vm((HEADS, PAD, HD), BF16), vm((HEADS, PAD, HD), BF16),
-        vm((d, 128), F32),
+        vm((images, 8, t), F32),
+        vm((images, 8, t), F32),
+        vm((images, 8, 128), F32),
+        column,
         vm((3 * d, 128), F32),
-        vm((d, 128), F32), vm((d, 128), F32),
-        vm((d, 128), F32),
+        column, column, column, column,
+        column,
         vm((8, ff), F32),
         vm((2, 128, 128), F32),
-        vm((256, 128), F32),
+        vm((8, d), F32),
+        vm((2, 32 * n, 128), BF16),
         vm((2, 128, 128), F32),
     ]
-    for slots in (16, 8, 4):
-        scratch += [vm((slots * 8, 128), F32)]
-    scratch += [vm((24, 128), F32)]
-    scratch += [vm((2, 2 * n, d), F32), vm((2, 4 * n, d), F32), vm((2, 8, 128), F32)]
-    scratch += [dma((4,))] + [dma((2, 7))] * 6 + [pltpu.SemaphoreType.REGULAR((4,))]
+    scratch += [vm((slots * 8, 128), F32) for slots in (16, 8, 4, 3)]
+    scratch += [vm((2, r, d), F32) for r in (2 * n, 2 * n + 16, n + 8)] + [vm((2, 2 * n, 128), F32), vm((2, 8, 128), F32)]
+    scratch += [dma((4,))] + [dma((2, 7))] * 9 + [pltpu.SemaphoreType.REGULAR((4,))]
     spec = pl.BlockSpec(memory_space=pltpu.VMEM)
     any_spec = pl.BlockSpec(memory_space=pl.ANY)
     return pl.pallas_call(

time: 127 us -> 119 us (0.937)
  Pallas kernels: 126 us -> 118 us
    pallas_call x1, Pallas kernels: 121 us -> 113 us  [block_call(): pl.pallas_call(block_body, out_shape=(sd(tok.shape, BF16), sd(tok.shape,...]
where the time goes in v4:
time: 119 us
  Pallas kernels  118 us (99%)
    pallas_call x1, Pallas kernels, block_call(): pl.pallas_call(block_body, out_shape=(sd(tok.shape, BF16), sd(tok.shape,...  113 us
    pallas_call x1, Pallas kernels, deliver_call(): pl.pallas_call(deliver_body, out_shape=(sd(out.shape, BF16), sd(gin.shape...  5.57 us

profile of v4, /device:TPU:0, one launch (start us, length us, event | category | flops | bytes accessed | tf_op | source)
XLA Modules:
  0.0 119.2 jit_solution(16054123287713470184)
XLA Ops:
  0.7 112.8 %block16.1 = (bf16[2056,384]{1,0:T(8,128)(2,1)}, f32[2056,384]{1,0:T(8,128)}, f32[24,1152]{1,0:T(8,128)}, f32[24,384]{1,0:T(8,128)}, f32[24,1536]{1,0:T(8,128)},...) custom-call(bf16[2056,384]{1,0:T(8,128)(2,1)} %bitcast.9, s32[8,257]{1,0:T(8,128)} %dup.1, f32[8,384]{1,0:T(8,128)} %tgt.1, ...), custom_call_target="tpu_custom_call" | custom-call | tf_op jit(solution)/shard_map/block16/pallas_call | solution.py:1199
  113.5 5.6 %deliver.1 = (bf16[2056,384]{1,0:T(8,128)(2,1)}, f32[2056,384]{1,0:T(8,128)}, f32[24]{0:T(128)}, f32[24]{0:T(128)}, f32[24,1152]{1,0:T(8,128)}, /*index=5*/f32[4...) custom-call(bf16[2056,384]{1,0:T(8,128)(2,1)} %get-tuple-element.35., ...), custom_call_target="tpu_custom_call" | custom-call | tf_op jit(solution)/shard_map/deliver/pallas_call | solution.py:1253

commit v5 on v4

--- a/solution.py
+++ b/solution.py
@@ -421,6 +421,9 @@
     def sibling(self):
         return (self.p, 1 - self.c)
 
+    def everyone(self):
+        return [(lax.rem(self.p + k, 16), self.c) for k in range(1, 16)]
+
 
 def slot_of(p, group):
     x, y, z = p % 2, (p // 2) % 2, p // 4
@@ -430,11 +433,9 @@
 
 def greet(at):
     barrier = pltpu.get_barrier_semaphore()
-    others = [at.along_a(), at.along_b(), at.sibling()]
-    others += [at.device(at.x, at.y, at.along_z(step)) for step in range(1, NZ)]
+    others = [at.sibling()] + at.everyone()
     for device in others:
         pl.semaphore_signal(barrier, inc=1, device_id=device, device_id_type=MESH_ID)
-    pl.semaphore_wait(barrier, len(others))
 
 
 def remote(src, dst, sems, k, device):
@@ -480,6 +481,29 @@
             for copy in steps[step - 1]():
                 copy.wait()
         if step < 4:
+            for copy in steps[step]():
+                copy.start()
+
+
+class Spread:
+    def __init__(self, at, buf, r, sems):
+        self.at, self.buf, self.r, self.sems = at, buf, r, sems
+
+    def direct(self):
+        at, r = self.at, self.r
+        piece = self.buf.at[span((at.c * 16 + at.p) * r, r)]
+        return [remote(piece, piece, self.sems, k, device) for k, device in enumerate(at.everyone())]
+
+    def swap(self):
+        piece = self.buf.at[span(self.at.c * 16 * self.r, 16 * self.r)]
+        return [remote(piece, piece, self.sems, 15, self.at.sibling())]
+
+    def go(self, step):
+        steps = (self.direct, self.swap)
+        if step > 0:
+            for copy in steps[step - 1]():
+                copy.wait()
+        if step < 2:
             for copy in steps[step]():
                 copy.start()
 
@@ -589,6 +613,7 @@
         for b in range(blocks):
             stage[b, x0:, :] = values[:images, 128 * b : 128 * (b + 1)]
 
+    greet(at)
     tok_copy = pltpu.make_async_copy(tok, tokb, loc_sem.at[0])
     tok_copy.start()
 
@@ -610,7 +635,9 @@
     for k, line in enumerate(flat):
         lo = 128 * (k // 8)
         vec_s[k % 8 : k % 8 + 1, lo : lo + n] = line.astype(F32).reshape(1, n)
-    slots0[span(own * r0, r0), :] = jnp.concatenate([pair_of(0), vec_s[...]], 0).astype(BF16)
+    slot = jnp.concatenate([pair_of(0), vec_s[...]], 0)
+    half = r0 // 2
+    slots0[span((at.c * 16 + at.p) * half, half), :] = jnp.where(at.c == 0, slot[:half], slot[half:]).astype(BF16)
     own1, own2, own3 = (span(own * r, r) for r in (r0, r2, r3))
     w_out = s_out[...].astype(F32)
     blank = jnp.zeros((8, d), F32)
@@ -630,8 +657,8 @@
         parts = [s_fc2[r2:].astype(F32), w_out[16:], blank]
         slots3[own3, group[1]] = jnp.concatenate(parts, 0).astype(BF16)
 
-    greet(at)
-    g0 = Gather(at, slots0, r0, gsem0, False)
+    pl.semaphore_wait(pltpu.get_barrier_semaphore(), 16)
+    g0 = Spread(at, slots0, half, gsem0)
     g1 = Gather(at, slots1.at[:, mine], r0, gsem1, True)
     g2 = Gather(at, slots2.at[:, later_mine], r2, gsem2, True)
     g3 = Gather(at, slots3.at[:, mine], r3, gsem3, True)
@@ -670,20 +697,15 @@
     att[d : d + 16, :] = ones_row
     for ref in (attx, dqkvx, a_g1, a_b1, a_g2, a_b2):
         ref[...] = jnp.zeros_like(ref)
+    g0.go(1)
+    g1.go(1)
     g2.go(0)
-    g0.go(1)
     g0.go(2)
     g3.go(0)
-    g1.go(1)
-    g0.go(3)
-    g1.go(2)
-    g2.go(1)
 
     def slot_of_chip(p):
-        px, py, pz = p % 2, (p // 2) % 2, p // 4
-        pa = py + at.c * (px - py)
-        pb = px + at.c * (py - px)
-        return slots0[span(((pa * 2 + pb) * NZ + pz) * r0, r0), :].astype(F32)
+        parts = [slots0[(16 * k + p) * half : (16 * k + p + 1) * half, :].astype(F32) for k in range(2)]
+        return jnp.concatenate(parts, 0)
 
     first = [slot_of_chip(p) for p in every]
     for half in range(2):
@@ -824,7 +846,7 @@
     def later(item, step):
         return lambda: item.go(step)
 
-    forward_pair(0, [[later(g3, 1)], [], [later(g1, 3), later(g2, 2)], [], []])
+    forward_pair(0, [[later(g1, 2), later(g2, 1)], [], [later(g3, 1)], [], [later(g1, 3), later(g2, 2)]])
     g1.go(4)
     for k in range(2):
         put_pair(1 + k, jnp.concatenate(unpack(slots1, k, group[k], r0, 0, n), 0))
@@ -1014,13 +1036,14 @@
     def back_first(i, carry):
         attend_back([(UNITS1 * i + k, h) for k in range(UNITS1) for h in range(4)])
         run_steps(i, (
-            (2, [allowed(1), later(ra, 1)]),
-            (3, [later(rb, 1)]),
-            (7, [allowed(2), later(ra, 2)]),
+            (3, [allowed(1), later(ra, 1)]),
+            (4, [later(rb, 1)]),
         ))
         return carry
 
     lax.fori_loop(0, images // UNITS1, back_first, 0)
+    pl.semaphore_wait(ready.at[2], 1)
+    ra.go(2)
     qkv[: 2 * d, extra_lanes] = dqkvx[: 2 * d, :].astype(BF16)
 
     gain1, bias1 = c_ln1g[:, :1], c_ln1b[:, :1]
@@ -1046,9 +1069,8 @@
     def back_second(i, carry):
         attend_back([(UNITS2 * i + k, h) for k in range(UNITS2) for h in range(4, 6)])
         run_steps(i, (
-            (0, [allowed(3), later(ra, 3), later(rb, 2)]),
-            (1, [later(rc, 1)]),
-            (3, [later(rb, 3)]),
+            (0, [allowed(3), later(ra, 3)]),
+            (1, [later(rb, 2), later(rc, 1)]),
         ))
         return carry
 
@@ -1073,6 +1095,7 @@
     rd.go(0)
     rv.go(0)
     ra.go(4)
+    rb.go(3)
 
     def finals(lanes, count):
         return middle(lanes, count) + mm(w2_t[...], act[:ff, lanes]) + wide(c_b2[...], count)
@@ -1082,8 +1105,9 @@
         for m in range(CHUNK):
             store_image(CHUNK * k + m, final[:, m * t : (m + 1) * t].T)
         run_steps(k * CHUNK, (
-            (2, [later(rc, 2), later(rd, 1), later(rv, 1)]),
-            (6, [later(rb, 4), later(rc, 3)]),
+            (0, [later(rd, 1), later(rv, 1)]),
+            (2, [later(rc, 2)]),
+            (6, [later(rd, 2), later(rv, 2)]),
         ))
         return carry
 
@@ -1107,8 +1131,9 @@
         for m in range(CHUNK):
             store_image(CHUNK * k + m, grad[:, m * t : (m + 1) * t].T)
         run_steps(k * CHUNK, (
-            (0, [later(rd, 2), later(rv, 2)]),
-            (6, [later(rd, 3), later(rv, 3)]),
+            (0, [later(rc, 3)]),
+            (2, [later(rb, 4)]),
+            (4, [later(rd, 3), later(rv, 3)]),
         ))
         return carry
 
@@ -1193,7 +1218,7 @@
     ]
     scratch += [vm((slots * 8, 128), F32) for slots in (16, 8, 4, 3)]
     scratch += [vm((2, r, d), F32) for r in (2 * n, 2 * n + 16, n + 8)] + [vm((2, 2 * n, 128), F32), vm((2, 8, 128), F32)]
-    scratch += [dma((4,))] + [dma((2, 7))] * 9 + [pltpu.SemaphoreType.REGULAR((4,))]
+    scratch += [dma((4,)), dma((2, 16))] + [dma((2, 7))] * 8 + [pltpu.SemaphoreType.REGULAR((4,))]
     spec = pl.BlockSpec(memory_space=pltpu.VMEM)
     any_spec = pl.BlockSpec(memory_space=pl.ANY)
     return pl.pallas_call(

time: 119 us -> 114 us (0.958)
  Pallas kernels: 118 us -> 113 us
    pallas_call x1, Pallas kernels: 113 us -> 108 us  [block_call(): pl.pallas_call(block_body, out_shape=(sd(tok.shape, BF16), sd(tok.shape,...]
where the time goes in v5:
time: 114 us
  Pallas kernels  113 us (99%)
    pallas_call x1, Pallas kernels, block_call(): pl.pallas_call(block_body, out_shape=(sd(tok.shape, BF16), sd(tok.shape,...  108 us
    pallas_call x1, Pallas kernels, deliver_call(): pl.pallas_call(deliver_body, out_shape=(sd(out.shape, BF16), sd(gin.shape...  5.57 us

profile of v5, /device:TPU:0, one launch (start us, length us, event | category | flops | bytes accessed | tf_op | source)
XLA Modules:
  0.0 114.2 jit_solution(5583834848994742879)
XLA Ops:
  0.7 107.8 %block16.1 = (bf16[2056,384]{1,0:T(8,128)(2,1)}, f32[2056,384]{1,0:T(8,128)}, f32[24,1152]{1,0:T(8,128)}, f32[24,384]{1,0:T(8,128)}, f32[24,1536]{1,0:T(8,128)},...) custom-call(bf16[2056,384]{1,0:T(8,128)(2,1)} %bitcast.9, s32[8,257]{1,0:T(8,128)} %dup.1, f32[8,384]{1,0:T(8,128)} %tgt.1, ...), custom_call_target="tpu_custom_call" | custom-call | tf_op jit(solution)/shard_map/block16/pallas_call | solution.py:1224
  108.4 5.6 %deliver.1 = (bf16[2056,384]{1,0:T(8,128)(2,1)}, f32[2056,384]{1,0:T(8,128)}, f32[24]{0:T(128)}, f32[24]{0:T(128)}, f32[24,1152]{1,0:T(8,128)}, /*index=5*/f32[4...) custom-call(bf16[2056,384]{1,0:T(8,128)(2,1)} %get-tuple-element.35., ...), custom_call_target="tpu_custom_call" | custom-call | tf_op jit(solution)/shard_map/deliver/pallas_call | solution.py:1278

commit v6 on v5

--- a/solution.py
+++ b/solution.py
@@ -771,9 +771,10 @@
     def score(i, h):
         q, k = (qkv[rows_of(part, h), lanes_of(i)] for part in range(2))
         qx, kx = (pick(qkv, rows_of(part, h), i) for part in range(2))
-        return mm(k.T, q), row_dot(q, kx), row_dot(k, qx), jnp.sum(qx * kx, 0, keepdims=True)
-
-    def share(i, h, s, sx, sq, sxq):
+        vx = pick(qkv, rows_of(2, h), i)
+        return mm(k.T, q), row_dot(q, kx), row_dot(k, qx), jnp.sum(qx * kx, 0, keepdims=True), vx
+
+    def share(i, h, s, sx, sq, sxq, vx):
         top = jnp.maximum(jnp.max(s, 0, keepdims=True), sx)
         e = jnp.exp(s - top)
         ex = jnp.exp(sx - top)
@@ -790,11 +791,10 @@
         pxq = exq * rlq
         pq_s[i, h : h + 1, :] = pq
         pxq_s[i, h : h + 1, :] = jnp.broadcast_to(pxq, (1, 128))
-        return e, ex, rl, pq, pxq
-
-    def mix(i, h, e, ex, rl, pq, pxq):
+        return e, ex, rl, pq, pxq, vx
+
+    def mix(i, h, e, ex, rl, pq, pxq, vx):
         v = qkv[rows_of(2, h), lanes_of(i)]
-        vx = pick(qkv, rows_of(2, h), i)
         rows = slice(h * HD, (h + 1) * HD)
         att[rows, lanes_of(i)] = ((mm(v, e) + vx * ex) * rl).astype(BF16)
         place_column(attx, rows, i, column_dot(v, pq) + vx * pxq)
@@ -989,9 +989,10 @@
         dot_o = jnp.sum(do * att[rows, lanes_of(i)].astype(F32), 0, keepdims=True)
         dol = do.astype(BF16)
         dp = mm(v.T, dol)
-        return dol, dot_o, dp, row_dot(do, vx), doq, row_dot(v, doq), jnp.sum(vx * doq, 0, keepdims=True)
-
-    def scores_back(i, h, dol, dot_o, dp, dpx, doq, dpq, dpxq):
+        qx, kx = (pick(qkv, rows_of(part, h), i) for part in range(2))
+        return qx, kx, dol, dot_o, dp, row_dot(do, vx), doq, row_dot(v, doq), jnp.sum(vx * doq, 0, keepdims=True)
+
+    def scores_back(i, h, qx, kx, dol, dot_o, dp, dpx, doq, dpq, dpxq):
         p = probs[i * HEADS + h]
         ex = ex_s[i, h : h + 1, :]
         ds = (p.astype(F32) * (dp - dot_o)).astype(BF16)
@@ -999,11 +1000,10 @@
         pq = pq_s[i, h : h + 1, :]
         pxq = pxq_s[i, h : h + 1, :1]
         total = jnp.sum(pq * dpq, 1, keepdims=True) + pxq * dpxq
-        return dol, p, ex, ds, dsx, doq, pq, pxq, pq * (dpq - total), pxq * (dpxq - total)
-
-    def heads_back(i, h, dol, p, ex, ds, dsx, doq, pq, pxq, dsq, dsxq):
+        return qx, kx, dol, p, ex, ds, dsx, doq, pq, pxq, pq * (dpq - total), pxq * (dpxq - total)
+
+    def heads_back(i, h, qx, kx, dol, p, ex, ds, dsx, doq, pq, pxq, dsq, dsxq):
         q, k = (qkv[rows_of(part, h), lanes_of(i)] for part in range(2))
-        qx, kx = (pick(qkv, rows_of(part, h), i) for part in range(2))
         scale = HD**-0.5
         dq = (mm(k, ds) + kx * dsx) * scale
         dk = mm(q, ds, NT) + qx * dsq

time: 114 us -> 114 us (level)
  no operation moved by 1% of the time
where the time goes in v6:
time: 114 us
  Pallas kernels  113 us (99%)
    pallas_call x1, Pallas kernels, block_call(): pl.pallas_call(block_body, out_shape=(sd(tok.shape, BF16), sd(tok.shape,...  107 us
    pallas_call x1, Pallas kernels, deliver_call(): pl.pallas_call(deliver_body, out_shape=(sd(out.shape, BF16), sd(gin.shape...  5.57 us

profile of v6, /device:TPU:0, one launch (start us, length us, event | category | flops | bytes accessed | tf_op | source)
XLA Modules:
  0.0 113.7 jit_solution(8106022680125527205)
XLA Ops:
  0.7 107.3 %block16.1 = (bf16[2056,384]{1,0:T(8,128)(2,1)}, f32[2056,384]{1,0:T(8,128)}, f32[24,1152]{1,0:T(8,128)}, f32[24,384]{1,0:T(8,128)}, f32[24,1536]{1,0:T(8,128)},...) custom-call(bf16[2056,384]{1,0:T(8,128)(2,1)} %bitcast.9, s32[8,257]{1,0:T(8,128)} %dup.1, f32[8,384]{1,0:T(8,128)} %tgt.1, ...), custom_call_target="tpu_custom_call" | custom-call | tf_op jit(solution)/shard_map/block16/pallas_call | solution.py:1224
  108.0 5.6 %deliver.1 = (bf16[2056,384]{1,0:T(8,128)(2,1)}, f32[2056,384]{1,0:T(8,128)}, f32[24]{0:T(128)}, f32[24]{0:T(128)}, f32[24,1152]{1,0:T(8,128)}, /*index=5*/f32[4...) custom-call(bf16[2056,384]{1,0:T(8,128)(2,1)} %get-tuple-element.35., ...), custom_call_target="tpu_custom_call" | custom-call | tf_op jit(solution)/shard_map/deliver/pallas_call | solution.py:1278

commit v7 on v6

--- a/solution.py
+++ b/solution.py
@@ -570,6 +570,44 @@
                 copy.start()
 
 
+class ReduceAtOnce:
+    def __init__(self, at, full, got, landing, total, r, sems):
+        self.at, self.full, self.got, self.landing, self.total = at, full, got, landing, total
+        self.r, self.sems = r, sems
+
+    def first(self):
+        return [remote(self.full.at[1 - self.at.c], self.got, self.sems, 15, self.at.sibling())]
+
+    def direct(self):
+        at, r = self.at, self.r
+        return [
+            remote(self.full.at[at.c, span(device[0] * r, r)], self.landing.at[pl.ds(k * r, r)], self.sems, k, device)
+            for k, device in enumerate(at.everyone())
+        ]
+
+    def last(self):
+        piece = self.total.at[self.at.c]
+        return [remote(piece, piece, self.sems, 16, self.at.sibling())]
+
+    def go(self, step):
+        at, r = self.at, self.r
+        steps = (self.first, self.direct, self.last)
+        if step > 0:
+            for copy in steps[step - 1]():
+                copy.wait()
+        if step == 1:
+            ref = self.full.at[at.c]
+            ref[...] = (ref[...].astype(F32) + self.got[...].astype(F32)).astype(ref.dtype)
+        elif step == 2:
+            total = self.full[at.c, span(at.p * r, r), :].astype(F32)
+            for k in range(15):
+                total = total + self.landing[k * r : (k + 1) * r, :].astype(F32)
+            self.total[at.c] = total
+        if step < 3:
+            for copy in steps[step]():
+                copy.start()
+
+
 V_LN1G, V_LN1B, V_QV, V_BOUT, V_LN2G, V_LN2B, V_BFC2, V_BFC1 = 0, 1, 2, 4, 5, 6, 7, 8
 
 
@@ -580,7 +618,7 @@
     wqkv, wout, wout_t, w1, w2_t, wt_a, wf,
     c_ln1g, c_ln1b, c_q, c_v, c_bout, c_ln2g, c_ln2b, c_b1, c_b2,
     stat_s, rl_s, ex_s, pq_s, pxq_s, attx, dqkvx, a_g1, a_b1, a_g2, a_b2, tgt_t, gvec, allc, vec_s,
-    tail_s, tv, uv, av, bv, zv, f_a, f_b, f_c, f_d, f_v,
+    tail_s, tail_g, tail_l, tv, uv, av, f_a, f_b, f_c, f_d, f_v,
     loc_sem, gsem0, gsem1, gsem2, gsem3, rsem_a, rsem_b, rsem_c, rsem_d, rsem_v, ready,
 ):
     images, seq = dup.shape
@@ -923,10 +961,10 @@
     scale_x = jnp.concatenate([scale_x, jnp.zeros((128 - images, 128), F32)], 0).T[:1, :]
     feed(extra_lanes, 128, tgt_t[...] * scale_x)
 
-    def put(buf, which, parts, lo=0, step=None):
+    def put(buf, which, parts, lo=0, step=None, slot_at=slot_of):
         for p in every:
             slot = jnp.concatenate([part[n * p + a : n * p + b] for part, a, b in parts], 0).astype(BF16)
-            start = step * slot_of(p, which) + lo
+            start = step * slot_at(p, which) + lo
             buf[which, start : start + slot.shape[0], :] = slot
 
     for j in range(ff // 256):
@@ -951,8 +989,8 @@
     rc = reducer(
         wf.at[:, 16 * r2 : 16 * r2 + 16 * r0], f_c, r0, rsem_c, d, [(k * r0, 3 * d) for k in (0, 16, 24, 28)]
     )
-    rd = reducer(tail_s, f_d, r2, rsem_d, 128, [(k * r2, 4 * d) for k in (0, 16, 24, 28)])
-    rv = Reduce(at, tv, uv, av, bv, zv, f_v, 8, rsem_v)
+    rd = ReduceAtOnce(at, tail_s, tail_g, tail_l, f_d, r2, rsem_d)
+    rv = ReduceAtOnce(at, tv, uv, av, f_v, 8, rsem_v)
     gw = mm(att[...], db1[...], NT)
     gvec[BOUT : BOUT + 1, :d] = gw[d : d + 1]
     gw = gw[:d]
@@ -1077,16 +1115,16 @@
     lax.fori_loop(0, images // UNITS2, back_second, 0)
     qkv[2 * d :, extra_lanes] = dqkvx[2 * d :, :].astype(BF16)
     g = weight_sums(2, 1)
-    put(tail_s, 0, [(g[:, :128], 0, n), (g[:, 128:256], 0, n)], step=r2)
-    put(tail_s, 1, [(g[:, 256:], 0, n), (jnp.zeros((d, 128), F32), 0, n)], step=r2)
+    put(tail_s, 0, [(g[:, :128], 0, n), (g[:, 128:256], 0, n)], step=r2, slot_at=lambda p, which: p)
+    put(tail_s, 1, [(g[:, 256:], 0, n), (jnp.zeros((d, 128), F32), 0, n)], step=r2, slot_at=lambda p, which: p)
     scale1 = a_g1[...] * (1.0 / c_ln1g[...])
     for row, acc in ((LN1G, scale1), (LN1B, a_b1[...]), (LN2G, a_g2[...]), (LN2B, a_b2[...])):
         gvec[row : row + 1, :d] = jnp.sum(acc.T, 0, keepdims=True)
     tv[...] = jnp.zeros_like(tv)
     for p in every:
-        s0 = 8 * slot_of(p, 0)
+        s0 = 8 * p
         tv[0, s0 : s0 + 8, :n] = gvec[:, n * p : n * (p + 1)]
-        s1 = 8 * slot_of(p, 1)
+        s1 = 8 * p
         lo = 2 * n * p if p < 8 else 2 * d + 2 * n * (p - 8)
         parts = [gvec[BQKV : BQKV + 1, lo + n * k : lo + n * (k + 1)] for k in range(2)]
         lo = 4 * n * p
@@ -1096,6 +1134,7 @@
     rv.go(0)
     ra.go(4)
     rb.go(3)
+    rc.go(2)
 
     def finals(lanes, count):
         return middle(lanes, count) + mm(w2_t[...], act[:ff, lanes]) + wide(c_b2[...], count)
@@ -1106,8 +1145,7 @@
             store_image(CHUNK * k + m, final[:, m * t : (m + 1) * t].T)
         run_steps(k * CHUNK, (
             (0, [later(rd, 1), later(rv, 1)]),
-            (2, [later(rc, 2)]),
-            (6, [later(rd, 2), later(rv, 2)]),
+            (4, [later(rc, 3)]),
         ))
         return carry
 
@@ -1131,9 +1169,8 @@
         for m in range(CHUNK):
             store_image(CHUNK * k + m, grad[:, m * t : (m + 1) * t].T)
         run_steps(k * CHUNK, (
-            (0, [later(rc, 3)]),
-            (2, [later(rb, 4)]),
-            (4, [later(rd, 3), later(rv, 3)]),
+            (0, [later(rb, 4)]),
+
         ))
         return carry
 
@@ -1152,14 +1189,14 @@
     o2[r2:] = f_b[1, :r2]
     oout[:16] = f_b[0, r2:]
     oout[16:] = f_b[1, r2 : r2 + 8]
-    rd.go(4)
-    rv.go(4)
+    rd.go(2)
+    rv.go(2)
     rc.go(5)
     for k in range(3):
         for p in range(2):
             oqkv[:, d * k + 128 * p : d * k + 128 * (p + 1)] = f_c[p, :n, 128 * k : 128 * (k + 1)]
-    rd.go(5)
-    rv.go(5)
+    rd.go(3)
+    rv.go(3)
     for k in range(3):
         oqkv[:, d * k + 256 : d * (k + 1)] = f_d[k // 2, (k % 2) * n : (k % 2 + 1) * n]
     ovec[...] = f_v[...]
@@ -1213,12 +1250,12 @@
         vm((8, ff), F32),
         vm((2, 128, 128), F32),
         vm((8, d), F32),
-        vm((2, 32 * n, 128), BF16),
+        vm((2, 32 * n, 128), BF16), vm((32 * n, 128), BF16), vm((30 * n, 128), BF16),
         vm((2, 128, 128), F32),
     ]
-    scratch += [vm((slots * 8, 128), F32) for slots in (16, 8, 4, 3)]
+    scratch += [vm((128, 128), F32), vm((120, 128), F32)]
     scratch += [vm((2, r, d), F32) for r in (2 * n, 2 * n + 16, n + 8)] + [vm((2, 2 * n, 128), F32), vm((2, 8, 128), F32)]
-    scratch += [dma((4,)), dma((2, 16))] + [dma((2, 7))] * 8 + [pltpu.SemaphoreType.REGULAR((4,))]
+    scratch += [dma((4,)), dma((2, 16))] + [dma((2, 7))] * 6 + [dma((2, 17))] * 2 + [pltpu.SemaphoreType.REGULAR((4,))]
     spec = pl.BlockSpec(memory_space=pltpu.VMEM)
     any_spec = pl.BlockSpec(memory_space=pl.ANY)
     return pl.pallas_call(

time: 114 us -> 114 us (level)
  no operation moved by 1% of the time
where the time goes in v7:
time: 114 us
  Pallas kernels  113 us (99%)
    pallas_call x1, Pallas kernels, block_call(): pl.pallas_call(block_body, out_shape=(sd(tok.shape, BF16), sd(tok.shape,...  107 us
    pallas_call x1, Pallas kernels, deliver_call(): pl.pallas_call(deliver_body, out_shape=(sd(out.shape, BF16), sd(gin.shape...  5.57 us

profile of v7, /device:TPU:0, one launch (start us, length us, event | category | flops | bytes accessed | tf_op | source)
XLA Modules:
  0.0 113.7 jit_solution(4685549026567739144)
XLA Ops:
  0.7 107.3 %block16.1 = (bf16[2056,384]{1,0:T(8,128)(2,1)}, f32[2056,384]{1,0:T(8,128)}, f32[24,1152]{1,0:T(8,128)}, f32[24,384]{1,0:T(8,128)}, f32[24,1536]{1,0:T(8,128)},...) custom-call(bf16[2056,384]{1,0:T(8,128)(2,1)} %bitcast.9, s32[8,257]{1,0:T(8,128)} %dup.1, f32[8,384]{1,0:T(8,128)} %tgt.1, ...), custom_call_target="tpu_custom_call" | custom-call | tf_op jit(solution)/shard_map/block16/pallas_call | solution.py:1261
  107.9 5.6 %deliver.1 = (bf16[2056,384]{1,0:T(8,128)(2,1)}, f32[2056,384]{1,0:T(8,128)}, f32[24]{0:T(128)}, f32[24]{0:T(128)}, f32[24,1152]{1,0:T(8,128)}, /*index=5*/f32[4...) custom-call(bf16[2056,384]{1,0:T(8,128)(2,1)} %get-tuple-element.35., ...), custom_call_target="tpu_custom_call" | custom-call | tf_op jit(solution)/shard_map/deliver/pallas_call | solution.py:1315
